TPU v7x, 256 devices: a whole 4x4x8 slice. The times are simulated.
256 devices in a mesh: row: 32 (over y_lo, z, core), col: 8 (over y_hi, x).
Axes of the slice: x: 4, y: 4 (y_hi: 2, y_lo: 2; y = y_hi * 2 + y_lo), z: 8, core: 2. Of those that a mesh axis runs over, the one named last changes fastest.
Arguments:
- tokens: bfloat16 [16384, 5120], P('row'), may hold values from -6 to 6
- cotangent: bfloat16 [16384, 3072], P('row', 'col'), may hold values from -0.125 to 0.125
- teacher: bfloat16 [4096, 2048], P('row', 'col'), may hold values from -0.09375 to 0.09375
- expand_model: float32 [5120, 4096], P('row', 'col'), may hold values from -0.09375 to 0.09375
- expand_heads: float32 [3072, 2048], P('col', 'row'), may hold values from -0.125 to 0.125
Outputs:
- queries: float32 [16384, 3072], P('row', 'col')
- grad_model: float32 [5120, 4096], P('row', 'col')
- grad_heads: float32 [3072, 2048], P('col', 'row')
All inputs are finite; a program needn't handle non-finite values.
Results may differ from a plain program's by a relative error of at most 0.0029.
Values may be sent and summed in bfloat16 or wider, within the bound.
No kernel may reach another device: no remote copies, remote signals or barrier semaphores. Data moves between devices by JAX's collectives and lax.ppermute only.
A program may use at most 128 MiB of HBM per device.

v0:
```python
import jax
import jax.numpy as jnp
from jax import lax
from jax.experimental import pallas as pl
from jax.experimental.pallas import tpu as pltpu
from jax.sharding import Mesh, PartitionSpec as P

f32, f16, bf16 = jnp.float32, jnp.float16, jnp.bfloat16
HIGH = lax.Precision.HIGH
PAD = 16
TOP = 14.0
ROW, COL = ("yl", "z", "c"), ("yh", "x")
MIB = 2**20
VMEM, SMEM = pl.BlockSpec(memory_space=pltpu.VMEM), pl.BlockSpec(memory_space=pltpu.SMEM)


def swap(a, axis):
    return lax.ppermute(a, axis, [(0, 1), (1, 0)])


def after(a, *others):
    return lax.optimization_barrier((a, *others))[0]


def scale_of(top):
    return jnp.ceil(jnp.log2(jnp.maximum(top, 2.0**-100)))


def rows_of(a):
    return lax.broadcasted_iota(jnp.int32, a.shape, a.ndim - 2)


def payload(a):
    n = a.shape[-2] - PAD
    k = scale_of(a[..., n : n + 1, :])
    return jnp.where(rows_of(a) < n, a * jnp.exp2(TOP - k), k).astype(f16)


def dec(p):
    return p[..., :-PAD, :].astype(f32) * jnp.exp2(p[..., -1:, :].astype(f32) - TOP)


def enc(a):
    wide = jnp.pad(a, [(0, PAD), (0, 0)])
    k = scale_of(jnp.max(jnp.abs(a)))
    return jnp.where(rows_of(wide) < a.shape[0], wide * jnp.exp2(TOP - k), k).astype(f16)


def halves(a):
    high = a.astype(bf16)
    return high, (a - high.astype(f32)).astype(bf16)


def halves_outside(a):
    high = lax.reduce_precision(a, 8, 7)
    return high.astype(bf16), (a - high).astype(bf16)


def pair_y(a, yl):
    mate = swap(a, "yl")
    return jnp.stack([jnp.where(yl == 0, a, mate), jnp.where(yl == 0, mate, a)])


def gather_z(two):
    return lax.all_gather(two, "z").reshape((16,) + two.shape[1:])


def place(where, parts, shape, put):
    def kernel(where_ref, *refs):
        i = 0
        for src in refs[: len(parts)]:
            for j in range(src.shape[0]):
                put(refs[len(parts) :], where_ref[i], src[j])
                i += 1

    return pl.pallas_call(
        kernel,
        out_shape=shape,
        in_specs=[SMEM] + [VMEM] * len(parts),
        out_specs=jax.tree.map(lambda _: VMEM, shape),
        compiler_params=pltpu.CompilerParams(vmem_limit_bytes=24 * MIB),
    )(jnp.stack(where).astype(jnp.int32), *parts)


def put_rows(outs, at, block):
    outs[0][at] = block


def put_columns(outs, at, block):
    m = block.shape[1]
    outs[0][:, pl.ds(pl.multiple_of(at * m, 128), m)] = block


def put_teacher_heads(outs, at, block):
    teacher, heads = outs
    teacher[at] = block[:128]
    both = block[128:224].astype(f32) + block[224:].astype(f32)
    heads[at, :, :256] = both[:64]
    heads[at, :32, 256:] = both[64:, :128]
    heads[at, 32:, 256:] = both[64:, 128:]


def pack_teacher_heads(teacher, heads_t):
    rows = [teacher]
    for half in halves_outside(heads_t):
        rows += [half[:, :256], jnp.concatenate([half[:32, 256:], half[32:, 256:]], axis=1)]
    return jnp.concatenate(rows)


def weave(own, c, shape, put, pieces=1):
    where = [i * 16 + z * 2 + k for k in (c, 1 - c) for z in range(8) for i in (0, 1)]
    mine = jnp.split(own, pieces)
    return place(where, mine + [swap(p, "c") for p in mine], shape, put)


def pair_col(a):
    p = enc(a)
    return jnp.stack([p, swap(p, "yh")])


def gather_col(two, yh, x):
    parts = [two]
    parts += [lax.ppermute(two, "x", [(i, (i + d) % 4) for i in range(4)]) for d in (1, -1, 2)]
    where = [(yh ^ j) * 4 + ((x - d) & 3) for d in (0, 1, -1, 2) for j in (0, 1)]
    n, m = two.shape[1] - PAD, two.shape[2]
    shape = jax.ShapeDtypeStruct((n, 8 * m), f32)
    return place(where, [dec(p) for p in parts], shape, put_columns)


def swap_col(blocks):
    return lax.all_to_all(blocks, COL, 0, 0, tiled=True)


def sum_mates(keep, send):
    x = keep + swap(send, "c").astype(f32)
    return payload(x[1]), x[0]


def blocks_z(sent, own):
    mate = swap(sent, "yl")
    n = own.shape[1] - PAD
    k = mate[:, n : n + 1].astype(f32)
    got = jnp.where(rows_of(own) < n, mate.astype(f32) * jnp.exp2(k - TOP), jnp.exp2(k))
    return payload(own + got)


def parts_z(blocks, z):
    got = [lax.dynamic_index_in_dim(blocks, z, 0, keepdims=False)]
    for d in range(1, 8):
        block = lax.dynamic_index_in_dim(blocks, (z + d) & 7, 0, keepdims=False)
        got.append(lax.ppermute(block, "z", [(i, (i + d) % 8) for i in range(8)]))
    return got


def with_top(a, rows):
    return jnp.broadcast_to(jnp.max(jnp.abs(a), axis=0, keepdims=True), (rows, a.shape[1]))


def split_cores(core, total_ref, j, n, keep_ref, send_ref, at):
    keep = total_ref[pl.ds(pl.multiple_of(2 * n * j + n * core, 8), n), :]
    send = total_ref[pl.ds(pl.multiple_of(2 * n * j + n * (1 - core), 8), n), :]
    keep_ref[(*at, slice(0, n))] = keep
    keep_ref[(*at, slice(n, n + PAD))] = with_top(keep, PAD)
    send_ref[(*at, slice(0, n))] = send.astype(bf16)
    send_ref[(*at, slice(n, n + PAD))] = with_top(send, PAD).astype(bf16)


def weight_kernel(place_ref, tokens_ref, cotangent_ref, keep_ref, send_ref, total_ref):
    total_ref[...] = lax.dot_general(
        tokens_ref[...],
        cotangent_ref[...],
        (((0,), (0,)), ((), ())),
        preferred_element_type=f32,
    )
    for j in range(2):
        split_cores(place_ref[1], total_ref, j, 160, keep_ref, send_ref, (0, j))


def split_shapes(n):
    return [jax.ShapeDtypeStruct((2, 8, n + PAD, 384), kind) for kind in (f32, bf16)]


def weight_parts(yl, c, tokens, cotangent):
    block = pl.BlockSpec((1, 2, 160 + PAD, 384), lambda i, where: (where[0] ^ (i // 4), i % 4, 0, 0))
    return pl.pallas_call(
        weight_kernel,
        grid_spec=pltpu.PrefetchScalarGridSpec(
            num_scalar_prefetch=1,
            grid=(8,),
            in_specs=[
                pl.BlockSpec((512, 640), lambda i, where: (0, i)),
                pl.BlockSpec((512, 384), lambda i, where: (0, 0)),
            ],
            out_specs=[block, block],
            scratch_shapes=[pltpu.VMEM((640, 384), f32)],
        ),
        out_shape=split_shapes(160),
        compiler_params=pltpu.CompilerParams(vmem_limit_bytes=56 * MIB),
        cost_estimate=pl.CostEstimate(
            flops=2 * 512 * 5120 * 384, bytes_accessed=12 * MIB, transcendentals=0
        ),
    )(jnp.stack([yl, c]).astype(jnp.int32), tokens, cotangent)


def product(a, b, contract):
    return sum(
        lax.dot_general(u, v, (contract, ((), ())), preferred_element_type=f32)
        for u, v in ((a[0], b[0]), (a[0], b[1]), (a[1], b[0]))
    )


def share_kernel(place_ref, expanded_ref, grad_ref, keep_ref, send_ref, total_ref):
    grad = halves(grad_ref[...])
    for i in range(4):
        rows = slice(512 * i, 512 * i + 512)
        total_ref[rows] = product(halves(expanded_ref[:, rows]), grad, ((0,), (0,)))
    for j in range(16):
        split_cores(
            place_ref[1], total_ref, j, 64, keep_ref, send_ref, (place_ref[0] ^ (j // 8), j % 8)
        )


def share_parts(yl, c, expanded, grad):
    return pl.pallas_call(
        share_kernel,
        in_specs=[SMEM, VMEM, VMEM],
        out_specs=[VMEM, VMEM],
        out_shape=split_shapes(64),
        scratch_shapes=[pltpu.VMEM((2048, 384), f32)],
        compiler_params=pltpu.CompilerParams(vmem_limit_bytes=24 * MIB),
        cost_estimate=pl.CostEstimate(
            flops=6 * 160 * 2048 * 384, bytes_accessed=6 * MIB, transcendentals=0
        ),
    )(jnp.stack([yl, c]).astype(jnp.int32), expanded, grad)


def blocks_kernel(a_ref, b_ref, out_ref):
    a = halves(a_ref[...])
    n, m = a[0].shape[0], out_ref.shape[2]
    for q in range(8):
        b = b_ref[q * m : q * m + m, :]
        if b.dtype == bf16:
            total = sum(
                lax.dot_general(u, b, (((1,), (1,)), ((), ())), preferred_element_type=f32) for u in a
            )
        else:
            total = product(a, halves(b), ((1,), (1,)))
        out_ref[q, :n] = total
        out_ref[q, n:] = with_top(total, PAD)


def blocks_of(a, b):
    n, m = a.shape[0], b.shape[0] // 8
    return pl.pallas_call(
        blocks_kernel,
        in_specs=[VMEM, VMEM],
        out_specs=VMEM,
        out_shape=jax.ShapeDtypeStruct((8, n + PAD, m), f32),
        compiler_params=pltpu.CompilerParams(vmem_limit_bytes=24 * MIB),
        cost_estimate=pl.CostEstimate(
            flops=6 * a.shape[0] * b.size, bytes_accessed=6 * MIB, transcendentals=0
        ),
    )(a, b)


def shards(tokens, cotangent, teacher, expand_model, expand_heads):
    yl, z, c = [lax.axis_index(name) for name in ROW]
    yh, x = [lax.axis_index(name) for name in COL]

    packed = pair_y(pack_teacher_heads(teacher, expand_heads.T), yl)
    tokens_late = after(tokens, packed)
    sent, own = sum_mates(*weight_parts(yl, c, tokens_late, cotangent))
    packed = after(gather_z(packed), sent)
    model_two = after(pair_col(expand_model), sent)

    shapes = [jax.ShapeDtypeStruct((32, 128, 256), bf16), jax.ShapeDtypeStruct((32, 64, 384), f32)]
    teacher_block, heads = weave(packed, c, shapes, put_teacher_heads)
    teacher_block, heads = teacher_block.reshape(4096, 256), heads.reshape(2048, 384)
    model_rows = gather_col(model_two, yh, x)
    expanded_two = pair_col(jnp.dot(model_rows, teacher_block.astype(f32), precision=HIGH))
    expanded = gather_col(expanded_two, yh, x)
    blocks = lax.all_to_all(blocks_z(sent, own), "z", 0, 0, tiled=True)

    student = jnp.dot(expanded, heads, precision=HIGH).astype(bf16)
    student_two = pair_y(student, yl)
    student_own = gather_z(student_two)

    grad = jnp.sum(dec(after(blocks, student)), axis=0)
    sent, own = sum_mates(*share_parts(yl, c, expanded, grad))
    side = swap_col(payload(blocks_of(grad, heads)))
    side = jnp.sum(dec(after(side, sent, student_two)), axis=0)
    blocks = payload(blocks_of(side, teacher_block))
    grad_model = jnp.sum(dec(swap_col(blocks)), axis=0)
    shares = parts_z(after(blocks_z(sent, own), blocks), z)
    grad_heads = sum(dec(p) for p in shares).T

    shape = jax.ShapeDtypeStruct((32, 160, 384), bf16)
    student = weave(after(student_own, blocks), c, shape, put_rows, 4).reshape(5120, 384)
    queries = jnp.dot(tokens, student, preferred_element_type=f32)
    return (queries, grad_model, grad_heads)


def solution(mesh):
    mesh = Mesh(mesh.devices.reshape(2, 8, 2, 2, 4), ROW + COL)
    in_specs = (P(ROW, None), P(ROW, COL), P(ROW, COL), P(ROW, COL), P(COL, ROW))
    out_specs = (P(ROW, COL), P(ROW, COL), P(COL, ROW))
    return jax.shard_map(
        shards, mesh=mesh, in_specs=in_specs, out_specs=out_specs, check_vma=False
    )
```

profile of v0, /device:TPU:1, one launch (start us, length us, event | category | flops | bytes accessed | tf_op | source)
XLA Modules:
  0.0 205.0 jit_solution(992829480250220954)
XLA Ops:
  9.0 2.2 %collective-permute-start.1 = (bf16[320,256]{1,0:T(8,128)(2,1)S(1)}, bf16[320,256]{1,0:T(8,128)(2,1)S(1)}, u32[]{:S(2)}, u32[]{:S(2)}) collective-permute-start(bf16[320,256]{1,0:T(8,128)(2,1)S(1)} %maximum_dynamic-update-slice_fusion), channel_id=1, source_target_pairs={{0,128},{128,0},{1,129},{129,1},{2,130},{130,2},{3,131},{131,3},{4... | collective-permute-start | bytes 491528 | tf_op jit(solution)/shard_map/ppermute | solution.py:18
  11.2 2.7 %collective-permute-done.1 = bf16[320,256]{1,0:T(8,128)(2,1)S(1)} collective-permute-done((bf16[320,256]{1,0:T(8,128)(2,1)S(1)}, bf16[320,256]{1,0:T(8,128)(2,1)S(1)}, u32[]{:S(2)}, u32[]{:S(2)}) %collective-permute-start.1) | collective-permute-done | bytes 163872 | tf_op jit(solution)/shard_map/ppermute | solution.py:18
  15.4 10.3 %shard_map.76 = (f32[2,8,176,384]{3,2,1,0:T(8,128)}, bf16[2,8,176,384]{3,2,1,0:T(8,128)(2,1)}) custom-call(s32[2]{0:T(128)} %pad_add_fusion.place_ref, bf16[512,5120]{1,0:T(8,128)(2,1)} %tokens_ref, bf16[512,384]{1,0:T(8,128)(2,1)} %cotangent_ref.1), custom_call_target="tpu_custom_call" | custom-call | flops 2013265920 | bytes 12582912 | tf_op jit(solution)/shard_map/pallas_call | solution.py:185
  25.7 3.7 %collective-permute-start.2 = (bf16[2,8,176,384]{3,2,1,0:T(8,128)(2,1)}, bf16[2,8,176,384]{3,2,1,0:T(8,128)(2,1)S(1)}, u32[]{:S(2)}, u32[]{:S(2)}) collective-permute-start(bf16[2,8,176,384]{3,2,1,0:T(8,128)(2,1)} %get-tuple-element.18), channel_id=1, source_target_pairs={{0,8},{8,0},{1,9},{9,1},{2,10},{10,2},{3,11},{11,3},{4,12},{12,4},... | collective-permute-start | bytes 6488072 | tf_op jit(solution)/shard_map/ppermute | solution.py:18
  30.9 1.9 collective-permute-start
  33.1 5.6 %collective-permute-done = f16[176,512]{1,0:T(8,128)(2,1)S(1)} collective-permute-done((f16[176,512]{1,0:T(8,128)(2,1)S(1)}, f16[176,512]{1,0:T(8,128)(2,1)S(1)}, u32[]{:S(2)}, u32[]{:S(2)}) %collective-permute-start) | collective-permute-done | bytes 180256 | tf_op jit(solution)/shard_map/ppermute | solution.py:18
  38.8 2.8 %convert_add_fusion = f32[2,8,176,384]{3,2,1,0:T(8,128)S(1)} fusion(f32[2,8,176,384]{3,2,1,0:T(8,128)} %get-tuple-element.17, bf16[2,8,176,384]{3,2,1,0:T(8,128)(2,1)S(1)} %collective-permute-done.2), kind=kLoop, calls=%fused_computation | loop fusion | flops 2162688 | bytes 10813440 | tf_op jit(solution)/shard_map/add | solution.py:135
  41.8 1.8 copy-done.12
  45.3 2.7 %collective-permute-start.5 = (f16[2,176,512]{2,1,0:T(8,128)(2,1)S(1)}, f16[2,176,512]{2,1,0:T(8,128)(2,1)S(1)}, u32[]{:S(2)}, u32[]{:S(2)}) collective-permute-start(f16[2,176,512]{2,1,0:T(8,128)(2,1)S(1)} %pad_maximum_fusion), channel_id=1, source_target_pairs={{0,2},{1,3},{2,0},{3,1},{4,6},{5,7},{6,4},{7,5},{8,10},{9,11},{10,... | collective-permute-start | bytes 1081352 | tf_op jit(solution)/shard_map/ppermute | solution.py:123
  49.5 9.9 %all-gather.5.cloned.1.call-done.refs_0_ = bf16[16,320,256]{2,1,0:T(8,128)(2,1)} async-done(((bf16[2,320,256]{2,1,0:T(8,128)(2,1)}), bf16[16,320,256]{2,1,0:T(8,128)(2,1)}) %all-gather.5.cloned.1.call-update) | async-done | bytes 2621456 | tf_op jit(solution)/shard_map/all_gather | solution.py:65
  59.4 3.7 %collective-permute-start.6 = (bf16[16,320,256]{2,1,0:T(8,128)(2,1)}, bf16[16,320,256]{2,1,0:T(8,128)(2,1)S(1)}, u32[]{:S(2)}, u32[]{:S(2)}) collective-permute-start(bf16[16,320,256]{2,1,0:T(8,128)(2,1)} %all-gather.5.cloned.1.call-done.refs_0_), channel_id=1, source_target_pairs={{0,8},{8,0},{1,9},{9,1},{2,10},{10,2},{3,11},{11,3},{4,12},{12,4},... | collective-permute-start | bytes 7864328 | tf_op jit(solution)/shard_map/ppermute | solution.py:18
  71.1 1.6 fusion
  72.8 1.3 select_convert_fusion.1
  74.1 8.2 %all-to-all-start = ((f16[8,176,384]{2,1,0:T(8,128)(2,1)}), f16[8,176,384]{2,1,0:T(8,128)(2,1)}, u32[]{:S(2)}, u32[]{:S(2)}) async-start(f16[8,176,384]{2,1,0:T(8,128)(2,1)} %select_convert_fusion.1), calls=%async_computation | async-start | bytes 2162688 | tf_op jit(solution)/shard_map/all_to_all | solution.py:282
  82.3 1.5 copy-done.7
  83.8 2.0 copy-done.6
  85.8 1.7 copy-done.8
  88.4 1.5 abs_reduce_fusion.1
  90.7 2.6 %collective-permute-start.7 = (f16[176,256]{1,0:T(8,128)(2,1)S(1)}, f16[176,256]{1,0:T(8,128)(2,1)S(1)}, u32[]{:S(2)}, u32[]{:S(2)}) collective-permute-start(f16[176,256]{1,0:T(8,128)(2,1)S(1)} %select_convert_fusion.7), channel_id=1, source_target_pairs={{0,4},{4,0},{1,5},{5,1},{2,6},{6,2},{3,7},{7,3},{8,12},{12,8},{9,1... | collective-permute-start | bytes 270344 | tf_op jit(solution)/shard_map/ppermute | solution.py:18
  93.4 2.7 %collective-permute-done.7 = f16[176,256]{1,0:T(8,128)(2,1)S(1)} collective-permute-done((f16[176,256]{1,0:T(8,128)(2,1)S(1)}, f16[176,256]{1,0:T(8,128)(2,1)S(1)}, u32[]{:S(2)}, u32[]{:S(2)}) %collective-permute-start.7) | collective-permute-done | bytes 90144 | tf_op jit(solution)/shard_map/ppermute | solution.py:18
  96.1 2.8 %collective-permute-start.10 = (f16[2,176,256]{2,1,0:T(8,128)(2,1)S(1)}, f16[2,176,256]{2,1,0:T(8,128)(2,1)S(1)}, u32[]{:S(2)}, u32[]{:S(2)}) collective-permute-start(f16[2,176,256]{2,1,0:T(8,128)(2,1)S(1)} %pad_maximum_fusion.3), channel_id=1, source_target_pairs={{0,2},{1,3},{2,0},{3,1},{4,6},{5,7},{6,4},{7,5},{8,10},{9,11},{10,... | collective-permute-start | bytes 540680 | tf_op jit(solution)/shard_map/ppermute | solution.py:123
  99.0 1.7 collective-permute-start.9
  100.7 1.8 collective-permute-done.10
  102.5 4.7 %collective-permute-done.9 = f16[2,176,256]{2,1,0:T(8,128)(2,1)S(1)} collective-permute-done((f16[2,176,256]{2,1,0:T(8,128)(2,1)S(1)}, f16[2,176,256]{2,1,0:T(8,128)(2,1)S(1)}, u32[]{:S(2)}, u32[]{:S(2)}) %collective-permute-start.9) | collective-permute-done | bytes 180256 | tf_op jit(solution)/shard_map/ppermute | solution.py:123
  107.2 1.3 collective-permute-done.8
  109.3 1.5 convolution_convert_fusion
  113.1 1.4 multiply_reduce_fusion.1.a_ref.grad_ref
  115.9 3.6 %shard_map.81 = (f32[2,8,80,384]{3,2,1,0:T(8,128)S(1)}, bf16[2,8,80,384]{3,2,1,0:T(8,128)(2,1)}) custom-call(s32[2]{0:T(128)S(1)} %copy-done.11, f32[160,2048]{1,0:T(8,128)S(1)} %copy-done.5, f32[160,384]{1,0:T(8,128)S(1)} %multiply_reduce_fusion.1.a_ref.grad_ref), custom_call_target="tpu_custom_call" | custom-call | flops 754974720 | bytes 6291456 | tf_op jit(solution)/shard_map/pallas_call | solution.py:224
  122.0 1.7 shard_map.80
  124.9 6.6 %all-to-all-start.1 = ((f16[8,176,256]{2,1,0:T(8,128)(2,1)}), f16[8,176,256]{2,1,0:T(8,128)(2,1)S(1)}, u32[]{:S(2)}, u32[]{:S(2)}) async-start(f16[8,176,256]{2,1,0:T(8,128)(2,1)} %select_convert_fusion.3), calls=%async_computation.1 | async-start | bytes 1441792 | tf_op jit(solution)/shard_map/all_to_all | solution.py:131
  133.3 1.4 convert_add_fusion.1
  137.3 8.0 %all-to-all-done.1 = f16[8,176,256]{2,1,0:T(8,128)(2,1)S(1)} async-done(((f16[8,176,256]{2,1,0:T(8,128)(2,1)}), f16[8,176,256]{2,1,0:T(8,128)(2,1)S(1)}, u32[]{:S(2)}, u32[]{:S(2)}) %all-to-all-start.1) | async-done | bytes 720928 | tf_op jit(solution)/shard_map/all_to_all | solution.py:131
  145.5 1.5 shard_map.82
  147.2 1.7 select_convert_fusion
  148.9 3.6 %collective-permute-done.18 = f16[8,80,384]{2,1,0:T(8,128)(2,1)S(1)} collective-permute-done((f16[8,80,384]{2,1,0:T(8,128)(2,1)}, f16[8,80,384]{2,1,0:T(8,128)(2,1)S(1)}, u32[]{:S(2)}, u32[]{:S(2)}) %collective-permute-start.18) | collective-permute-done | bytes 491552 | tf_op jit(solution)/shard_map/ppermute | solution.py:18
  153.1 1.8 collective-permute-start.25
  155.0 6.4 %all-to-all-start.2 = ((f16[8,176,512]{2,1,0:T(8,128)(2,1)}), f16[8,176,512]{2,1,0:T(8,128)(2,1)}, u32[]{:S(2)}, u32[]{:S(2)}) async-start(f16[8,176,512]{2,1,0:T(8,128)(2,1)} %select_convert_fusion), calls=%async_computation.2 | async-start | bytes 2883584 | tf_op jit(solution)/shard_map/all_to_all | solution.py:131
  161.4 2.1 %collective-permute-start.24 = (f16[80,384]{1,0:T(8,128)(2,1)S(1)}, f16[80,384]{1,0:T(8,128)(2,1)S(1)}, u32[]{:S(2)}, u32[]{:S(2)}) collective-permute-start(f16[80,384]{1,0:T(8,128)(2,1)S(1)} %get-tuple-element.58), channel_id=1, source_target_pairs={{0,96},{16,112},{32,0},{48,16},{64,32},{80,48},{96,64},{112,80},{1... | collective-permute-start | bytes 184328 | tf_op jit(solution)/shard_map/ppermute | solution.py:151
  164.7 3.3 %collective-permute-start.22 = (f16[80,384]{1,0:T(8,128)(2,1)S(1)}, f16[80,384]{1,0:T(8,128)(2,1)S(1)}, u32[]{:S(2)}, u32[]{:S(2)}) collective-permute-start(f16[80,384]{1,0:T(8,128)(2,1)S(1)} %get-tuple-element.60), channel_id=1, source_target_pairs={{0,64},{16,80},{32,96},{48,112},{64,0},{80,16},{96,32},{112,48},{1... | collective-permute-start | bytes 184328 | tf_op jit(solution)/shard_map/ppermute | solution.py:151
  168.0 3.3 %collective-permute-start.20 = (f16[80,384]{1,0:T(8,128)(2,1)S(1)}, f16[80,384]{1,0:T(8,128)(2,1)S(1)}, u32[]{:S(2)}, u32[]{:S(2)}) collective-permute-start(f16[80,384]{1,0:T(8,128)(2,1)S(1)} %get-tuple-element.62), channel_id=1, source_target_pairs={{0,32},{16,48},{32,64},{48,80},{64,96},{80,112},{96,0},{112,16},{1... | collective-permute-start | bytes 184328 | tf_op jit(solution)/shard_map/ppermute | solution.py:151
  173.7 5.6 %collective-permute-done.21 = f16[80,384]{1,0:T(8,128)(2,1)S(1)} collective-permute-done((f16[80,384]{1,0:T(8,128)(2,1)S(1)}, f16[80,384]{1,0:T(8,128)(2,1)S(1)}, u32[]{:S(2)}, u32[]{:S(2)}) %collective-permute-start.21) | collective-permute-done | bytes 61472 | tf_op jit(solution)/shard_map/ppermute | solution.py:151
  179.3 1.7 collective-permute-done.20
  181.0 3.2 %collective-permute-done.19 = f16[80,384]{1,0:T(8,128)(2,1)S(1)} collective-permute-done((f16[80,384]{1,0:T(8,128)(2,1)S(1)}, f16[80,384]{1,0:T(8,128)(2,1)S(1)}, u32[]{:S(2)}, u32[]{:S(2)}) %collective-permute-start.19) | collective-permute-done | bytes 61472 | tf_op jit(solution)/shard_map/ppermute | solution.py:151
  184.8 1.7 fusion.89
  188.3 1.5 fusion.11
  190.7 2.5 %multiply_reduce_fusion = f32[160,512]{1,0:T(8,128)} fusion(f16[8,176,512]{2,1,0:T(8,128)(2,1)} %all-to-all-done.2, f32[8,512]{1,0:T(8,128)S(1)} %bitcast.198), kind=kLoop, calls=%fused_computation.2 | loop fusion | flops 1884160 | bytes 1654784 | tf_op jit(solution)/shard_map/reduce_sum | solution.py:293
  193.2 1.5 shard_map.83
  194.7 2.2 %convolution_bitcast_fusion = f32[512,384]{0,1:T(8,128)S(1)} fusion(bf16[5120,384]{1,0:T(8,128)(2,1)S(1)} %bitcast.191, bf16[512,5120]{1,0:T(8,128)(2,1)S(1)} %bitcast.224), kind=kOutput, calls=%fused_computation.12 | convolution fusion | flops 2013265920 | bytes 9961472 | tf_op jit(solution)/shard_map/dot_general | solution.py:299
  (196 shorter events, 38.0 us)
Async XLA Ops:
  7.2 52.3 %all-gather.5.cloned.1.call-start = ((), (), s32[]{:S(2)}) async-start(), calls=%async_computation.3 | async-start | bytes 2949120 | tf_op jit(solution)/shard_map/all_gather | solution.py:65
  9.0 4.9 %collective-permute-start.1 = (bf16[320,256]{1,0:T(8,128)(2,1)S(1)}, bf16[320,256]{1,0:T(8,128)(2,1)S(1)}, u32[]{:S(2)}, u32[]{:S(2)}) collective-permute-start(bf16[320,256]{1,0:T(8,128)(2,1)S(1)} %maximum_dynamic-update-slice_fusion), channel_id=1, source_target_pairs={{0,128},{128,0},{1,129},{129,1},{2,130},{130,2},{3,131},{131,3},{4... | collective-permute-start | bytes 491528 | tf_op jit(solution)/shard_map/ppermute | solution.py:18
  15.4 14.0 %copy-start.16 = (f32[160,512]{1,0:T(8,128)S(1)}, f32[160,512]{1,0:T(8,128)}, u32[]{:S(2)}) copy-start(f32[160,512]{1,0:T(8,128)} %param.8) | copy-start | bytes 983044
  25.7 13.1 %collective-permute-start.2 = (bf16[2,8,176,384]{3,2,1,0:T(8,128)(2,1)}, bf16[2,8,176,384]{3,2,1,0:T(8,128)(2,1)S(1)}, u32[]{:S(2)}, u32[]{:S(2)}) collective-permute-start(bf16[2,8,176,384]{3,2,1,0:T(8,128)(2,1)} %get-tuple-element.18), channel_id=1, source_target_pairs={{0,8},{8,0},{1,9},{9,1},{2,10},{10,2},{3,11},{11,3},{4,12},{12,4},... | collective-permute-start | bytes 6488072 | tf_op jit(solution)/shard_map/ppermute | solution.py:18
  30.9 7.8 %collective-permute-start = (f16[176,512]{1,0:T(8,128)(2,1)S(1)}, f16[176,512]{1,0:T(8,128)(2,1)S(1)}, u32[]{:S(2)}, u32[]{:S(2)}) collective-permute-start(f16[176,512]{1,0:T(8,128)(2,1)S(1)} %select_convert_fusion.6), channel_id=1, source_target_pairs={{0,4},{4,0},{1,5},{5,1},{2,6},{6,2},{3,7},{7,3},{8,12},{12,8},{9,1... | collective-permute-start | bytes 540680 | tf_op jit(solution)/shard_map/ppermute | solution.py:18
  44.9 24.9 %collective-permute-start.12 = (f16[8,176,384]{2,1,0:T(8,128)(2,1)}, f16[8,176,384]{2,1,0:T(8,128)(2,1)}, u32[]{:S(2)}, u32[]{:S(2)}) collective-permute-start(f16[8,176,384]{2,1,0:T(8,128)(2,1)} %select_convert_fusion.2), channel_id=1, source_target_pairs={{0,128},{128,0},{1,129},{129,1},{2,130},{130,2},{3,131},{131,3},{4... | collective-permute-start | bytes 3244040 | tf_op jit(solution)/shard_map/ppermute | solution.py:18
  45.3 17.9 %collective-permute-start.5 = (f16[2,176,512]{2,1,0:T(8,128)(2,1)S(1)}, f16[2,176,512]{2,1,0:T(8,128)(2,1)S(1)}, u32[]{:S(2)}, u32[]{:S(2)}) collective-permute-start(f16[2,176,512]{2,1,0:T(8,128)(2,1)S(1)} %pad_maximum_fusion), channel_id=1, source_target_pairs={{0,2},{1,3},{2,0},{3,1},{4,6},{5,7},{6,4},{7,5},{8,10},{9,11},{10,... | collective-permute-start | bytes 1081352 | tf_op jit(solution)/shard_map/ppermute | solution.py:123
  48.0 15.9 %collective-permute-start.4 = (f16[2,176,512]{2,1,0:T(8,128)(2,1)S(1)}, f16[2,176,512]{2,1,0:T(8,128)(2,1)}, u32[]{:S(2)}, u32[]{:S(2)}) collective-permute-start(f16[2,176,512]{2,1,0:T(8,128)(2,1)S(1)} %pad_maximum_fusion), channel_id=1, source_target_pairs={{0,3},{1,0},{2,1},{3,2},{4,7},{5,4},{6,5},{7,6},{8,11},{9,8},{10,9... | collective-permute-start | bytes 1081352 | tf_op jit(solution)/shard_map/ppermute | solution.py:123
  48.9 16.1 %collective-permute-start.3 = (f16[2,176,512]{2,1,0:T(8,128)(2,1)S(1)}, f16[2,176,512]{2,1,0:T(8,128)(2,1)}, u32[]{:S(2)}, u32[]{:S(2)}) collective-permute-start(f16[2,176,512]{2,1,0:T(8,128)(2,1)S(1)} %pad_maximum_fusion), channel_id=1, source_target_pairs={{0,1},{1,2},{2,3},{3,0},{4,5},{5,6},{6,7},{7,4},{8,9},{9,10},{10,1... | collective-permute-start | bytes 1081352 | tf_op jit(solution)/shard_map/ppermute | solution.py:123
  59.4 22.9 %collective-permute-start.6 = (bf16[16,320,256]{2,1,0:T(8,128)(2,1)}, bf16[16,320,256]{2,1,0:T(8,128)(2,1)S(1)}, u32[]{:S(2)}, u32[]{:S(2)}) collective-permute-start(bf16[16,320,256]{2,1,0:T(8,128)(2,1)} %all-gather.5.cloned.1.call-done.refs_0_), channel_id=1, source_target_pairs={{0,8},{8,0},{1,9},{9,1},{2,10},{10,2},{3,11},{11,3},{4,12},{12,4},... | collective-permute-start | bytes 7864328 | tf_op jit(solution)/shard_map/ppermute | solution.py:18
  68.6 4.1 %copy-start = (f32[160,4096]{1,0:T(8,128)}, f32[160,4096]{1,0:T(8,128)S(1)}, u32[]{:S(2)}) copy-start(f32[160,4096]{1,0:T(8,128)S(1)} %shard_map.77) | copy-start | bytes 7864324
  74.1 38.2 %all-to-all-start = ((f16[8,176,384]{2,1,0:T(8,128)(2,1)}), f16[8,176,384]{2,1,0:T(8,128)(2,1)}, u32[]{:S(2)}, u32[]{:S(2)}) async-start(f16[8,176,384]{2,1,0:T(8,128)(2,1)} %select_convert_fusion.1), calls=%async_computation | async-start | bytes 2162688 | tf_op jit(solution)/shard_map/all_to_all | solution.py:282
  82.3 6.1 %copy-start.1 = (f32[160,4096]{1,0:T(8,128)S(1)}, f32[160,4096]{1,0:T(8,128)}, u32[]{:S(2)}) copy-start(f32[160,4096]{1,0:T(8,128)} %copy-done) | copy-start | bytes 7864324
  90.7 5.4 %collective-permute-start.7 = (f16[176,256]{1,0:T(8,128)(2,1)S(1)}, f16[176,256]{1,0:T(8,128)(2,1)S(1)}, u32[]{:S(2)}, u32[]{:S(2)}) collective-permute-start(f16[176,256]{1,0:T(8,128)(2,1)S(1)} %select_convert_fusion.7), channel_id=1, source_target_pairs={{0,4},{4,0},{1,5},{5,1},{2,6},{6,2},{3,7},{7,3},{8,12},{12,8},{9,1... | collective-permute-start | bytes 270344 | tf_op jit(solution)/shard_map/ppermute | solution.py:18
  96.1 6.3 %collective-permute-start.10 = (f16[2,176,256]{2,1,0:T(8,128)(2,1)S(1)}, f16[2,176,256]{2,1,0:T(8,128)(2,1)S(1)}, u32[]{:S(2)}, u32[]{:S(2)}) collective-permute-start(f16[2,176,256]{2,1,0:T(8,128)(2,1)S(1)} %pad_maximum_fusion.3), channel_id=1, source_target_pairs={{0,2},{1,3},{2,0},{3,1},{4,6},{5,7},{6,4},{7,5},{8,10},{9,11},{10,... | collective-permute-start | bytes 540680 | tf_op jit(solution)/shard_map/ppermute | solution.py:123
  99.0 8.2 %collective-permute-start.9 = (f16[2,176,256]{2,1,0:T(8,128)(2,1)S(1)}, f16[2,176,256]{2,1,0:T(8,128)(2,1)S(1)}, u32[]{:S(2)}, u32[]{:S(2)}) collective-permute-start(f16[2,176,256]{2,1,0:T(8,128)(2,1)S(1)} %pad_maximum_fusion.3), channel_id=1, source_target_pairs={{0,3},{1,0},{2,1},{3,2},{4,7},{5,4},{6,5},{7,6},{8,11},{9,8},{10,9... | collective-permute-start | bytes 540680 | tf_op jit(solution)/shard_map/ppermute | solution.py:123
  100.6 7.9 %collective-permute-start.8 = (f16[2,176,256]{2,1,0:T(8,128)(2,1)S(1)}, f16[2,176,256]{2,1,0:T(8,128)(2,1)S(1)}, u32[]{:S(2)}, u32[]{:S(2)}) collective-permute-start(f16[2,176,256]{2,1,0:T(8,128)(2,1)S(1)} %pad_maximum_fusion.3), channel_id=1, source_target_pairs={{0,1},{1,2},{2,3},{3,0},{4,5},{5,6},{6,7},{7,4},{8,9},{9,10},{10,1... | collective-permute-start | bytes 540680 | tf_op jit(solution)/shard_map/ppermute | solution.py:123
  109.3 5.2 %copy-start.11 = (s32[2]{0:T(128)S(1)}, s32[2]{0:T(128)}, u32[]{:S(2)}) copy-start(s32[2]{0:T(128)} %pad_add_fusion.place_ref) | copy-start | bytes 28
  120.8 12.5 %collective-permute-start.13 = (bf16[2,8,80,384]{3,2,1,0:T(8,128)(2,1)}, bf16[2,8,80,384]{3,2,1,0:T(8,128)(2,1)}, u32[]{:S(2)}, u32[]{:S(2)}) collective-permute-start(bf16[2,8,80,384]{3,2,1,0:T(8,128)(2,1)} %get-tuple-element.25), channel_id=1, source_target_pairs={{0,8},{8,0},{1,9},{9,1},{2,10},{10,2},{3,11},{11,3},{4,12},{12,4},... | collective-permute-start | bytes 2949128 | tf_op jit(solution)/shard_map/ppermute | solution.py:18
  121.9 9.6 %collective-permute-start.11 = (bf16[160,384]{1,0:T(8,128)(2,1)S(1)}, bf16[160,384]{1,0:T(8,128)(2,1)}, u32[]{:S(2)}, u32[]{:S(2)}) collective-permute-start(bf16[160,384]{1,0:T(8,128)(2,1)S(1)} %convolution_convert_fusion), channel_id=1, source_target_pairs={{0,128},{128,0},{1,129},{129,1},{2,130},{130,2},{3,131},{131,3},{4... | collective-permute-start | bytes 368648 | tf_op jit(solution)/shard_map/ppermute | solution.py:18
  123.8 9.4 %copy-start.10 = (f32[2,8,80,384]{3,2,1,0:T(8,128)S(1)}, f32[2,8,80,384]{3,2,1,0:T(8,128)}, u32[]{:S(2)}) copy-start(f32[2,8,80,384]{3,2,1,0:T(8,128)} %copy-done.9) | copy-start | bytes 5898244
  124.9 20.4 %all-to-all-start.1 = ((f16[8,176,256]{2,1,0:T(8,128)(2,1)}), f16[8,176,256]{2,1,0:T(8,128)(2,1)S(1)}, u32[]{:S(2)}, u32[]{:S(2)}) async-start(f16[8,176,256]{2,1,0:T(8,128)(2,1)} %select_convert_fusion.3), calls=%async_computation.1 | async-start | bytes 1441792 | tf_op jit(solution)/shard_map/all_to_all | solution.py:131
  131.5 53.3 %all-gather.7.cloned.1.call-start = ((), (), s32[]{:S(2)}) async-start(), calls=%async_computation.4 | async-start | bytes 2211840 | tf_op jit(solution)/shard_map/all_gather | solution.py:65
  134.7 10.8 %copy-start.3 = (bf16[32,128,256]{2,1,0:T(8,128)(2,1)S(1)}, bf16[32,128,256]{2,1,0:T(8,128)(2,1)}, u32[]{:S(2)}) copy-start(bf16[32,128,256]{2,1,0:T(8,128)(2,1)} %copy-done.2) | copy-start | bytes 6291460
  137.0 15.4 %collective-permute-start.18 = (f16[8,80,384]{2,1,0:T(8,128)(2,1)}, f16[8,80,384]{2,1,0:T(8,128)(2,1)S(1)}, u32[]{:S(2)}, u32[]{:S(2)}) collective-permute-start(f16[8,80,384]{2,1,0:T(8,128)(2,1)} %select_convert_fusion.5), channel_id=1, source_target_pairs={{0,128},{128,0},{1,129},{129,1},{2,130},{130,2},{3,131},{131,3},{4... | collective-permute-start | bytes 1474568 | tf_op jit(solution)/shard_map/ppermute | solution.py:18
  147.1 5.3 %copy-start.15 = (f32[2,8,80,384]{3,2,1,0:T(8,128)S(1)}, f32[2,8,80,384]{3,2,1,0:T(8,128)}, u32[]{:S(2)}) copy-start(f32[2,8,80,384]{3,2,1,0:T(8,128)} %copy-done.14) | copy-start | bytes 5898244
  153.0 31.2 %copy-start.17 = (f16[8,80,384]{2,1,0:T(8,128)(2,1)}, f16[8,80,384]{2,1,0:T(8,128)(2,1)S(1)}, u32[]{:S(2)}) copy-start(f16[8,80,384]{2,1,0:T(8,128)(2,1)S(1)} %select_convert_fusion.4) | copy-start | bytes 1474564
  153.1 14.8 %collective-permute-start.25 = (f16[80,384]{1,0:T(8,128)(2,1)S(1)}, f16[80,384]{1,0:T(8,128)(2,1)S(1)}, u32[]{:S(2)}, u32[]{:S(2)}) collective-permute-start(f16[80,384]{1,0:T(8,128)(2,1)S(1)} %get-tuple-element.57), channel_id=1, source_target_pairs={{0,112},{16,0},{32,16},{48,32},{64,48},{80,64},{96,80},{112,96},{1... | collective-permute-start | bytes 184328 | tf_op jit(solution)/shard_map/ppermute | solution.py:151
  155.0 34.8 %all-to-all-start.2 = ((f16[8,176,512]{2,1,0:T(8,128)(2,1)}), f16[8,176,512]{2,1,0:T(8,128)(2,1)}, u32[]{:S(2)}, u32[]{:S(2)}) async-start(f16[8,176,512]{2,1,0:T(8,128)(2,1)} %select_convert_fusion), calls=%async_computation.2 | async-start | bytes 2883584 | tf_op jit(solution)/shard_map/all_to_all | solution.py:131
  161.4 10.0 %collective-permute-start.24 = (f16[80,384]{1,0:T(8,128)(2,1)S(1)}, f16[80,384]{1,0:T(8,128)(2,1)S(1)}, u32[]{:S(2)}, u32[]{:S(2)}) collective-permute-start(f16[80,384]{1,0:T(8,128)(2,1)S(1)} %get-tuple-element.58), channel_id=1, source_target_pairs={{0,96},{16,112},{32,0},{48,16},{64,32},{80,48},{96,64},{112,80},{1... | collective-permute-start | bytes 184328 | tf_op jit(solution)/shard_map/ppermute | solution.py:151
  163.5 9.2 %collective-permute-start.23 = (f16[80,384]{1,0:T(8,128)(2,1)S(1)}, f16[80,384]{1,0:T(8,128)(2,1)S(1)}, u32[]{:S(2)}, u32[]{:S(2)}) collective-permute-start(f16[80,384]{1,0:T(8,128)(2,1)S(1)} %get-tuple-element.59), channel_id=1, source_target_pairs={{0,80},{16,96},{32,112},{48,0},{64,16},{80,32},{96,48},{112,64},{1... | collective-permute-start | bytes 184328 | tf_op jit(solution)/shard_map/ppermute | solution.py:151
  164.7 9.0 %collective-permute-start.22 = (f16[80,384]{1,0:T(8,128)(2,1)S(1)}, f16[80,384]{1,0:T(8,128)(2,1)S(1)}, u32[]{:S(2)}, u32[]{:S(2)}) collective-permute-start(f16[80,384]{1,0:T(8,128)(2,1)S(1)} %get-tuple-element.60), channel_id=1, source_target_pairs={{0,64},{16,80},{32,96},{48,112},{64,0},{80,16},{96,32},{112,48},{1... | collective-permute-start | bytes 184328 | tf_op jit(solution)/shard_map/ppermute | solution.py:151
  167.9 11.3 %collective-permute-start.21 = (f16[80,384]{1,0:T(8,128)(2,1)S(1)}, f16[80,384]{1,0:T(8,128)(2,1)S(1)}, u32[]{:S(2)}, u32[]{:S(2)}) collective-permute-start(f16[80,384]{1,0:T(8,128)(2,1)S(1)} %get-tuple-element.61), channel_id=1, source_target_pairs={{0,48},{16,64},{32,80},{48,96},{64,112},{80,0},{96,16},{112,32},{1... | collective-permute-start | bytes 184328 | tf_op jit(solution)/shard_map/ppermute | solution.py:151
  168.0 13.0 %collective-permute-start.20 = (f16[80,384]{1,0:T(8,128)(2,1)S(1)}, f16[80,384]{1,0:T(8,128)(2,1)S(1)}, u32[]{:S(2)}, u32[]{:S(2)}) collective-permute-start(f16[80,384]{1,0:T(8,128)(2,1)S(1)} %get-tuple-element.62), channel_id=1, source_target_pairs={{0,32},{16,48},{32,64},{48,80},{64,96},{80,112},{96,0},{112,16},{1... | collective-permute-start | bytes 184328 | tf_op jit(solution)/shard_map/ppermute | solution.py:151
  171.3 12.9 %copy-start.18 = (f16[80,384]{1,0:T(8,128)(2,1)}, f16[80,384]{1,0:T(8,128)(2,1)S(1)}, u32[]{:S(2)}) copy-start(f16[80,384]{1,0:T(8,128)(2,1)S(1)} %collective-permute-done.24) | copy-start | bytes 184324
  171.4 12.8 %collective-permute-start.19 = (f16[80,384]{1,0:T(8,128)(2,1)S(1)}, f16[80,384]{1,0:T(8,128)(2,1)S(1)}, u32[]{:S(2)}, u32[]{:S(2)}) collective-permute-start(f16[80,384]{1,0:T(8,128)(2,1)S(1)} %get-tuple-element.56), channel_id=1, source_target_pairs={{0,16},{16,32},{32,48},{48,64},{64,80},{80,96},{96,112},{112,0},{1... | collective-permute-start | bytes 184328 | tf_op jit(solution)/shard_map/ppermute | solution.py:151
  172.7 11.6 %copy-start.20 = (f16[80,384]{1,0:T(8,128)(2,1)}, f16[80,384]{1,0:T(8,128)(2,1)S(1)}, u32[]{:S(2)}) copy-start(f16[80,384]{1,0:T(8,128)(2,1)S(1)} %collective-permute-done.23) | copy-start | bytes 184324
  173.7 10.6 %copy-start.22 = (f16[80,384]{1,0:T(8,128)(2,1)}, f16[80,384]{1,0:T(8,128)(2,1)S(1)}, u32[]{:S(2)}) copy-start(f16[80,384]{1,0:T(8,128)(2,1)S(1)} %collective-permute-done.22) | copy-start | bytes 184324
  179.2 5.0 %copy-start.24 = (f16[80,384]{1,0:T(8,128)(2,1)}, f16[80,384]{1,0:T(8,128)(2,1)S(1)}, u32[]{:S(2)}) copy-start(f16[80,384]{1,0:T(8,128)(2,1)S(1)} %collective-permute-done.21) | copy-start | bytes 184324
  184.8 3.4 %copy-start.19 = (f16[80,384]{1,0:T(8,128)(2,1)S(1)}, f16[80,384]{1,0:T(8,128)(2,1)}, u32[]{:S(2)}) copy-start(f16[80,384]{1,0:T(8,128)(2,1)} %copy-done.18) | copy-start | bytes 184324
  184.8 3.4 %copy-start.21 = (f16[80,384]{1,0:T(8,128)(2,1)S(1)}, f16[80,384]{1,0:T(8,128)(2,1)}, u32[]{:S(2)}) copy-start(f16[80,384]{1,0:T(8,128)(2,1)} %copy-done.20) | copy-start | bytes 184324
  184.8 3.4 %copy-start.23 = (f16[80,384]{1,0:T(8,128)(2,1)S(1)}, f16[80,384]{1,0:T(8,128)(2,1)}, u32[]{:S(2)}) copy-start(f16[80,384]{1,0:T(8,128)(2,1)} %copy-done.22) | copy-start | bytes 184324
  184.8 3.4 %copy-start.25 = (f16[80,384]{1,0:T(8,128)(2,1)S(1)}, f16[80,384]{1,0:T(8,128)(2,1)}, u32[]{:S(2)}) copy-start(f16[80,384]{1,0:T(8,128)(2,1)} %copy-done.24) | copy-start | bytes 184324
  186.6 6.6 %collective-permute-start.14 = (bf16[4,160,384]{2,1,0:T(8,128)(2,1)S(1)}, bf16[4,160,384]{2,1,0:T(8,128)(2,1)S(1)}, u32[]{:S(2)}, u32[]{:S(2)}) collective-permute-start(bf16[4,160,384]{2,1,0:T(8,128)(2,1)S(1)} %get-tuple-element.53.refs_0_), channel_id=1, source_target_pairs={{0,8},{8,0},{1,9},{9,1},{2,10},{10,2},{3,11},{11,3},{4,12},{12,4},... | collective-permute-start | bytes 1474568 | tf_op jit(solution)/shard_map/ppermute | solution.py:18
  187.6 5.6 %collective-permute-start.15 = (bf16[4,160,384]{2,1,0:T(8,128)(2,1)S(1)}, bf16[4,160,384]{2,1,0:T(8,128)(2,1)S(1)}, u32[]{:S(2)}, u32[]{:S(2)}) collective-permute-start(bf16[4,160,384]{2,1,0:T(8,128)(2,1)S(1)} %get-tuple-element.52.refs_1_), channel_id=1, source_target_pairs={{0,8},{8,0},{1,9},{9,1},{2,10},{10,2},{3,11},{11,3},{4,12},{12,4},... | collective-permute-start | bytes 1474568 | tf_op jit(solution)/shard_map/ppermute | solution.py:18
  187.7 5.5 %collective-permute-start.16 = (bf16[4,160,384]{2,1,0:T(8,128)(2,1)S(1)}, bf16[4,160,384]{2,1,0:T(8,128)(2,1)S(1)}, u32[]{:S(2)}, u32[]{:S(2)}) collective-permute-start(bf16[4,160,384]{2,1,0:T(8,128)(2,1)S(1)} %get-tuple-element.51.refs_2_), channel_id=1, source_target_pairs={{0,8},{8,0},{1,9},{9,1},{2,10},{10,2},{3,11},{11,3},{4,12},{12,4},... | collective-permute-start | bytes 1474568 | tf_op jit(solution)/shard_map/ppermute | solution.py:18
  188.1 5.1 %collective-permute-start.17 = (bf16[4,160,384]{2,1,0:T(8,128)(2,1)S(1)}, bf16[4,160,384]{2,1,0:T(8,128)(2,1)}, u32[]{:S(2)}, u32[]{:S(2)}) collective-permute-start(bf16[4,160,384]{2,1,0:T(8,128)(2,1)S(1)} %get-tuple-element.50.refs_3_), channel_id=1, source_target_pairs={{0,8},{8,0},{1,9},{9,1},{2,10},{10,2},{3,11},{11,3},{4,12},{12,4},... | collective-permute-start | bytes 1474568 | tf_op jit(solution)/shard_map/ppermute | solution.py:18
  190.7 4.0 %slice-start = ((s8[5242880]{0:T(1024)(128)(4,1)}), s8[4194304]{0:T(1024)(128)(4,1)S(1)}, s32[]{:S(2)}) async-start(s8[5242880]{0:T(1024)(128)(4,1)} %bitcast.223), calls=%async_computation.5 | async-start | bytes 8388608
  (15 other events, 29.2 us)
Sparse Core Ops, SparseCore 0:
  14.9 44.4 all-gather.4
  134.7 47.4 all-gather.6
where the time goes:
time: 206 us; the launch traced here: 205 us
  starting transfers between devices  60.7 us (29%)
  waiting for transfers between devices  54.3 us (26%)
  other arithmetic  30.7 us (15%)
  Pallas kernels  20.8 us (10%)
  local copies, waits for them, and re-layouts  16.9 us (8%)
  between operations  16.5 us (8%)
  matrix products  5.14 us (2%)
    ppermute x13, starting transfers between devices, swap(): return lax.ppermute(a, axis, [(0, 1), (1, 0)])  17.8 us
    ppermute x13, waiting for transfers between devices, swap(): return lax.ppermute(a, axis, [(0, 1), (1, 0)])  15.8 us
    unnamed x95, local copies, waits for them, and re-layouts  14.6 us
    ppermute x7, starting transfers between devices, parts_z(): got.append(lax.ppermute(block, 'z', [(i, (i + d) % 8) for i in range(8)]))  13 us
    all_to_all x2, starting transfers between devices, swap_col(): return lax.all_to_all(blocks, COL, 0, 0, tiled=True)  13 us
    ppermute x7, waiting for transfers between devices, parts_z(): got.append(lax.ppermute(block, 'z', [(i, (i + d) % 8) for i in range(8)]))  11.4 us
    pallas_call x1, Pallas kernels, weight_parts(): pl.pallas_call(weight_kernel, grid_spec=pltpu.PrefetchScalarGridSpec(num_...  10.3 us
    all_gather x2, waiting for transfers between devices, gather_z(): return lax.all_gather(two, 'z').reshape((16,) + two.shape[1:])  9.9 us
  transfers between devices with their start and end apart: 31, of which 17 were waited for; matrix products, arithmetic and copies ran while one was open for 16% of the time, Pallas kernels for 8%

commit v1 on v0

--- a/solution.py
+++ b/solution.py
@@ -91,13 +91,11 @@
     outs[0][:, pl.ds(pl.multiple_of(at * m, 128), m)] = block
 
 
-def put_teacher_heads(outs, at, block):
-    teacher, heads = outs
-    teacher[at] = block[:128]
-    both = block[128:224].astype(f32) + block[224:].astype(f32)
-    heads[at, :, :256] = both[:64]
-    heads[at, :32, 256:] = both[64:, :128]
-    heads[at, 32:, 256:] = both[64:, 128:]
+def put_heads(outs, at, block):
+    both = block[:96].astype(f32) + block[96:].astype(f32)
+    outs[0][at, :, :256] = both[:64]
+    outs[0][at, :32, 256:] = both[64:, :128]
+    outs[0][at, 32:, 256:] = both[64:, 128:]
 
 
 def pack_teacher_heads(teacher, heads_t):
@@ -173,15 +171,15 @@
         preferred_element_type=f32,
     )
     for j in range(2):
-        split_cores(place_ref[1], total_ref, j, 160, keep_ref, send_ref, (0, j))
+        split_cores(place_ref[0], total_ref, j, 160, keep_ref, send_ref, (0, j))
 
 
 def split_shapes(n):
     return [jax.ShapeDtypeStruct((2, 8, n + PAD, 384), kind) for kind in (f32, bf16)]
 
 
-def weight_parts(yl, c, tokens, cotangent):
-    block = pl.BlockSpec((1, 2, 160 + PAD, 384), lambda i, where: (where[0] ^ (i // 4), i % 4, 0, 0))
+def weight_parts(c, tokens, cotangent):
+    block = pl.BlockSpec((1, 2, 160 + PAD, 384), lambda i, where: (i // 4, i % 4, 0, 0))
     return pl.pallas_call(
         weight_kernel,
         grid_spec=pltpu.PrefetchScalarGridSpec(
@@ -199,7 +197,7 @@
         cost_estimate=pl.CostEstimate(
             flops=2 * 512 * 5120 * 384, bytes_accessed=12 * MIB, transcendentals=0
         ),
-    )(jnp.stack([yl, c]).astype(jnp.int32), tokens, cotangent)
+    )(c[None].astype(jnp.int32), tokens, cotangent)
 
 
 def product(a, b, contract):
@@ -269,26 +267,29 @@
 
     packed = pair_y(pack_teacher_heads(teacher, expand_heads.T), yl)
     tokens_late = after(tokens, packed)
-    sent, own = sum_mates(*weight_parts(yl, c, tokens_late, cotangent))
-    packed = after(gather_z(packed), sent)
-    model_two = after(pair_col(expand_model), sent)
-
-    shapes = [jax.ShapeDtypeStruct((32, 128, 256), bf16), jax.ShapeDtypeStruct((32, 64, 384), f32)]
-    teacher_block, heads = weave(packed, c, shapes, put_teacher_heads)
-    teacher_block, heads = teacher_block.reshape(4096, 256), heads.reshape(2048, 384)
+    keep, send = weight_parts(c, tokens_late, cotangent)
+    blocks = payload(keep + swap(send, "c").astype(f32)).reshape(16, 160 + PAD, 384)
+    packed = after(gather_z(packed), blocks)
+    model_two = after(pair_col(expand_model), blocks)
+    blocks = lax.all_to_all(blocks, ("yl", "z"), 0, 0, tiled=True)
+
+    shape = jax.ShapeDtypeStruct((32, 128, 256), bf16)
+    teacher_block = weave(packed[:, :128], c, shape, put_rows).reshape(4096, 256)
+    shape = jax.ShapeDtypeStruct((32, 64, 384), f32)
+    heads = weave(packed[:, 128:], c, shape, put_heads).reshape(2048, 384)
     model_rows = gather_col(model_two, yh, x)
     expanded_two = pair_col(jnp.dot(model_rows, teacher_block.astype(f32), precision=HIGH))
     expanded = gather_col(expanded_two, yh, x)
-    blocks = lax.all_to_all(blocks_z(sent, own), "z", 0, 0, tiled=True)
 
     student = jnp.dot(expanded, heads, precision=HIGH).astype(bf16)
     student_two = pair_y(student, yl)
     student_own = gather_z(student_two)
 
     grad = jnp.sum(dec(after(blocks, student)), axis=0)
-    sent, own = sum_mates(*share_parts(yl, c, expanded, grad))
-    side = swap_col(payload(blocks_of(grad, heads)))
-    side = jnp.sum(dec(after(side, sent, student_two)), axis=0)
+    blocks = after(payload(blocks_of(grad, heads)), student_two)
+    side = swap_col(blocks)
+    sent, own = sum_mates(*share_parts(yl, c, after(expanded, blocks), grad))
+    side = jnp.sum(dec(after(side, sent)), axis=0)
     blocks = payload(blocks_of(side, teacher_block))
     grad_model = jnp.sum(dec(swap_col(blocks)), axis=0)
     shares = parts_z(after(blocks_z(sent, own), blocks), z)

time: 206 us -> 213 us (1.034)
  starting transfers between devices: 60.7 us -> 82.6 us
  other arithmetic: 30.7 us -> 23 us
  local copies, waits for them, and re-layouts: 16.9 us -> 13.3 us
  waiting for transfers between devices: 54.3 us -> 51.3 us
    ppermute x6, starting transfers between devices: 8.7 us -> 18.3 us  [gather_col(): lax.ppermute(two, 'x', [(i, (i + d) % 4) for i in range(4)])]
    ppermute x13, starting transfers between devices: 17.8 us -> 25.2 us  [swap(): return lax.ppermute(a, axis, [(0, 1), (1, 0)])]
    unnamed x95 -> x80, local copies, waits for them, and re-layouts: 14.6 us -> 7.45 us
    add x2 -> x1, other arithmetic: 4.25 us -> 0.17 us  [sum_mates(): x = keep + swap(send, 'c').astype(f32)]
    ppermute x7, starting transfers between devices: 13 us -> 16.8 us  [parts_z(): got.append(lax.ppermute(block, 'z', [(i, (i + d) % 8) for i in range(8)]))]
    all_to_all x2, waiting for transfers between devices: 8.01 us -> 11 us  [swap_col(): return lax.all_to_all(blocks, COL, 0, 0, tiled=True)]
    add x0 -> x1, other arithmetic: none -> 2.63 us  [shards(): keep + swap(send, 'c').astype(f32)]
    all_gather x2, waiting for transfers between devices: 9.9 us -> 7.4 us  [gather_z(): return lax.all_gather(two, 'z').reshape((16,) + two.shape[1:])]
  transfers between devices with their start and end apart: 31 -> 31, of which waited for: 17 -> 13; matrix products, arithmetic and copies ran while one was open for 16% -> 13% of each run, Pallas kernels for 8% -> 7%
where the time goes in v1:
time: 213 us; the launch traced here: 212 us
  starting transfers between devices  82.6 us (39%)
  waiting for transfers between devices  51.3 us (24%)
  other arithmetic  23 us (11%)
  Pallas kernels  20.6 us (10%)
  between operations  16.5 us (8%)
  local copies, waits for them, and re-layouts  13.3 us (6%)
  matrix products  5.01 us (2%)
    ppermute x13, starting transfers between devices, swap(): return lax.ppermute(a, axis, [(0, 1), (1, 0)])  25.2 us
    ppermute x6, starting transfers between devices, gather_col(): lax.ppermute(two, 'x', [(i, (i + d) % 4) for i in range(4)])  18.3 us
    ppermute x7, starting transfers between devices, parts_z(): got.append(lax.ppermute(block, 'z', [(i, (i + d) % 8) for i in range(8)]))  16.8 us
    ppermute x13, waiting for transfers between devices, swap(): return lax.ppermute(a, axis, [(0, 1), (1, 0)])  14.2 us
    all_to_all x2, starting transfers between devices, swap_col(): return lax.all_to_all(blocks, COL, 0, 0, tiled=True)  12.9 us
    ppermute x7, waiting for transfers between devices, parts_z(): got.append(lax.ppermute(block, 'z', [(i, (i + d) % 8) for i in range(8)]))  11.5 us
    all_to_all x2, waiting for transfers between devices, swap_col(): return lax.all_to_all(blocks, COL, 0, 0, tiled=True)  11 us
    pallas_call x1, Pallas kernels, weight_parts(): pl.pallas_call(weight_kernel, grid_spec=pltpu.PrefetchScalarGridSpec(num_...  9.48 us
  transfers between devices with their start and end apart: 31, of which 13 were waited for; matrix products, arithmetic and copies ran while one was open for 13% of the time, Pallas kernels for 7%

profile of v1, /device:TPU:1, one launch (start us, length us, event | category | flops | bytes accessed | tf_op | source)
XLA Modules:
  0.0 212.3 jit_solution(7104991467886341939)
XLA Ops:
  9.0 2.2 %collective-permute-start.1 = (bf16[320,256]{1,0:T(8,128)(2,1)S(1)}, bf16[320,256]{1,0:T(8,128)(2,1)S(1)}, u32[]{:S(2)}, u32[]{:S(2)}) collective-permute-start(bf16[320,256]{1,0:T(8,128)(2,1)S(1)} %maximum_dynamic-update-slice_fusion), channel_id=1, source_target_pairs={{0,128},{128,0},{1,129},{129,1},{2,130},{130,2},{3,131},{131,3},{4... | collective-permute-start | bytes 491528 | tf_op jit(solution)/shard_map/ppermute | solution.py:18
  11.2 2.7 %collective-permute-done.1 = bf16[320,256]{1,0:T(8,128)(2,1)S(1)} collective-permute-done((bf16[320,256]{1,0:T(8,128)(2,1)S(1)}, bf16[320,256]{1,0:T(8,128)(2,1)S(1)}, u32[]{:S(2)}, u32[]{:S(2)}) %collective-permute-start.1) | collective-permute-done | bytes 163872 | tf_op jit(solution)/shard_map/ppermute | solution.py:18
  14.8 9.5 %shard_map.76 = (f32[2,8,176,384]{3,2,1,0:T(8,128)}, bf16[2,8,176,384]{3,2,1,0:T(8,128)(2,1)}) custom-call(s32[1]{0:T(128)} %bitcast.place_ref, bf16[512,5120]{1,0:T(8,128)(2,1)} %tokens_ref, bf16[512,384]{1,0:T(8,128)(2,1)} %cotangent_ref.1), custom_call_target="tpu_custom_call" | custom-call | flops 2013265920 | bytes 12582912 | tf_op jit(solution)/shard_map/pallas_call | solution.py:183
  24.3 3.7 %collective-permute-start.2 = (bf16[2,8,176,384]{3,2,1,0:T(8,128)(2,1)}, bf16[2,8,176,384]{3,2,1,0:T(8,128)(2,1)S(1)}, u32[]{:S(2)}, u32[]{:S(2)}) collective-permute-start(bf16[2,8,176,384]{3,2,1,0:T(8,128)(2,1)} %get-tuple-element.18), channel_id=1, source_target_pairs={{0,8},{8,0},{1,9},{9,1},{2,10},{10,2},{3,11},{11,3},{4,12},{12,4},... | collective-permute-start | bytes 6488072 | tf_op jit(solution)/shard_map/ppermute | solution.py:18
  29.5 1.9 collective-permute-start
  31.8 5.5 %collective-permute-done = f16[176,512]{1,0:T(8,128)(2,1)S(1)} collective-permute-done((f16[176,512]{1,0:T(8,128)(2,1)S(1)}, f16[176,512]{1,0:T(8,128)(2,1)S(1)}, u32[]{:S(2)}, u32[]{:S(2)}) %collective-permute-start) | collective-permute-done | bytes 180256 | tf_op jit(solution)/shard_map/ppermute | solution.py:18
  37.3 2.6 %convert_add_fusion = f32[2,8,176,384]{3,2,1,0:T(8,128)S(1)} fusion(f32[2,8,176,384]{3,2,1,0:T(8,128)} %get-tuple-element.17, bf16[2,8,176,384]{3,2,1,0:T(8,128)(2,1)S(1)} %collective-permute-done.2), kind=kLoop, calls=%fused_computation.1 | loop fusion | flops 2162688 | bytes 10813440 | tf_op jit(solution)/shard_map/add | solution.py:271
  40.1 2.2 %select_convert_fusion = f16[2,8,176,384]{3,2,1,0:T(8,128)(2,1)} fusion(f32[2,8,176,384]{3,2,1,0:T(8,128)S(1)} %convert_add_fusion, f32[2,8,384]{2,1,0:T(8,128)S(1)} %bitcast.176, f32[2,8,384]{2,1,0:T(8,128)S(1)} %bitcast.177, pred[176]{0:T(512)(128)(4,1)S(1)} %iota_compare_fusion), kind=kLoop, calls=%fused_computation | loop fusion | flops 3244032 | bytes 6537392 | tf_op jit(solution)/shard_map/convert_element_type | solution.py:36
  42.3 1.6 collective-permute-start.5
  45.4 9.3 %all-to-all-start = ((f16[16,176,384]{2,1,0:T(8,128)(2,1)}), f16[16,176,384]{2,1,0:T(8,128)(2,1)}, u32[]{:S(2)}, u32[]{:S(2)}) async-start(f16[16,176,384]{2,1,0:T(8,128)(2,1)} %bitcast.45), calls=%async_computation | async-start | bytes 4325376 | tf_op jit(solution)/shard_map/all_to_all | solution.py:274
  54.9 7.4 %all-gather.5.cloned.1.call-done = bf16[16,320,256]{2,1,0:T(8,128)(2,1)} async-done(((bf16[2,320,256]{2,1,0:T(8,128)(2,1)}), bf16[16,320,256]{2,1,0:T(8,128)(2,1)}) %all-gather.5.cloned.1.call-update) | async-done | bytes 2621456 | tf_op jit(solution)/shard_map/all_gather | solution.py:65
  62.3 1.3 slice.179.refs_0_
  63.6 10.4 %collective-permute-start.6 = (bf16[16,128,256]{2,1,0:T(8,128)(2,1)S(1)}, bf16[16,128,256]{2,1,0:T(8,128)(2,1)S(1)}, u32[]{:S(2)}, u32[]{:S(2)}) collective-permute-start(bf16[16,128,256]{2,1,0:T(8,128)(2,1)S(1)} %slice.179.refs_0_), channel_id=1, source_target_pairs={{0,8},{8,0},{1,9},{9,1},{2,10},{10,2},{3,11},{11,3},{4,12},{12,4},... | collective-permute-start | bytes 3145736 | tf_op jit(solution)/shard_map/ppermute | solution.py:18
  77.0 1.5 abs_reduce_fusion.1
  79.3 2.5 %collective-permute-start.7 = (f16[176,256]{1,0:T(8,128)(2,1)S(1)}, f16[176,256]{1,0:T(8,128)(2,1)S(1)}, u32[]{:S(2)}, u32[]{:S(2)}) collective-permute-start(f16[176,256]{1,0:T(8,128)(2,1)S(1)} %select_convert_fusion.6), channel_id=1, source_target_pairs={{0,4},{4,0},{1,5},{5,1},{2,6},{6,2},{3,7},{7,3},{8,12},{12,8},{9,1... | collective-permute-start | bytes 270344 | tf_op jit(solution)/shard_map/ppermute | solution.py:18
  81.9 4.6 %collective-permute-done.7 = f16[176,256]{1,0:T(8,128)(2,1)S(1)} collective-permute-done((f16[176,256]{1,0:T(8,128)(2,1)S(1)}, f16[176,256]{1,0:T(8,128)(2,1)S(1)}, u32[]{:S(2)}, u32[]{:S(2)}) %collective-permute-start.7) | collective-permute-done | bytes 90144 | tf_op jit(solution)/shard_map/ppermute | solution.py:18
  86.5 13.8 %collective-permute-start.10 = (f16[2,176,256]{2,1,0:T(8,128)(2,1)S(1)}, f16[2,176,256]{2,1,0:T(8,128)(2,1)S(1)}, u32[]{:S(2)}, u32[]{:S(2)}) collective-permute-start(f16[2,176,256]{2,1,0:T(8,128)(2,1)S(1)} %pad_maximum_fusion.3), channel_id=1, source_target_pairs={{0,2},{1,3},{2,0},{3,1},{4,6},{5,7},{6,4},{7,5},{8,10},{9,11},{10,... | collective-permute-start | bytes 540680 | tf_op jit(solution)/shard_map/ppermute | solution.py:121
  100.3 1.5 collective-permute-start.8
  101.8 2.5 %collective-permute-done.10 = f16[2,176,256]{2,1,0:T(8,128)(2,1)S(1)} collective-permute-done((f16[2,176,256]{2,1,0:T(8,128)(2,1)S(1)}, f16[2,176,256]{2,1,0:T(8,128)(2,1)S(1)}, u32[]{:S(2)}, u32[]{:S(2)}) %collective-permute-start.10) | collective-permute-done | bytes 180256 | tf_op jit(solution)/shard_map/ppermute | solution.py:121
  105.2 3.1 %collective-permute-done.8 = f16[2,176,256]{2,1,0:T(8,128)(2,1)S(1)} collective-permute-done((f16[2,176,256]{2,1,0:T(8,128)(2,1)S(1)}, f16[2,176,256]{2,1,0:T(8,128)(2,1)S(1)}, u32[]{:S(2)}, u32[]{:S(2)}) %collective-permute-start.8) | collective-permute-done | bytes 180256 | tf_op jit(solution)/shard_map/ppermute | solution.py:121
  109.2 1.2 copy-done.6
  110.4 1.4 copy-done.7
  112.7 1.3 convolution_convert_fusion
  114.6 2.3 %copy.18 = f16[16,176,384]{2,0,1:T(8,128)(2,1)S(1)} copy(f16[16,176,384]{2,1,0:T(8,128)(2,1)} %all-to-all-done) | data formatting | bytes 4325376 | tf_op jit(solution)/shard_map/optimization_barrier | solution.py:22
  116.9 2.0 multiply_reduce_fusion.a_ref.grad_ref
  118.9 1.7 shard_map.81
  123.5 3.6 %shard_map.82 = (f32[2,8,80,384]{3,2,1,0:T(8,128)S(1)}, bf16[2,8,80,384]{3,2,1,0:T(8,128)(2,1)}) custom-call(s32[2]{0:T(128)S(1)} %pad_add_fusion.place_ref, f32[160,2048]{1,0:T(8,128)S(1)} %copy-done.5, f32[160,384]{1,0:T(8,128)S(1)} %multiply_reduce_fusion.a_ref.grad_ref), custom_call_target="tpu_custom_call" | custom-call | flops 754974720 | bytes 6291456 | tf_op jit(solution)/shard_map/pallas_call | solution.py:222
  127.0 1.6 collective-permute-start.13
  128.7 5.9 %all-to-all-start.1 = ((f16[8,176,256]{2,1,0:T(8,128)(2,1)}), f16[8,176,256]{2,1,0:T(8,128)(2,1)}, u32[]{:S(2)}, u32[]{:S(2)}) async-start(f16[8,176,256]{2,1,0:T(8,128)(2,1)} %select_convert_fusion.2), calls=%async_computation.1 | async-start | bytes 1441792 | tf_op jit(solution)/shard_map/all_to_all | solution.py:129
  137.6 11.0 %all-to-all-done.1 = f16[8,176,256]{2,1,0:T(8,128)(2,1)} async-done(((f16[8,176,256]{2,1,0:T(8,128)(2,1)}), f16[8,176,256]{2,1,0:T(8,128)(2,1)}, u32[]{:S(2)}, u32[]{:S(2)}) %all-to-all-start.1) | async-done | bytes 720928 | tf_op jit(solution)/shard_map/all_to_all | solution.py:129
  149.4 1.2 multiply_reduce_fusion.2.a_ref
  150.6 1.5 shard_map.83
  152.3 1.7 select_convert_fusion.1
  154.0 1.4 collective-permute-done.18
  156.1 8.6 %collective-permute-start.25 = (f16[80,384]{1,0:T(8,128)(2,1)S(1)}, f16[80,384]{1,0:T(8,128)(2,1)S(1)}, u32[]{:S(2)}, u32[]{:S(2)}) collective-permute-start(f16[80,384]{1,0:T(8,128)(2,1)S(1)} %get-tuple-element.56), channel_id=1, source_target_pairs={{0,112},{16,0},{32,16},{48,32},{64,48},{80,64},{96,80},{112,96},{1... | collective-permute-start | bytes 184328 | tf_op jit(solution)/shard_map/ppermute | solution.py:149
  164.7 6.9 %all-to-all-start.2 = ((f16[8,176,512]{2,1,0:T(8,128)(2,1)}), f16[8,176,512]{2,1,0:T(8,128)(2,1)}, u32[]{:S(2)}, u32[]{:S(2)}) async-start(f16[8,176,512]{2,1,0:T(8,128)(2,1)} %select_convert_fusion.1), calls=%async_computation.2 | async-start | bytes 2883584 | tf_op jit(solution)/shard_map/all_to_all | solution.py:129
  171.7 5.3 %collective-permute-start.22 = (f16[80,384]{1,0:T(8,128)(2,1)S(1)}, f16[80,384]{1,0:T(8,128)(2,1)S(1)}, u32[]{:S(2)}, u32[]{:S(2)}) collective-permute-start(f16[80,384]{1,0:T(8,128)(2,1)S(1)} %get-tuple-element.59), channel_id=1, source_target_pairs={{0,64},{16,80},{32,96},{48,112},{64,0},{80,16},{96,32},{112,48},{1... | collective-permute-start | bytes 184328 | tf_op jit(solution)/shard_map/ppermute | solution.py:149
  177.1 1.5 collective-permute-start.20
  178.7 1.3 collective-permute-start.19
  180.0 2.1 collective-permute-done.22
  182.1 4.3 %collective-permute-done.21 = f16[80,384]{1,0:T(8,128)(2,1)S(1)} collective-permute-done((f16[80,384]{1,0:T(8,128)(2,1)S(1)}, f16[80,384]{1,0:T(8,128)(2,1)S(1)}, u32[]{:S(2)}, u32[]{:S(2)}) %collective-permute-start.21) | collective-permute-done | bytes 61472 | tf_op jit(solution)/shard_map/ppermute | solution.py:149
  186.4 3.1 %collective-permute-done.20 = f16[80,384]{1,0:T(8,128)(2,1)S(1)} collective-permute-done((f16[80,384]{1,0:T(8,128)(2,1)S(1)}, f16[80,384]{1,0:T(8,128)(2,1)S(1)}, u32[]{:S(2)}, u32[]{:S(2)}) %collective-permute-start.20) | collective-permute-done | bytes 61472 | tf_op jit(solution)/shard_map/ppermute | solution.py:149
  189.5 2.1 collective-permute-done.19
  192.3 1.7 fusion.84
  195.6 1.5 fusion.10
  198.1 2.5 %multiply_reduce_fusion.1 = f32[160,512]{1,0:T(8,128)} fusion(f16[8,176,512]{2,1,0:T(8,128)(2,1)} %all-to-all-done.2, f32[8,512]{1,0:T(8,128)S(1)} %bitcast.180), kind=kLoop, calls=%fused_computation.4 | loop fusion | flops 1884160 | bytes 1654784 | tf_op jit(solution)/shard_map/reduce_sum | solution.py:294
  200.6 1.5 shard_map.84
  202.1 2.2 %convolution_bitcast_fusion = f32[512,384]{0,1:T(8,128)S(1)} fusion(bf16[5120,384]{1,0:T(8,128)(2,1)S(1)} %bitcast.171, bf16[512,5120]{1,0:T(8,128)(2,1)S(1)} %bitcast.199), kind=kOutput, calls=%fused_computation.8 | convolution fusion | flops 2013265920 | bytes 9961472 | tf_op jit(solution)/shard_map/dot_general | solution.py:300
  (180 shorter events, 23.4 us)
Async XLA Ops:
  7.2 55.1 %all-gather.5.cloned.1.call-start = ((), (), s32[]{:S(2)}) async-start(), calls=%async_computation.3 | async-start | bytes 2949120 | tf_op jit(solution)/shard_map/all_gather | solution.py:65
  9.0 4.9 %collective-permute-start.1 = (bf16[320,256]{1,0:T(8,128)(2,1)S(1)}, bf16[320,256]{1,0:T(8,128)(2,1)S(1)}, u32[]{:S(2)}, u32[]{:S(2)}) collective-permute-start(bf16[320,256]{1,0:T(8,128)(2,1)S(1)} %maximum_dynamic-update-slice_fusion), channel_id=1, source_target_pairs={{0,128},{128,0},{1,129},{129,1},{2,130},{130,2},{3,131},{131,3},{4... | collective-permute-start | bytes 491528 | tf_op jit(solution)/shard_map/ppermute | solution.py:18
  14.8 13.2 %copy-start.10 = (f32[160,512]{1,0:T(8,128)S(1)}, f32[160,512]{1,0:T(8,128)}, u32[]{:S(2)}) copy-start(f32[160,512]{1,0:T(8,128)} %param.8) | copy-start | bytes 983044
  24.3 13.1 %collective-permute-start.2 = (bf16[2,8,176,384]{3,2,1,0:T(8,128)(2,1)}, bf16[2,8,176,384]{3,2,1,0:T(8,128)(2,1)S(1)}, u32[]{:S(2)}, u32[]{:S(2)}) collective-permute-start(bf16[2,8,176,384]{3,2,1,0:T(8,128)(2,1)} %get-tuple-element.18), channel_id=1, source_target_pairs={{0,8},{8,0},{1,9},{9,1},{2,10},{10,2},{3,11},{11,3},{4,12},{12,4},... | collective-permute-start | bytes 6488072 | tf_op jit(solution)/shard_map/ppermute | solution.py:18
  29.5 7.8 %collective-permute-start = (f16[176,512]{1,0:T(8,128)(2,1)S(1)}, f16[176,512]{1,0:T(8,128)(2,1)S(1)}, u32[]{:S(2)}, u32[]{:S(2)}) collective-permute-start(f16[176,512]{1,0:T(8,128)(2,1)S(1)} %select_convert_fusion.5), channel_id=1, source_target_pairs={{0,4},{4,0},{1,5},{5,1},{2,6},{6,2},{3,7},{7,3},{8,12},{12,8},{9,1... | collective-permute-start | bytes 540680 | tf_op jit(solution)/shard_map/ppermute | solution.py:18
  42.3 12.6 %collective-permute-start.5 = (f16[2,176,512]{2,1,0:T(8,128)(2,1)S(1)}, f16[2,176,512]{2,1,0:T(8,128)(2,1)S(1)}, u32[]{:S(2)}, u32[]{:S(2)}) collective-permute-start(f16[2,176,512]{2,1,0:T(8,128)(2,1)S(1)} %pad_maximum_fusion), channel_id=1, source_target_pairs={{0,2},{1,3},{2,0},{3,1},{4,6},{5,7},{6,4},{7,5},{8,10},{9,11},{10,... | collective-permute-start | bytes 1081352 | tf_op jit(solution)/shard_map/ppermute | solution.py:121
  43.9 30.1 %collective-permute-start.4 = (f16[2,176,512]{2,1,0:T(8,128)(2,1)S(1)}, f16[2,176,512]{2,1,0:T(8,128)(2,1)S(1)}, u32[]{:S(2)}, u32[]{:S(2)}) collective-permute-start(f16[2,176,512]{2,1,0:T(8,128)(2,1)S(1)} %pad_maximum_fusion), channel_id=1, source_target_pairs={{0,3},{1,0},{2,1},{3,2},{4,7},{5,4},{6,5},{7,6},{8,11},{9,8},{10,9... | collective-permute-start | bytes 1081352 | tf_op jit(solution)/shard_map/ppermute | solution.py:121
  44.8 29.3 %collective-permute-start.3 = (f16[2,176,512]{2,1,0:T(8,128)(2,1)S(1)}, f16[2,176,512]{2,1,0:T(8,128)(2,1)S(1)}, u32[]{:S(2)}, u32[]{:S(2)}) collective-permute-start(f16[2,176,512]{2,1,0:T(8,128)(2,1)S(1)} %pad_maximum_fusion), channel_id=1, source_target_pairs={{0,1},{1,2},{2,3},{3,0},{4,5},{5,6},{6,7},{7,4},{8,9},{9,10},{10,1... | collective-permute-start | bytes 1081352 | tf_op jit(solution)/shard_map/ppermute | solution.py:121
  45.4 69.2 %all-to-all-start = ((f16[16,176,384]{2,1,0:T(8,128)(2,1)}), f16[16,176,384]{2,1,0:T(8,128)(2,1)}, u32[]{:S(2)}, u32[]{:S(2)}) async-start(f16[16,176,384]{2,1,0:T(8,128)(2,1)} %bitcast.45), calls=%async_computation | async-start | bytes 4325376 | tf_op jit(solution)/shard_map/all_to_all | solution.py:274
  63.6 12.7 %collective-permute-start.6 = (bf16[16,128,256]{2,1,0:T(8,128)(2,1)S(1)}, bf16[16,128,256]{2,1,0:T(8,128)(2,1)S(1)}, u32[]{:S(2)}, u32[]{:S(2)}) collective-permute-start(bf16[16,128,256]{2,1,0:T(8,128)(2,1)S(1)} %slice.179.refs_0_), channel_id=1, source_target_pairs={{0,8},{8,0},{1,9},{9,1},{2,10},{10,2},{3,11},{11,3},{4,12},{12,4},... | collective-permute-start | bytes 3145736 | tf_op jit(solution)/shard_map/ppermute | solution.py:18
  76.2 32.9 %collective-permute-start.11 = (bf16[16,192,256]{2,1,0:T(8,128)(2,1)S(1)}, bf16[16,192,256]{2,1,0:T(8,128)(2,1)S(1)}, u32[]{:S(2)}, u32[]{:S(2)}) collective-permute-start(bf16[16,192,256]{2,1,0:T(8,128)(2,1)S(1)} %slice.188.refs_0_), channel_id=1, source_target_pairs={{0,8},{8,0},{1,9},{9,1},{2,10},{10,2},{3,11},{11,3},{4,12},{12,4},... | collective-permute-start | bytes 4718600 | tf_op jit(solution)/shard_map/ppermute | solution.py:18
  79.3 7.2 %collective-permute-start.7 = (f16[176,256]{1,0:T(8,128)(2,1)S(1)}, f16[176,256]{1,0:T(8,128)(2,1)S(1)}, u32[]{:S(2)}, u32[]{:S(2)}) collective-permute-start(f16[176,256]{1,0:T(8,128)(2,1)S(1)} %select_convert_fusion.6), channel_id=1, source_target_pairs={{0,4},{4,0},{1,5},{5,1},{2,6},{6,2},{3,7},{7,3},{8,12},{12,8},{9,1... | collective-permute-start | bytes 270344 | tf_op jit(solution)/shard_map/ppermute | solution.py:18
  86.5 17.8 %collective-permute-start.10 = (f16[2,176,256]{2,1,0:T(8,128)(2,1)S(1)}, f16[2,176,256]{2,1,0:T(8,128)(2,1)S(1)}, u32[]{:S(2)}, u32[]{:S(2)}) collective-permute-start(f16[2,176,256]{2,1,0:T(8,128)(2,1)S(1)} %pad_maximum_fusion.3), channel_id=1, source_target_pairs={{0,2},{1,3},{2,0},{3,1},{4,6},{5,7},{6,4},{7,5},{8,10},{9,11},{10,... | collective-permute-start | bytes 540680 | tf_op jit(solution)/shard_map/ppermute | solution.py:121
  100.3 4.9 %collective-permute-start.9 = (f16[2,176,256]{2,1,0:T(8,128)(2,1)S(1)}, f16[2,176,256]{2,1,0:T(8,128)(2,1)S(1)}, u32[]{:S(2)}, u32[]{:S(2)}) collective-permute-start(f16[2,176,256]{2,1,0:T(8,128)(2,1)S(1)} %pad_maximum_fusion.3), channel_id=1, source_target_pairs={{0,3},{1,0},{2,1},{3,2},{4,7},{5,4},{6,5},{7,6},{8,11},{9,8},{10,9... | collective-permute-start | bytes 540680 | tf_op jit(solution)/shard_map/ppermute | solution.py:121
  100.3 8.1 %collective-permute-start.8 = (f16[2,176,256]{2,1,0:T(8,128)(2,1)S(1)}, f16[2,176,256]{2,1,0:T(8,128)(2,1)S(1)}, u32[]{:S(2)}, u32[]{:S(2)}) collective-permute-start(f16[2,176,256]{2,1,0:T(8,128)(2,1)S(1)} %pad_maximum_fusion.3), channel_id=1, source_target_pairs={{0,1},{1,2},{2,3},{3,0},{4,5},{5,6},{6,7},{7,4},{8,9},{9,10},{10,1... | collective-permute-start | bytes 540680 | tf_op jit(solution)/shard_map/ppermute | solution.py:121
  101.8 8.6 %copy-start.3 = (bf16[16,192,256]{2,1,0:T(8,128)(2,1)S(1)}, bf16[16,192,256]{2,1,0:T(8,128)(2,1)}, u32[]{:S(2)}) copy-start(bf16[16,192,256]{2,1,0:T(8,128)(2,1)} %copy-done.2) | copy-start | bytes 4718596
  109.1 3.5 %copy-start.4 = (f32[160,2048]{1,0:T(8,128)}, f32[160,2048]{1,0:T(8,128)S(1)}, u32[]{:S(2)}) copy-start(f32[160,2048]{1,0:T(8,128)S(1)} %shard_map.79.expanded_ref) | copy-start | bytes 3932164
  114.0 7.8 %collective-permute-start.12 = (bf16[160,384]{1,0:T(8,128)(2,1)S(1)}, bf16[160,384]{1,0:T(8,128)(2,1)}, u32[]{:S(2)}, u32[]{:S(2)}) collective-permute-start(bf16[160,384]{1,0:T(8,128)(2,1)S(1)} %convolution_convert_fusion), channel_id=1, source_target_pairs={{0,128},{128,0},{1,129},{129,1},{2,130},{130,2},{3,131},{131,3},{4... | collective-permute-start | bytes 368648 | tf_op jit(solution)/shard_map/ppermute | solution.py:18
  127.0 8.3 %collective-permute-start.13 = (bf16[2,8,80,384]{3,2,1,0:T(8,128)(2,1)}, bf16[2,8,80,384]{3,2,1,0:T(8,128)(2,1)S(1)}, u32[]{:S(2)}, u32[]{:S(2)}) collective-permute-start(bf16[2,8,80,384]{3,2,1,0:T(8,128)(2,1)} %get-tuple-element.25), channel_id=1, source_target_pairs={{0,8},{8,0},{1,9},{9,1},{2,10},{10,2},{3,11},{11,3},{4,12},{12,4},... | collective-permute-start | bytes 2949128 | tf_op jit(solution)/shard_map/ppermute | solution.py:18
  128.7 19.9 %all-to-all-start.1 = ((f16[8,176,256]{2,1,0:T(8,128)(2,1)}), f16[8,176,256]{2,1,0:T(8,128)(2,1)}, u32[]{:S(2)}, u32[]{:S(2)}) async-start(f16[8,176,256]{2,1,0:T(8,128)(2,1)} %select_convert_fusion.2), calls=%async_computation.1 | async-start | bytes 1441792 | tf_op jit(solution)/shard_map/all_to_all | solution.py:129
  134.6 57.6 %all-gather.7.cloned.1.call-start = ((), (), s32[]{:S(2)}) async-start(), calls=%async_computation.4 | async-start | bytes 2211840 | tf_op jit(solution)/shard_map/all_gather | solution.py:65
  135.5 15.1 %copy-start.1 = (bf16[32,128,256]{2,1,0:T(8,128)(2,1)S(1)}, bf16[32,128,256]{2,1,0:T(8,128)(2,1)}, u32[]{:S(2)}) copy-start(bf16[32,128,256]{2,1,0:T(8,128)(2,1)} %copy-done) | copy-start | bytes 6291460
  137.0 18.3 %collective-permute-start.18 = (f16[8,80,384]{2,1,0:T(8,128)(2,1)S(1)}, f16[8,80,384]{2,1,0:T(8,128)(2,1)S(1)}, u32[]{:S(2)}, u32[]{:S(2)}) collective-permute-start(f16[8,80,384]{2,1,0:T(8,128)(2,1)S(1)} %select_convert_fusion.4), channel_id=1, source_target_pairs={{0,128},{128,0},{1,129},{129,1},{2,130},{130,2},{3,131},{131,3},{4... | collective-permute-start | bytes 1474568 | tf_op jit(solution)/shard_map/ppermute | solution.py:18
  152.3 3.2 %copy-start.9 = (f32[2,8,80,384]{3,2,1,0:T(8,128)S(1)}, f32[2,8,80,384]{3,2,1,0:T(8,128)}, u32[]{:S(2)}) copy-start(f32[2,8,80,384]{3,2,1,0:T(8,128)} %copy-done.8) | copy-start | bytes 5898244
  156.0 35.7 %copy-start.12 = (f16[8,80,384]{2,1,0:T(8,128)(2,1)}, f16[8,80,384]{2,1,0:T(8,128)(2,1)S(1)}, u32[]{:S(2)}) copy-start(f16[8,80,384]{2,1,0:T(8,128)(2,1)S(1)} %select_convert_fusion.3) | copy-start | bytes 1474564
  156.1 21.0 %collective-permute-start.25 = (f16[80,384]{1,0:T(8,128)(2,1)S(1)}, f16[80,384]{1,0:T(8,128)(2,1)S(1)}, u32[]{:S(2)}, u32[]{:S(2)}) collective-permute-start(f16[80,384]{1,0:T(8,128)(2,1)S(1)} %get-tuple-element.56), channel_id=1, source_target_pairs={{0,112},{16,0},{32,16},{48,32},{64,48},{80,64},{96,80},{112,96},{1... | collective-permute-start | bytes 184328 | tf_op jit(solution)/shard_map/ppermute | solution.py:149
  164.7 32.4 %all-to-all-start.2 = ((f16[8,176,512]{2,1,0:T(8,128)(2,1)}), f16[8,176,512]{2,1,0:T(8,128)(2,1)}, u32[]{:S(2)}, u32[]{:S(2)}) async-start(f16[8,176,512]{2,1,0:T(8,128)(2,1)} %select_convert_fusion.1), calls=%async_computation.2 | async-start | bytes 2883584 | tf_op jit(solution)/shard_map/all_to_all | solution.py:129
  171.6 7.0 %collective-permute-start.24 = (f16[80,384]{1,0:T(8,128)(2,1)S(1)}, f16[80,384]{1,0:T(8,128)(2,1)S(1)}, u32[]{:S(2)}, u32[]{:S(2)}) collective-permute-start(f16[80,384]{1,0:T(8,128)(2,1)S(1)} %get-tuple-element.57), channel_id=1, source_target_pairs={{0,96},{16,112},{32,0},{48,16},{64,32},{80,48},{96,64},{112,80},{1... | collective-permute-start | bytes 184328 | tf_op jit(solution)/shard_map/ppermute | solution.py:149
  171.7 8.3 %collective-permute-start.23 = (f16[80,384]{1,0:T(8,128)(2,1)S(1)}, f16[80,384]{1,0:T(8,128)(2,1)S(1)}, u32[]{:S(2)}, u32[]{:S(2)}) collective-permute-start(f16[80,384]{1,0:T(8,128)(2,1)S(1)} %get-tuple-element.58), channel_id=1, source_target_pairs={{0,80},{16,96},{32,112},{48,0},{64,16},{80,32},{96,48},{112,64},{1... | collective-permute-start | bytes 184328 | tf_op jit(solution)/shard_map/ppermute | solution.py:149
  171.7 10.3 %collective-permute-start.22 = (f16[80,384]{1,0:T(8,128)(2,1)S(1)}, f16[80,384]{1,0:T(8,128)(2,1)S(1)}, u32[]{:S(2)}, u32[]{:S(2)}) collective-permute-start(f16[80,384]{1,0:T(8,128)(2,1)S(1)} %get-tuple-element.59), channel_id=1, source_target_pairs={{0,64},{16,80},{32,96},{48,112},{64,0},{80,16},{96,32},{112,48},{1... | collective-permute-start | bytes 184328 | tf_op jit(solution)/shard_map/ppermute | solution.py:149
  177.0 9.4 %collective-permute-start.21 = (f16[80,384]{1,0:T(8,128)(2,1)S(1)}, f16[80,384]{1,0:T(8,128)(2,1)S(1)}, u32[]{:S(2)}, u32[]{:S(2)}) collective-permute-start(f16[80,384]{1,0:T(8,128)(2,1)S(1)} %get-tuple-element.60), channel_id=1, source_target_pairs={{0,48},{16,64},{32,80},{48,96},{64,112},{80,0},{96,16},{112,32},{1... | collective-permute-start | bytes 184328 | tf_op jit(solution)/shard_map/ppermute | solution.py:149
  177.1 12.4 %collective-permute-start.20 = (f16[80,384]{1,0:T(8,128)(2,1)S(1)}, f16[80,384]{1,0:T(8,128)(2,1)S(1)}, u32[]{:S(2)}, u32[]{:S(2)}) collective-permute-start(f16[80,384]{1,0:T(8,128)(2,1)S(1)} %get-tuple-element.61), channel_id=1, source_target_pairs={{0,32},{16,48},{32,64},{48,80},{64,96},{80,112},{96,0},{112,16},{1... | collective-permute-start | bytes 184328 | tf_op jit(solution)/shard_map/ppermute | solution.py:149
  178.6 13.0 %copy-start.13 = (f16[80,384]{1,0:T(8,128)(2,1)}, f16[80,384]{1,0:T(8,128)(2,1)S(1)}, u32[]{:S(2)}) copy-start(f16[80,384]{1,0:T(8,128)(2,1)S(1)} %collective-permute-done.24) | copy-start | bytes 184324
  178.7 13.0 %collective-permute-start.19 = (f16[80,384]{1,0:T(8,128)(2,1)S(1)}, f16[80,384]{1,0:T(8,128)(2,1)S(1)}, u32[]{:S(2)}, u32[]{:S(2)}) collective-permute-start(f16[80,384]{1,0:T(8,128)(2,1)S(1)} %get-tuple-element.55), channel_id=1, source_target_pairs={{0,16},{16,32},{32,48},{48,64},{64,80},{80,96},{96,112},{112,0},{1... | collective-permute-start | bytes 184328 | tf_op jit(solution)/shard_map/ppermute | solution.py:149
  180.0 11.7 %copy-start.15 = (f16[80,384]{1,0:T(8,128)(2,1)}, f16[80,384]{1,0:T(8,128)(2,1)S(1)}, u32[]{:S(2)}) copy-start(f16[80,384]{1,0:T(8,128)(2,1)S(1)} %collective-permute-done.23) | copy-start | bytes 184324
  182.1 9.6 %copy-start.17 = (f16[80,384]{1,0:T(8,128)(2,1)}, f16[80,384]{1,0:T(8,128)(2,1)S(1)}, u32[]{:S(2)}) copy-start(f16[80,384]{1,0:T(8,128)(2,1)S(1)} %collective-permute-done.22) | copy-start | bytes 184324
  186.4 5.3 %copy-start.19 = (f16[80,384]{1,0:T(8,128)(2,1)}, f16[80,384]{1,0:T(8,128)(2,1)S(1)}, u32[]{:S(2)}) copy-start(f16[80,384]{1,0:T(8,128)(2,1)S(1)} %collective-permute-done.21) | copy-start | bytes 184324
  192.2 3.3 %copy-start.14 = (f16[80,384]{1,0:T(8,128)(2,1)S(1)}, f16[80,384]{1,0:T(8,128)(2,1)}, u32[]{:S(2)}) copy-start(f16[80,384]{1,0:T(8,128)(2,1)} %copy-done.13) | copy-start | bytes 184324
  192.2 3.3 %copy-start.16 = (f16[80,384]{1,0:T(8,128)(2,1)S(1)}, f16[80,384]{1,0:T(8,128)(2,1)}, u32[]{:S(2)}) copy-start(f16[80,384]{1,0:T(8,128)(2,1)} %copy-done.15) | copy-start | bytes 184324
  192.2 3.3 %copy-start.18 = (f16[80,384]{1,0:T(8,128)(2,1)S(1)}, f16[80,384]{1,0:T(8,128)(2,1)}, u32[]{:S(2)}) copy-start(f16[80,384]{1,0:T(8,128)(2,1)} %copy-done.17) | copy-start | bytes 184324
  192.2 3.3 %copy-start.20 = (f16[80,384]{1,0:T(8,128)(2,1)S(1)}, f16[80,384]{1,0:T(8,128)(2,1)}, u32[]{:S(2)}) copy-start(f16[80,384]{1,0:T(8,128)(2,1)} %copy-done.19) | copy-start | bytes 184324
  192.3 3.3 %copy-start.22 = (f16[80,384]{1,0:T(8,128)(2,1)S(1)}, f16[80,384]{1,0:T(8,128)(2,1)}, u32[]{:S(2)}) copy-start(f16[80,384]{1,0:T(8,128)(2,1)} %copy-done.21) | copy-start | bytes 184324
  192.3 3.3 %copy-start.24 = (f16[80,384]{1,0:T(8,128)(2,1)S(1)}, f16[80,384]{1,0:T(8,128)(2,1)}, u32[]{:S(2)}) copy-start(f16[80,384]{1,0:T(8,128)(2,1)} %copy-done.23) | copy-start | bytes 184324
  194.0 6.5 %collective-permute-start.14 = (bf16[4,160,384]{2,1,0:T(8,128)(2,1)S(1)}, bf16[4,160,384]{2,1,0:T(8,128)(2,1)S(1)}, u32[]{:S(2)}, u32[]{:S(2)}) collective-permute-start(bf16[4,160,384]{2,1,0:T(8,128)(2,1)S(1)} %get-tuple-element.54.refs_0_), channel_id=1, source_target_pairs={{0,8},{8,0},{1,9},{9,1},{2,10},{10,2},{3,11},{11,3},{4,12},{12,4},... | collective-permute-start | bytes 1474568 | tf_op jit(solution)/shard_map/ppermute | solution.py:18
  195.0 5.6 %collective-permute-start.15 = (bf16[4,160,384]{2,1,0:T(8,128)(2,1)S(1)}, bf16[4,160,384]{2,1,0:T(8,128)(2,1)S(1)}, u32[]{:S(2)}, u32[]{:S(2)}) collective-permute-start(bf16[4,160,384]{2,1,0:T(8,128)(2,1)S(1)} %get-tuple-element.53.refs_1_), channel_id=1, source_target_pairs={{0,8},{8,0},{1,9},{9,1},{2,10},{10,2},{3,11},{11,3},{4,12},{12,4},... | collective-permute-start | bytes 1474568 | tf_op jit(solution)/shard_map/ppermute | solution.py:18
  195.1 5.5 %collective-permute-start.16 = (bf16[4,160,384]{2,1,0:T(8,128)(2,1)S(1)}, bf16[4,160,384]{2,1,0:T(8,128)(2,1)S(1)}, u32[]{:S(2)}, u32[]{:S(2)}) collective-permute-start(bf16[4,160,384]{2,1,0:T(8,128)(2,1)S(1)} %get-tuple-element.52.refs_2_), channel_id=1, source_target_pairs={{0,8},{8,0},{1,9},{9,1},{2,10},{10,2},{3,11},{11,3},{4,12},{12,4},... | collective-permute-start | bytes 1474568 | tf_op jit(solution)/shard_map/ppermute | solution.py:18
  195.5 5.1 %collective-permute-start.17 = (bf16[4,160,384]{2,1,0:T(8,128)(2,1)S(1)}, bf16[4,160,384]{2,1,0:T(8,128)(2,1)}, u32[]{:S(2)}, u32[]{:S(2)}) collective-permute-start(bf16[4,160,384]{2,1,0:T(8,128)(2,1)S(1)} %get-tuple-element.51.refs_3_), channel_id=1, source_target_pairs={{0,8},{8,0},{1,9},{9,1},{2,10},{10,2},{3,11},{11,3},{4,12},{12,4},... | collective-permute-start | bytes 1474568 | tf_op jit(solution)/shard_map/ppermute | solution.py:18
  198.0 4.0 %slice-start = ((s8[5242880]{0:T(1024)(128)(4,1)}), s8[4194304]{0:T(1024)(128)(4,1)S(1)}, s32[]{:S(2)}) async-start(s8[5242880]{0:T(1024)(128)(4,1)} %bitcast.198), calls=%async_computation.5 | async-start | bytes 8388608
  (10 other events, 16.5 us)
Sparse Core Ops, SparseCore 0:
  14.9 47.3 all-gather.4
  137.8 51.9 all-gather.6

commit v2 on v0

--- a/solution.py
+++ b/solution.py
@@ -8,6 +8,7 @@
 f32, f16, bf16 = jnp.float32, jnp.float16, jnp.bfloat16
 HIGH = lax.Precision.HIGH
 PAD = 16
+KEY = 8
 TOP = 14.0
 ROW, COL = ("yl", "z", "c"), ("yh", "x")
 MIB = 2**20
@@ -31,17 +32,18 @@
 
 
 def payload(a):
-    n = a.shape[-2] - PAD
+    n = a.shape[-2] - a.shape[-2] % 32
+    a = a[..., : n + KEY, :]
     k = scale_of(a[..., n : n + 1, :])
     return jnp.where(rows_of(a) < n, a * jnp.exp2(TOP - k), k).astype(f16)
 
 
 def dec(p):
-    return p[..., :-PAD, :].astype(f32) * jnp.exp2(p[..., -1:, :].astype(f32) - TOP)
+    return p[..., :-KEY, :].astype(f32) * jnp.exp2(p[..., -1:, :].astype(f32) - TOP)
 
 
 def enc(a):
-    wide = jnp.pad(a, [(0, PAD), (0, 0)])
+    wide = jnp.pad(a, [(0, KEY), (0, 0)])
     k = scale_of(jnp.max(jnp.abs(a)))
     return jnp.where(rows_of(wide) < a.shape[0], wide * jnp.exp2(TOP - k), k).astype(f16)
 
@@ -122,7 +124,7 @@
     parts = [two]
     parts += [lax.ppermute(two, "x", [(i, (i + d) % 4) for i in range(4)]) for d in (1, -1, 2)]
     where = [(yh ^ j) * 4 + ((x - d) & 3) for d in (0, 1, -1, 2) for j in (0, 1)]
-    n, m = two.shape[1] - PAD, two.shape[2]
+    n, m = two.shape[1] - KEY, two.shape[2]
     shape = jax.ShapeDtypeStruct((n, 8 * m), f32)
     return place(where, [dec(p) for p in parts], shape, put_columns)
 
@@ -132,16 +134,16 @@
 
 
 def sum_mates(keep, send):
-    x = keep + swap(send, "c").astype(f32)
-    return payload(x[1]), x[0]
+    got = swap(send, "c")
+    return payload(keep[1] + got[1].astype(f32)), (keep[0], got[0])
 
 
 def blocks_z(sent, own):
     mate = swap(sent, "yl")
-    n = own.shape[1] - PAD
+    n = mate.shape[1] - KEY
     k = mate[:, n : n + 1].astype(f32)
-    got = jnp.where(rows_of(own) < n, mate.astype(f32) * jnp.exp2(k - TOP), jnp.exp2(k))
-    return payload(own + got)
+    got = jnp.where(rows_of(mate) < n, mate.astype(f32) * jnp.exp2(k - TOP), jnp.exp2(k))
+    return payload(own[0][:, : n + KEY] + own[1][:, : n + KEY].astype(f32) + got)
 
 
 def parts_z(blocks, z):

time: 206 us -> 203 us (0.985)
  waiting for transfers between devices: 54.3 us -> 47.8 us
  other arithmetic: 30.7 us -> 33.7 us
    squeeze x0 -> x2, other arithmetic: none -> 5.37 us  [sum_mates(): return (payload(keep[1] + got[1].astype(f32)), (keep[0], got[0]))]
    ppermute x13, waiting for transfers between devices: 15.8 us -> 11.2 us  [swap(): return lax.ppermute(a, axis, [(0, 1), (1, 0)])]
    add x4 -> x2, other arithmetic: 6.08 us -> 1.89 us  [blocks_z(): return payload(own[0][:, :n + KEY] + own[1][:, :n + KEY].astype(f32) + got)]
    unnamed x95 -> x91, local copies, waits for them, and re-layouts: 14.6 us -> 11.6 us
  transfers between devices with their start and end apart: 31 -> 31, of which waited for: 17 -> 14; matrix products, arithmetic and copies ran while one was open for 16% -> 18% of each run, Pallas kernels for 8% -> 8%
where the time goes in v2:
time: 203 us; the launch traced here: 201 us
  starting transfers between devices  61.3 us (30%)
  waiting for transfers between devices  47.8 us (24%)
  other arithmetic  33.7 us (17%)
  Pallas kernels  20.9 us (10%)
  between operations  16.5 us (8%)
  local copies, waits for them, and re-layouts  15.7 us (8%)
  matrix products  5.14 us (3%)
    ppermute x13, starting transfers between devices, swap(): return lax.ppermute(a, axis, [(0, 1), (1, 0)])  19.7 us
    ppermute x7, starting transfers between devices, parts_z(): got.append(lax.ppermute(block, 'z', [(i, (i + d) % 8) for i in range(8)]))  13.7 us
    unnamed x91, local copies, waits for them, and re-layouts  11.6 us
    all_to_all x2, starting transfers between devices, swap_col(): return lax.all_to_all(blocks, COL, 0, 0, tiled=True)  11.4 us
    ppermute x13, waiting for transfers between devices, swap(): return lax.ppermute(a, axis, [(0, 1), (1, 0)])  11.2 us
    all_gather x2, waiting for transfers between devices, gather_z(): return lax.all_gather(two, 'z').reshape((16,) + two.shape[1:])  10.5 us
    pallas_call x1, Pallas kernels, weight_parts(): pl.pallas_call(weight_kernel, grid_spec=pltpu.PrefetchScalarGridSpec(num_...  10.3 us
    ppermute x7, waiting for transfers between devices, parts_z(): got.append(lax.ppermute(block, 'z', [(i, (i + d) % 8) for i in range(8)]))  9.34 us
  transfers between devices with their start and end apart: 31, of which 14 were waited for; matrix products, arithmetic and copies ran while one was open for 18% of the time, Pallas kernels for 8%

profile of v2, /device:TPU:1, one launch (start us, length us, event | category | flops | bytes accessed | tf_op | source)
XLA Modules:
  0.0 201.1 jit_solution(1417839807201062877)
XLA Ops:
  9.0 2.2 %collective-permute-start.1 = (bf16[320,256]{1,0:T(8,128)(2,1)S(1)}, bf16[320,256]{1,0:T(8,128)(2,1)S(1)}, u32[]{:S(2)}, u32[]{:S(2)}) collective-permute-start(bf16[320,256]{1,0:T(8,128)(2,1)S(1)} %maximum_dynamic-update-slice_fusion), channel_id=1, source_target_pairs={{0,128},{128,0},{1,129},{129,1},{2,130},{130,2},{3,131},{131,3},{4... | collective-permute-start | bytes 491528 | tf_op jit(solution)/shard_map/ppermute | solution.py:19
  11.2 2.7 %collective-permute-done.1 = bf16[320,256]{1,0:T(8,128)(2,1)S(1)} collective-permute-done((bf16[320,256]{1,0:T(8,128)(2,1)S(1)}, bf16[320,256]{1,0:T(8,128)(2,1)S(1)}, u32[]{:S(2)}, u32[]{:S(2)}) %collective-permute-start.1) | collective-permute-done | bytes 163872 | tf_op jit(solution)/shard_map/ppermute | solution.py:19
  15.4 10.3 %shard_map.76 = (f32[2,8,176,384]{3,2,1,0:T(8,128)}, bf16[2,8,176,384]{3,2,1,0:T(8,128)(2,1)}) custom-call(s32[2]{0:T(128)} %pad_add_fusion.place_ref, bf16[512,5120]{1,0:T(8,128)(2,1)} %tokens_ref, bf16[512,384]{1,0:T(8,128)(2,1)} %cotangent_ref.1), custom_call_target="tpu_custom_call" | custom-call | flops 2013265920 | bytes 12582912 | tf_op jit(solution)/shard_map/pallas_call | solution.py:187
  25.6 3.7 %collective-permute-start.2 = (bf16[2,8,176,384]{3,2,1,0:T(8,128)(2,1)}, bf16[2,8,176,384]{3,2,1,0:T(8,128)(2,1)S(1)}, u32[]{:S(2)}, u32[]{:S(2)}) collective-permute-start(bf16[2,8,176,384]{3,2,1,0:T(8,128)(2,1)} %get-tuple-element.18), channel_id=1, source_target_pairs={{0,8},{8,0},{1,9},{9,1},{2,10},{10,2},{3,11},{11,3},{4,12},{12,4},... | collective-permute-start | bytes 6488072 | tf_op jit(solution)/shard_map/ppermute | solution.py:19
  30.9 1.9 collective-permute-start
  33.1 5.4 %collective-permute-done = f16[168,512]{1,0:T(8,128)(2,1)S(1)} collective-permute-done((f16[168,512]{1,0:T(8,128)(2,1)S(1)}, f16[168,512]{1,0:T(8,128)(2,1)S(1)}, u32[]{:S(2)}, u32[]{:S(2)}) %collective-permute-start) | collective-permute-done | bytes 172064 | tf_op jit(solution)/shard_map/ppermute | solution.py:19
  38.5 4.2 %slice_bitcast_fusion = (f32[8,176,384]{2,1,0:T(8,128)}, f32[8,176,384]{2,1,0:T(8,128)S(1)}) fusion(f32[2,8,176,384]{3,2,1,0:T(8,128)} %get-tuple-element.17, bf16[2,8,176,384]{3,2,1,0:T(8,128)(2,1)S(1)} %collective-permute-done.2), kind=kLoop, calls=%fused_computation.4 | loop fusion | flops 1081344 | bytes 9732096 | tf_op jit(solution)/shard_map/squeeze | solution.py:138
  42.8 1.3 fusion.4
  44.4 2.7 %collective-permute-start.5 = (f16[2,168,512]{2,1,0:T(8,128)(2,1)S(1)}, f16[2,168,512]{2,1,0:T(8,128)(2,1)S(1)}, u32[]{:S(2)}, u32[]{:S(2)}) collective-permute-start(f16[2,168,512]{2,1,0:T(8,128)(2,1)S(1)} %pad_maximum_fusion), channel_id=1, source_target_pairs={{0,2},{1,3},{2,0},{3,1},{4,6},{5,7},{6,4},{7,5},{8,10},{9,11},{10,... | collective-permute-start | bytes 1032200 | tf_op jit(solution)/shard_map/ppermute | solution.py:125
  49.8 9.8 %all-gather.5.cloned.1.call-done.refs_0_ = bf16[16,320,256]{2,1,0:T(8,128)(2,1)} async-done(((bf16[2,320,256]{2,1,0:T(8,128)(2,1)}), bf16[16,320,256]{2,1,0:T(8,128)(2,1)}) %all-gather.5.cloned.1.call-update) | async-done | bytes 2621456 | tf_op jit(solution)/shard_map/all_gather | solution.py:67
  59.6 3.4 %collective-permute-start.6 = (bf16[16,320,256]{2,1,0:T(8,128)(2,1)}, bf16[16,320,256]{2,1,0:T(8,128)(2,1)S(1)}, u32[]{:S(2)}, u32[]{:S(2)}) collective-permute-start(bf16[16,320,256]{2,1,0:T(8,128)(2,1)} %all-gather.5.cloned.1.call-done.refs_0_), channel_id=1, source_target_pairs={{0,8},{8,0},{1,9},{9,1},{2,10},{10,2},{3,11},{11,3},{4,12},{12,4},... | collective-permute-start | bytes 7864328 | tf_op jit(solution)/shard_map/ppermute | solution.py:19
  69.3 1.7 fusion.2
  71.0 1.3 select_convert_fusion
  72.3 7.8 %all-to-all-start = ((f16[8,168,384]{2,1,0:T(8,128)(2,1)}), f16[8,168,384]{2,1,0:T(8,128)(2,1)}, u32[]{:S(2)}, u32[]{:S(2)}) async-start(f16[8,168,384]{2,1,0:T(8,128)(2,1)} %select_convert_fusion), calls=%async_computation | async-start | bytes 2064384 | tf_op jit(solution)/shard_map/all_to_all | solution.py:284
  80.1 1.6 copy-done.7
  81.7 1.9 copy-done.6
  83.6 1.7 copy-done.8
  86.2 1.5 abs_reduce_fusion.1
  88.5 2.6 %collective-permute-start.7 = (f16[168,256]{1,0:T(8,128)(2,1)S(1)}, f16[168,256]{1,0:T(8,128)(2,1)S(1)}, u32[]{:S(2)}, u32[]{:S(2)}) collective-permute-start(f16[168,256]{1,0:T(8,128)(2,1)S(1)} %select_convert_fusion.3), channel_id=1, source_target_pairs={{0,4},{4,0},{1,5},{5,1},{2,6},{6,2},{3,7},{7,3},{8,12},{12,8},{9,1... | collective-permute-start | bytes 258056 | tf_op jit(solution)/shard_map/ppermute | solution.py:19
  91.2 2.6 %collective-permute-done.7 = f16[168,256]{1,0:T(8,128)(2,1)S(1)} collective-permute-done((f16[168,256]{1,0:T(8,128)(2,1)S(1)}, f16[168,256]{1,0:T(8,128)(2,1)S(1)}, u32[]{:S(2)}, u32[]{:S(2)}) %collective-permute-start.7) | collective-permute-done | bytes 86048 | tf_op jit(solution)/shard_map/ppermute | solution.py:19
  93.9 2.8 %collective-permute-start.10 = (f16[2,168,256]{2,1,0:T(8,128)(2,1)S(1)}, f16[2,168,256]{2,1,0:T(8,128)(2,1)S(1)}, u32[]{:S(2)}, u32[]{:S(2)}) collective-permute-start(f16[2,168,256]{2,1,0:T(8,128)(2,1)S(1)} %pad_maximum_fusion.3), channel_id=1, source_target_pairs={{0,2},{1,3},{2,0},{3,1},{4,6},{5,7},{6,4},{7,5},{8,10},{9,11},{10,... | collective-permute-start | bytes 516104 | tf_op jit(solution)/shard_map/ppermute | solution.py:125
  96.7 1.6 collective-permute-start.9
  98.4 1.6 collective-permute-done.10
  100.0 4.5 %collective-permute-done.9 = f16[2,168,256]{2,1,0:T(8,128)(2,1)S(1)} collective-permute-done((f16[2,168,256]{2,1,0:T(8,128)(2,1)S(1)}, f16[2,168,256]{2,1,0:T(8,128)(2,1)S(1)}, u32[]{:S(2)}, u32[]{:S(2)}) %collective-permute-start.9) | collective-permute-done | bytes 172064 | tf_op jit(solution)/shard_map/ppermute | solution.py:125
  104.5 1.4 collective-permute-done.8
  106.7 1.5 convolution_convert_fusion
  110.1 1.4 multiply_reduce_fusion.1.a_ref.grad_ref
  112.9 3.7 %shard_map.81 = (f32[2,8,80,384]{3,2,1,0:T(8,128)S(1)}, bf16[2,8,80,384]{3,2,1,0:T(8,128)(2,1)}) custom-call(s32[2]{0:T(128)S(1)} %copy-done.11, f32[160,2048]{1,0:T(8,128)S(1)} %copy-done.5, f32[160,384]{1,0:T(8,128)S(1)} %multiply_reduce_fusion.1.a_ref.grad_ref), custom_call_target="tpu_custom_call" | custom-call | flops 754974720 | bytes 6291456 | tf_op jit(solution)/shard_map/pallas_call | solution.py:226
  117.8 1.7 collective-permute-start.13
  119.8 1.7 shard_map.80
  122.6 5.6 %all-to-all-start.1 = ((f16[8,168,256]{2,1,0:T(8,128)(2,1)}), f16[8,168,256]{2,1,0:T(8,128)(2,1)}, u32[]{:S(2)}, u32[]{:S(2)}) async-start(f16[8,168,256]{2,1,0:T(8,128)(2,1)} %fusion.6), calls=%async_computation.1 | async-start | bytes 1376256 | tf_op jit(solution)/shard_map/all_to_all | solution.py:133
  132.6 9.3 %all-to-all-done.1 = f16[8,168,256]{2,1,0:T(8,128)(2,1)} async-done(((f16[8,168,256]{2,1,0:T(8,128)(2,1)}), f16[8,168,256]{2,1,0:T(8,128)(2,1)}, u32[]{:S(2)}, u32[]{:S(2)}) %all-to-all-start.1) | async-done | bytes 688160 | tf_op jit(solution)/shard_map/all_to_all | solution.py:133
  143.9 1.5 shard_map.82
  146.6 1.7 fusion.1
  148.9 2.5 %collective-permute-start.25 = (f16[72,384]{1,0:T(8,128)(2,1)S(1)}, f16[72,384]{1,0:T(8,128)(2,1)S(1)}, u32[]{:S(2)}, u32[]{:S(2)}) collective-permute-start(f16[72,384]{1,0:T(8,128)(2,1)S(1)} %get-tuple-element.61), channel_id=1, source_target_pairs={{0,112},{16,0},{32,16},{48,32},{64,48},{80,64},{96,80},{112,96},{1... | collective-permute-start | bytes 165896 | tf_op jit(solution)/shard_map/ppermute | solution.py:153
  151.5 5.8 %all-to-all-start.2 = ((f16[8,168,512]{2,1,0:T(8,128)(2,1)}), f16[8,168,512]{2,1,0:T(8,128)(2,1)}, u32[]{:S(2)}, u32[]{:S(2)}) async-start(f16[8,168,512]{2,1,0:T(8,128)(2,1)} %fusion.1), calls=%async_computation.2 | async-start | bytes 2752512 | tf_op jit(solution)/shard_map/all_to_all | solution.py:133
  157.3 2.1 %collective-permute-start.24 = (f16[72,384]{1,0:T(8,128)(2,1)S(1)}, f16[72,384]{1,0:T(8,128)(2,1)S(1)}, u32[]{:S(2)}, u32[]{:S(2)}) collective-permute-start(f16[72,384]{1,0:T(8,128)(2,1)S(1)} %get-tuple-element.62), channel_id=1, source_target_pairs={{0,96},{16,112},{32,0},{48,16},{64,32},{80,48},{96,64},{112,80},{1... | collective-permute-start | bytes 165896 | tf_op jit(solution)/shard_map/ppermute | solution.py:153
  160.6 3.3 %collective-permute-start.22 = (f16[72,384]{1,0:T(8,128)(2,1)S(1)}, f16[72,384]{1,0:T(8,128)(2,1)S(1)}, u32[]{:S(2)}, u32[]{:S(2)}) collective-permute-start(f16[72,384]{1,0:T(8,128)(2,1)S(1)} %get-tuple-element.64), channel_id=1, source_target_pairs={{0,64},{16,80},{32,96},{48,112},{64,0},{80,16},{96,32},{112,48},{1... | collective-permute-start | bytes 165896 | tf_op jit(solution)/shard_map/ppermute | solution.py:153
  163.9 3.3 %collective-permute-start.20 = (f16[72,384]{1,0:T(8,128)(2,1)S(1)}, f16[72,384]{1,0:T(8,128)(2,1)S(1)}, u32[]{:S(2)}, u32[]{:S(2)}) collective-permute-start(f16[72,384]{1,0:T(8,128)(2,1)S(1)} %get-tuple-element.66), channel_id=1, source_target_pairs={{0,32},{16,48},{32,64},{48,80},{64,96},{80,112},{96,0},{112,16},{1... | collective-permute-start | bytes 165896 | tf_op jit(solution)/shard_map/ppermute | solution.py:153
  168.9 5.8 %collective-permute-done.21 = f16[72,384]{1,0:T(8,128)(2,1)S(1)} collective-permute-done((f16[72,384]{1,0:T(8,128)(2,1)S(1)}, f16[72,384]{1,0:T(8,128)(2,1)S(1)}, u32[]{:S(2)}, u32[]{:S(2)}) %collective-permute-start.21) | collective-permute-done | bytes 55328 | tf_op jit(solution)/shard_map/ppermute | solution.py:153
  174.7 1.7 collective-permute-done.20
  176.4 1.6 collective-permute-done.19
  179.4 1.7 fusion.97
  181.1 2.7 %collective-permute-start.14 = (bf16[4,160,384]{2,1,0:T(8,128)(2,1)S(1)}, bf16[4,160,384]{2,1,0:T(8,128)(2,1)S(1)}, u32[]{:S(2)}, u32[]{:S(2)}) collective-permute-start(bf16[4,160,384]{2,1,0:T(8,128)(2,1)S(1)} %get-tuple-element.57.refs_0_), channel_id=1, source_target_pairs={{0,8},{8,0},{1,9},{9,1},{2,10},{10,2},{3,11},{11,3},{4,12},{12,4},... | collective-permute-start | bytes 1474568 | tf_op jit(solution)/shard_map/ppermute | solution.py:19
  184.4 1.5 fusion.19
  186.9 2.5 %multiply_reduce_fusion = f32[160,512]{1,0:T(8,128)} fusion(f16[8,168,512]{2,1,0:T(8,128)(2,1)} %all-to-all-done.2, f32[8,512]{1,0:T(8,128)S(1)} %bitcast.194), kind=kLoop, calls=%fused_computation.3 | loop fusion | flops 1884160 | bytes 1654784 | tf_op jit(solution)/shard_map/reduce_sum | solution.py:295
  189.4 1.5 shard_map.83
  190.9 2.2 %convolution_bitcast_fusion = f32[512,384]{0,1:T(8,128)S(1)} fusion(bf16[5120,384]{1,0:T(8,128)(2,1)S(1)} %bitcast.187, bf16[512,5120]{1,0:T(8,128)(2,1)S(1)} %bitcast.220), kind=kOutput, calls=%fused_computation.17 | convolution fusion | flops 2013265920 | bytes 9961472 | tf_op jit(solution)/shard_map/dot_general | solution.py:301
  (192 shorter events, 36.3 us)
Async XLA Ops:
  7.2 52.4 %all-gather.5.cloned.1.call-start = ((), (), s32[]{:S(2)}) async-start(), calls=%async_computation.3 | async-start | bytes 2949120 | tf_op jit(solution)/shard_map/all_gather | solution.py:67
  9.0 4.9 %collective-permute-start.1 = (bf16[320,256]{1,0:T(8,128)(2,1)S(1)}, bf16[320,256]{1,0:T(8,128)(2,1)S(1)}, u32[]{:S(2)}, u32[]{:S(2)}) collective-permute-start(bf16[320,256]{1,0:T(8,128)(2,1)S(1)} %maximum_dynamic-update-slice_fusion), channel_id=1, source_target_pairs={{0,128},{128,0},{1,129},{129,1},{2,130},{130,2},{3,131},{131,3},{4... | collective-permute-start | bytes 491528 | tf_op jit(solution)/shard_map/ppermute | solution.py:19
  15.4 14.0 %copy-start.14 = (f32[160,512]{1,0:T(8,128)S(1)}, f32[160,512]{1,0:T(8,128)}, u32[]{:S(2)}) copy-start(f32[160,512]{1,0:T(8,128)} %param.8) | copy-start | bytes 983044
  25.6 12.9 %collective-permute-start.2 = (bf16[2,8,176,384]{3,2,1,0:T(8,128)(2,1)}, bf16[2,8,176,384]{3,2,1,0:T(8,128)(2,1)S(1)}, u32[]{:S(2)}, u32[]{:S(2)}) collective-permute-start(bf16[2,8,176,384]{3,2,1,0:T(8,128)(2,1)} %get-tuple-element.18), channel_id=1, source_target_pairs={{0,8},{8,0},{1,9},{9,1},{2,10},{10,2},{3,11},{11,3},{4,12},{12,4},... | collective-permute-start | bytes 6488072 | tf_op jit(solution)/shard_map/ppermute | solution.py:19
  30.9 7.6 %collective-permute-start = (f16[168,512]{1,0:T(8,128)(2,1)S(1)}, f16[168,512]{1,0:T(8,128)(2,1)S(1)}, u32[]{:S(2)}, u32[]{:S(2)}) collective-permute-start(f16[168,512]{1,0:T(8,128)(2,1)S(1)} %select_convert_fusion.2), channel_id=1, source_target_pairs={{0,4},{4,0},{1,5},{5,1},{2,6},{6,2},{3,7},{7,3},{8,12},{12,8},{9,1... | collective-permute-start | bytes 516104 | tf_op jit(solution)/shard_map/ppermute | solution.py:19
  44.1 23.9 %collective-permute-start.12 = (f16[8,168,384]{2,1,0:T(8,128)(2,1)}, f16[8,168,384]{2,1,0:T(8,128)(2,1)}, u32[]{:S(2)}, u32[]{:S(2)}) collective-permute-start(f16[8,168,384]{2,1,0:T(8,128)(2,1)} %fusion.4), channel_id=1, source_target_pairs={{0,128},{128,0},{1,129},{129,1},{2,130},{130,2},{3,131},{131,3},{4... | collective-permute-start | bytes 3096584 | tf_op jit(solution)/shard_map/ppermute | solution.py:19
  44.4 18.6 %collective-permute-start.5 = (f16[2,168,512]{2,1,0:T(8,128)(2,1)S(1)}, f16[2,168,512]{2,1,0:T(8,128)(2,1)S(1)}, u32[]{:S(2)}, u32[]{:S(2)}) collective-permute-start(f16[2,168,512]{2,1,0:T(8,128)(2,1)S(1)} %pad_maximum_fusion), channel_id=1, source_target_pairs={{0,2},{1,3},{2,0},{3,1},{4,6},{5,7},{6,4},{7,5},{8,10},{9,11},{10,... | collective-permute-start | bytes 1032200 | tf_op jit(solution)/shard_map/ppermute | solution.py:125
  47.2 15.9 %collective-permute-start.4 = (f16[2,168,512]{2,1,0:T(8,128)(2,1)S(1)}, f16[2,168,512]{2,1,0:T(8,128)(2,1)}, u32[]{:S(2)}, u32[]{:S(2)}) collective-permute-start(f16[2,168,512]{2,1,0:T(8,128)(2,1)S(1)} %pad_maximum_fusion), channel_id=1, source_target_pairs={{0,3},{1,0},{2,1},{3,2},{4,7},{5,4},{6,5},{7,6},{8,11},{9,8},{10,9... | collective-permute-start | bytes 1032200 | tf_op jit(solution)/shard_map/ppermute | solution.py:125
  48.0 15.8 %collective-permute-start.3 = (f16[2,168,512]{2,1,0:T(8,128)(2,1)S(1)}, f16[2,168,512]{2,1,0:T(8,128)(2,1)}, u32[]{:S(2)}, u32[]{:S(2)}) collective-permute-start(f16[2,168,512]{2,1,0:T(8,128)(2,1)S(1)} %pad_maximum_fusion), channel_id=1, source_target_pairs={{0,1},{1,2},{2,3},{3,0},{4,5},{5,6},{6,7},{7,4},{8,9},{9,10},{10,1... | collective-permute-start | bytes 1032200 | tf_op jit(solution)/shard_map/ppermute | solution.py:125
  59.6 20.5 %collective-permute-start.6 = (bf16[16,320,256]{2,1,0:T(8,128)(2,1)}, bf16[16,320,256]{2,1,0:T(8,128)(2,1)S(1)}, u32[]{:S(2)}, u32[]{:S(2)}) collective-permute-start(bf16[16,320,256]{2,1,0:T(8,128)(2,1)} %all-gather.5.cloned.1.call-done.refs_0_), channel_id=1, source_target_pairs={{0,8},{8,0},{1,9},{9,1},{2,10},{10,2},{3,11},{11,3},{4,12},{12,4},... | collective-permute-start | bytes 7864328 | tf_op jit(solution)/shard_map/ppermute | solution.py:19
  72.3 36.9 %all-to-all-start = ((f16[8,168,384]{2,1,0:T(8,128)(2,1)}), f16[8,168,384]{2,1,0:T(8,128)(2,1)}, u32[]{:S(2)}, u32[]{:S(2)}) async-start(f16[8,168,384]{2,1,0:T(8,128)(2,1)} %select_convert_fusion), calls=%async_computation | async-start | bytes 2064384 | tf_op jit(solution)/shard_map/all_to_all | solution.py:284
  80.1 6.1 %copy-start.1 = (f32[160,4096]{1,0:T(8,128)S(1)}, f32[160,4096]{1,0:T(8,128)}, u32[]{:S(2)}) copy-start(f32[160,4096]{1,0:T(8,128)} %copy-done) | copy-start | bytes 7864324
  88.5 5.3 %collective-permute-start.7 = (f16[168,256]{1,0:T(8,128)(2,1)S(1)}, f16[168,256]{1,0:T(8,128)(2,1)S(1)}, u32[]{:S(2)}, u32[]{:S(2)}) collective-permute-start(f16[168,256]{1,0:T(8,128)(2,1)S(1)} %select_convert_fusion.3), channel_id=1, source_target_pairs={{0,4},{4,0},{1,5},{5,1},{2,6},{6,2},{3,7},{7,3},{8,12},{12,8},{9,1... | collective-permute-start | bytes 258056 | tf_op jit(solution)/shard_map/ppermute | solution.py:19
  93.9 6.1 %collective-permute-start.10 = (f16[2,168,256]{2,1,0:T(8,128)(2,1)S(1)}, f16[2,168,256]{2,1,0:T(8,128)(2,1)S(1)}, u32[]{:S(2)}, u32[]{:S(2)}) collective-permute-start(f16[2,168,256]{2,1,0:T(8,128)(2,1)S(1)} %pad_maximum_fusion.3), channel_id=1, source_target_pairs={{0,2},{1,3},{2,0},{3,1},{4,6},{5,7},{6,4},{7,5},{8,10},{9,11},{10,... | collective-permute-start | bytes 516104 | tf_op jit(solution)/shard_map/ppermute | solution.py:125
  96.7 7.8 %collective-permute-start.9 = (f16[2,168,256]{2,1,0:T(8,128)(2,1)S(1)}, f16[2,168,256]{2,1,0:T(8,128)(2,1)S(1)}, u32[]{:S(2)}, u32[]{:S(2)}) collective-permute-start(f16[2,168,256]{2,1,0:T(8,128)(2,1)S(1)} %pad_maximum_fusion.3), channel_id=1, source_target_pairs={{0,3},{1,0},{2,1},{3,2},{4,7},{5,4},{6,5},{7,6},{8,11},{9,8},{10,9... | collective-permute-start | bytes 516104 | tf_op jit(solution)/shard_map/ppermute | solution.py:125
  98.4 7.6 %collective-permute-start.8 = (f16[2,168,256]{2,1,0:T(8,128)(2,1)S(1)}, f16[2,168,256]{2,1,0:T(8,128)(2,1)S(1)}, u32[]{:S(2)}, u32[]{:S(2)}) collective-permute-start(f16[2,168,256]{2,1,0:T(8,128)(2,1)S(1)} %pad_maximum_fusion.3), channel_id=1, source_target_pairs={{0,1},{1,2},{2,3},{3,0},{4,5},{5,6},{6,7},{7,4},{8,9},{9,10},{10,1... | collective-permute-start | bytes 516104 | tf_op jit(solution)/shard_map/ppermute | solution.py:125
  106.7 4.8 %copy-start.11 = (s32[2]{0:T(128)S(1)}, s32[2]{0:T(128)}, u32[]{:S(2)}) copy-start(s32[2]{0:T(128)} %pad_add_fusion.place_ref) | copy-start | bytes 28
  117.8 12.2 %collective-permute-start.13 = (bf16[2,8,80,384]{3,2,1,0:T(8,128)(2,1)}, bf16[2,8,80,384]{3,2,1,0:T(8,128)(2,1)}, u32[]{:S(2)}, u32[]{:S(2)}) collective-permute-start(bf16[2,8,80,384]{3,2,1,0:T(8,128)(2,1)} %get-tuple-element.25), channel_id=1, source_target_pairs={{0,8},{8,0},{1,9},{9,1},{2,10},{10,2},{3,11},{11,3},{4,12},{12,4},... | collective-permute-start | bytes 2949128 | tf_op jit(solution)/shard_map/ppermute | solution.py:19
  119.5 8.8 %collective-permute-start.11 = (bf16[160,384]{1,0:T(8,128)(2,1)S(1)}, bf16[160,384]{1,0:T(8,128)(2,1)}, u32[]{:S(2)}, u32[]{:S(2)}) collective-permute-start(bf16[160,384]{1,0:T(8,128)(2,1)S(1)} %convolution_convert_fusion), channel_id=1, source_target_pairs={{0,128},{128,0},{1,129},{129,1},{2,130},{130,2},{3,131},{131,3},{4... | collective-permute-start | bytes 368648 | tf_op jit(solution)/shard_map/ppermute | solution.py:19
  121.6 8.4 %copy-start.10 = (f32[2,8,80,384]{3,2,1,0:T(8,128)S(1)}, f32[2,8,80,384]{3,2,1,0:T(8,128)}, u32[]{:S(2)}) copy-start(f32[2,8,80,384]{3,2,1,0:T(8,128)} %copy-done.9) | copy-start | bytes 5898244
  122.6 19.2 %all-to-all-start.1 = ((f16[8,168,256]{2,1,0:T(8,128)(2,1)}), f16[8,168,256]{2,1,0:T(8,128)(2,1)}, u32[]{:S(2)}, u32[]{:S(2)}) async-start(f16[8,168,256]{2,1,0:T(8,128)(2,1)} %fusion.6), calls=%async_computation.1 | async-start | bytes 1376256 | tf_op jit(solution)/shard_map/all_to_all | solution.py:133
  128.2 51.1 %all-gather.7.cloned.1.call-start = ((), (), s32[]{:S(2)}) async-start(), calls=%async_computation.4 | async-start | bytes 2211840 | tf_op jit(solution)/shard_map/all_gather | solution.py:67
  131.2 12.7 %copy-start.3 = (bf16[32,128,256]{2,1,0:T(8,128)(2,1)S(1)}, bf16[32,128,256]{2,1,0:T(8,128)(2,1)}, u32[]{:S(2)}) copy-start(bf16[32,128,256]{2,1,0:T(8,128)(2,1)} %copy-done.2) | copy-start | bytes 6291460
  132.2 16.0 %collective-permute-start.18 = (f16[8,72,384]{2,1,0:T(8,128)(2,1)}, f16[8,72,384]{2,1,0:T(8,128)(2,1)S(1)}, u32[]{:S(2)}, u32[]{:S(2)}) collective-permute-start(f16[8,72,384]{2,1,0:T(8,128)(2,1)} %fusion.9), channel_id=1, source_target_pairs={{0,128},{128,0},{1,129},{129,1},{2,130},{130,2},{3,131},{131,3},{4... | collective-permute-start | bytes 1327112 | tf_op jit(solution)/shard_map/ppermute | solution.py:19
  148.8 29.3 %copy-start.15 = (f16[8,72,384]{2,1,0:T(8,128)(2,1)}, f16[8,72,384]{2,1,0:T(8,128)(2,1)S(1)}, u32[]{:S(2)}) copy-start(f16[8,72,384]{2,1,0:T(8,128)(2,1)S(1)} %select_convert_fusion.1) | copy-start | bytes 1327108
  148.9 15.0 %collective-permute-start.25 = (f16[72,384]{1,0:T(8,128)(2,1)S(1)}, f16[72,384]{1,0:T(8,128)(2,1)S(1)}, u32[]{:S(2)}, u32[]{:S(2)}) collective-permute-start(f16[72,384]{1,0:T(8,128)(2,1)S(1)} %get-tuple-element.61), channel_id=1, source_target_pairs={{0,112},{16,0},{32,16},{48,32},{64,48},{80,64},{96,80},{112,96},{1... | collective-permute-start | bytes 165896 | tf_op jit(solution)/shard_map/ppermute | solution.py:153
  151.5 34.5 %all-to-all-start.2 = ((f16[8,168,512]{2,1,0:T(8,128)(2,1)}), f16[8,168,512]{2,1,0:T(8,128)(2,1)}, u32[]{:S(2)}, u32[]{:S(2)}) async-start(f16[8,168,512]{2,1,0:T(8,128)(2,1)} %fusion.1), calls=%async_computation.2 | async-start | bytes 2752512 | tf_op jit(solution)/shard_map/all_to_all | solution.py:133
  157.3 10.0 %collective-permute-start.24 = (f16[72,384]{1,0:T(8,128)(2,1)S(1)}, f16[72,384]{1,0:T(8,128)(2,1)S(1)}, u32[]{:S(2)}, u32[]{:S(2)}) collective-permute-start(f16[72,384]{1,0:T(8,128)(2,1)S(1)} %get-tuple-element.62), channel_id=1, source_target_pairs={{0,96},{16,112},{32,0},{48,16},{64,32},{80,48},{96,64},{112,80},{1... | collective-permute-start | bytes 165896 | tf_op jit(solution)/shard_map/ppermute | solution.py:153
  159.4 9.2 %collective-permute-start.23 = (f16[72,384]{1,0:T(8,128)(2,1)S(1)}, f16[72,384]{1,0:T(8,128)(2,1)S(1)}, u32[]{:S(2)}, u32[]{:S(2)}) collective-permute-start(f16[72,384]{1,0:T(8,128)(2,1)S(1)} %get-tuple-element.63), channel_id=1, source_target_pairs={{0,80},{16,96},{32,112},{48,0},{64,16},{80,32},{96,48},{112,64},{1... | collective-permute-start | bytes 165896 | tf_op jit(solution)/shard_map/ppermute | solution.py:153
  160.6 8.2 %collective-permute-start.22 = (f16[72,384]{1,0:T(8,128)(2,1)S(1)}, f16[72,384]{1,0:T(8,128)(2,1)S(1)}, u32[]{:S(2)}, u32[]{:S(2)}) collective-permute-start(f16[72,384]{1,0:T(8,128)(2,1)S(1)} %get-tuple-element.64), channel_id=1, source_target_pairs={{0,64},{16,80},{32,96},{48,112},{64,0},{80,16},{96,32},{112,48},{1... | collective-permute-start | bytes 165896 | tf_op jit(solution)/shard_map/ppermute | solution.py:153
  163.9 10.8 %collective-permute-start.21 = (f16[72,384]{1,0:T(8,128)(2,1)S(1)}, f16[72,384]{1,0:T(8,128)(2,1)S(1)}, u32[]{:S(2)}, u32[]{:S(2)}) collective-permute-start(f16[72,384]{1,0:T(8,128)(2,1)S(1)} %get-tuple-element.65), channel_id=1, source_target_pairs={{0,48},{16,64},{32,80},{48,96},{64,112},{80,0},{96,16},{112,32},{1... | collective-permute-start | bytes 165896 | tf_op jit(solution)/shard_map/ppermute | solution.py:153
  163.9 12.5 %collective-permute-start.20 = (f16[72,384]{1,0:T(8,128)(2,1)S(1)}, f16[72,384]{1,0:T(8,128)(2,1)S(1)}, u32[]{:S(2)}, u32[]{:S(2)}) collective-permute-start(f16[72,384]{1,0:T(8,128)(2,1)S(1)} %get-tuple-element.66), channel_id=1, source_target_pairs={{0,32},{16,48},{32,64},{48,80},{64,96},{80,112},{96,0},{112,16},{1... | collective-permute-start | bytes 165896 | tf_op jit(solution)/shard_map/ppermute | solution.py:153
  167.3 10.8 %copy-start.16 = (f16[72,384]{1,0:T(8,128)(2,1)}, f16[72,384]{1,0:T(8,128)(2,1)S(1)}, u32[]{:S(2)}) copy-start(f16[72,384]{1,0:T(8,128)(2,1)S(1)} %collective-permute-done.24) | copy-start | bytes 165892
  167.3 10.8 %collective-permute-start.19 = (f16[72,384]{1,0:T(8,128)(2,1)S(1)}, f16[72,384]{1,0:T(8,128)(2,1)S(1)}, u32[]{:S(2)}, u32[]{:S(2)}) collective-permute-start(f16[72,384]{1,0:T(8,128)(2,1)S(1)} %get-tuple-element.60), channel_id=1, source_target_pairs={{0,16},{16,32},{32,48},{48,64},{64,80},{80,96},{96,112},{112,0},{1... | collective-permute-start | bytes 165896 | tf_op jit(solution)/shard_map/ppermute | solution.py:153
  168.6 9.5 %copy-start.18 = (f16[72,384]{1,0:T(8,128)(2,1)}, f16[72,384]{1,0:T(8,128)(2,1)S(1)}, u32[]{:S(2)}) copy-start(f16[72,384]{1,0:T(8,128)(2,1)S(1)} %collective-permute-done.23) | copy-start | bytes 165892
  168.9 9.3 %copy-start.20 = (f16[72,384]{1,0:T(8,128)(2,1)}, f16[72,384]{1,0:T(8,128)(2,1)S(1)}, u32[]{:S(2)}) copy-start(f16[72,384]{1,0:T(8,128)(2,1)S(1)} %collective-permute-done.22) | copy-start | bytes 165892
  174.7 3.4 %copy-start.22 = (f16[72,384]{1,0:T(8,128)(2,1)}, f16[72,384]{1,0:T(8,128)(2,1)S(1)}, u32[]{:S(2)}) copy-start(f16[72,384]{1,0:T(8,128)(2,1)S(1)} %collective-permute-done.21) | copy-start | bytes 165892
  179.4 5.0 %copy-start.17 = (f16[72,384]{1,0:T(8,128)(2,1)S(1)}, f16[72,384]{1,0:T(8,128)(2,1)}, u32[]{:S(2)}) copy-start(f16[72,384]{1,0:T(8,128)(2,1)} %copy-done.16) | copy-start | bytes 165892
  179.4 5.0 %copy-start.19 = (f16[72,384]{1,0:T(8,128)(2,1)S(1)}, f16[72,384]{1,0:T(8,128)(2,1)}, u32[]{:S(2)}) copy-start(f16[72,384]{1,0:T(8,128)(2,1)} %copy-done.18) | copy-start | bytes 165892
  179.4 5.0 %copy-start.21 = (f16[72,384]{1,0:T(8,128)(2,1)S(1)}, f16[72,384]{1,0:T(8,128)(2,1)}, u32[]{:S(2)}) copy-start(f16[72,384]{1,0:T(8,128)(2,1)} %copy-done.20) | copy-start | bytes 165892
  179.4 5.0 %copy-start.23 = (f16[72,384]{1,0:T(8,128)(2,1)S(1)}, f16[72,384]{1,0:T(8,128)(2,1)}, u32[]{:S(2)}) copy-start(f16[72,384]{1,0:T(8,128)(2,1)} %copy-done.22) | copy-start | bytes 165892
  179.4 5.0 %copy-start.25 = (f16[72,384]{1,0:T(8,128)(2,1)S(1)}, f16[72,384]{1,0:T(8,128)(2,1)}, u32[]{:S(2)}) copy-start(f16[72,384]{1,0:T(8,128)(2,1)} %copy-done.24) | copy-start | bytes 165892
  179.4 5.0 %copy-start.27 = (f16[72,384]{1,0:T(8,128)(2,1)S(1)}, f16[72,384]{1,0:T(8,128)(2,1)}, u32[]{:S(2)}) copy-start(f16[72,384]{1,0:T(8,128)(2,1)} %copy-done.26) | copy-start | bytes 165892
  181.1 8.2 %collective-permute-start.14 = (bf16[4,160,384]{2,1,0:T(8,128)(2,1)S(1)}, bf16[4,160,384]{2,1,0:T(8,128)(2,1)S(1)}, u32[]{:S(2)}, u32[]{:S(2)}) collective-permute-start(bf16[4,160,384]{2,1,0:T(8,128)(2,1)S(1)} %get-tuple-element.57.refs_0_), channel_id=1, source_target_pairs={{0,8},{8,0},{1,9},{9,1},{2,10},{10,2},{3,11},{11,3},{4,12},{12,4},... | collective-permute-start | bytes 1474568 | tf_op jit(solution)/shard_map/ppermute | solution.py:19
  183.8 5.6 %collective-permute-start.15 = (bf16[4,160,384]{2,1,0:T(8,128)(2,1)S(1)}, bf16[4,160,384]{2,1,0:T(8,128)(2,1)S(1)}, u32[]{:S(2)}, u32[]{:S(2)}) collective-permute-start(bf16[4,160,384]{2,1,0:T(8,128)(2,1)S(1)} %get-tuple-element.56.refs_1_), channel_id=1, source_target_pairs={{0,8},{8,0},{1,9},{9,1},{2,10},{10,2},{3,11},{11,3},{4,12},{12,4},... | collective-permute-start | bytes 1474568 | tf_op jit(solution)/shard_map/ppermute | solution.py:19
  183.9 5.5 %collective-permute-start.16 = (bf16[4,160,384]{2,1,0:T(8,128)(2,1)S(1)}, bf16[4,160,384]{2,1,0:T(8,128)(2,1)S(1)}, u32[]{:S(2)}, u32[]{:S(2)}) collective-permute-start(bf16[4,160,384]{2,1,0:T(8,128)(2,1)S(1)} %get-tuple-element.55.refs_2_), channel_id=1, source_target_pairs={{0,8},{8,0},{1,9},{9,1},{2,10},{10,2},{3,11},{11,3},{4,12},{12,4},... | collective-permute-start | bytes 1474568 | tf_op jit(solution)/shard_map/ppermute | solution.py:19
  184.3 5.1 %collective-permute-start.17 = (bf16[4,160,384]{2,1,0:T(8,128)(2,1)S(1)}, bf16[4,160,384]{2,1,0:T(8,128)(2,1)}, u32[]{:S(2)}, u32[]{:S(2)}) collective-permute-start(bf16[4,160,384]{2,1,0:T(8,128)(2,1)S(1)} %get-tuple-element.54.refs_3_), channel_id=1, source_target_pairs={{0,8},{8,0},{1,9},{9,1},{2,10},{10,2},{3,11},{11,3},{4,12},{12,4},... | collective-permute-start | bytes 1474568 | tf_op jit(solution)/shard_map/ppermute | solution.py:19
  186.8 4.0 %slice-start = ((s8[5242880]{0:T(1024)(128)(4,1)}), s8[4194304]{0:T(1024)(128)(4,1)S(1)}, s32[]{:S(2)}) async-start(s8[5242880]{0:T(1024)(128)(4,1)} %bitcast.219), calls=%async_computation.5 | async-start | bytes 8388608
  (13 other events, 22.5 us)
Sparse Core Ops, SparseCore 0:
  14.9 44.6 all-gather.4
  131.4 47.8 all-gather.6

commit v3 on v2

--- a/solution.py
+++ b/solution.py
@@ -133,9 +133,9 @@
     return lax.all_to_all(blocks, COL, 0, 0, tiled=True)
 
 
-def sum_mates(keep, send):
+def sum_mates(keep, keep_mate, send):
     got = swap(send, "c")
-    return payload(keep[1] + got[1].astype(f32)), (keep[0], got[0])
+    return payload(keep_mate + got[1].astype(f32)), (keep, got[0])
 
 
 def blocks_z(sent, own):
@@ -158,42 +158,53 @@
     return jnp.broadcast_to(jnp.max(jnp.abs(a), axis=0, keepdims=True), (rows, a.shape[1]))
 
 
-def split_cores(core, total_ref, j, n, keep_ref, send_ref, at):
+def split_cores(core, total_ref, j, n, keep_ref, send_ref, keep_at, send_at):
     keep = total_ref[pl.ds(pl.multiple_of(2 * n * j + n * core, 8), n), :]
     send = total_ref[pl.ds(pl.multiple_of(2 * n * j + n * (1 - core), 8), n), :]
-    keep_ref[(*at, slice(0, n))] = keep
-    keep_ref[(*at, slice(n, n + PAD))] = with_top(keep, PAD)
-    send_ref[(*at, slice(0, n))] = send.astype(bf16)
-    send_ref[(*at, slice(n, n + PAD))] = with_top(send, PAD).astype(bf16)
-
-
-def weight_kernel(place_ref, tokens_ref, cotangent_ref, keep_ref, send_ref, total_ref):
+    keep_ref[keep_at, :n] = keep
+    keep_ref[keep_at, n:] = with_top(keep, PAD)
+    send_ref[(*send_at, slice(0, n))] = send.astype(bf16)
+    send_ref[(*send_at, slice(n, n + PAD))] = with_top(send, PAD).astype(bf16)
+
+
+def weight_kernel(place_ref, tokens_ref, cotangent_ref, keep_ref, mate_ref, send_ref, total_ref):
     total_ref[...] = lax.dot_general(
         tokens_ref[...],
         cotangent_ref[...],
         (((0,), (0,)), ((), ())),
         preferred_element_type=f32,
     )
-    for j in range(2):
-        split_cores(place_ref[1], total_ref, j, 160, keep_ref, send_ref, (0, j))
+
+    def write(to_ref):
+        for j in range(2):
+            split_cores(place_ref[1], total_ref, j, 160, to_ref, send_ref, j, (0, j))
+
+    step = pl.program_id(0)
+    pl.when(step < 4)(lambda: write(keep_ref))
+    pl.when(step >= 4)(lambda: write(mate_ref))
 
 
 def split_shapes(n):
-    return [jax.ShapeDtypeStruct((2, 8, n + PAD, 384), kind) for kind in (f32, bf16)]
+    keep = jax.ShapeDtypeStruct((8, n + PAD, 384), f32)
+    return [keep, keep, jax.ShapeDtypeStruct((2, 8, n + PAD, 384), bf16)]
 
 
 def weight_parts(yl, c, tokens, cotangent):
-    block = pl.BlockSpec((1, 2, 160 + PAD, 384), lambda i, where: (where[0] ^ (i // 4), i % 4, 0, 0))
+    rows = 160 + PAD
     return pl.pallas_call(
         weight_kernel,
         grid_spec=pltpu.PrefetchScalarGridSpec(
             num_scalar_prefetch=1,
             grid=(8,),
             in_specs=[
-                pl.BlockSpec((512, 640), lambda i, where: (0, i)),
+                pl.BlockSpec((512, 640), lambda i, where: (0, (where[0] ^ (i // 4)) * 4 + i % 4)),
                 pl.BlockSpec((512, 384), lambda i, where: (0, 0)),
             ],
-            out_specs=[block, block],
+            out_specs=[
+                pl.BlockSpec((2, rows, 384), lambda i, where: (jnp.minimum(i, 3), 0, 0)),
+                pl.BlockSpec((2, rows, 384), lambda i, where: (jnp.maximum(i - 4, 0), 0, 0)),
+                pl.BlockSpec((1, 2, rows, 384), lambda i, where: (i // 4, i % 4, 0, 0)),
+            ],
             scratch_shapes=[pltpu.VMEM((640, 384), f32)],
         ),
         out_shape=split_shapes(160),
@@ -211,22 +222,22 @@
     )
 
 
-def share_kernel(place_ref, expanded_ref, grad_ref, keep_ref, send_ref, total_ref):
+def share_kernel(place_ref, expanded_ref, grad_ref, keep_ref, mate_ref, send_ref, total_ref):
     grad = halves(grad_ref[...])
     for i in range(4):
         rows = slice(512 * i, 512 * i + 512)
         total_ref[rows] = product(halves(expanded_ref[:, rows]), grad, ((0,), (0,)))
-    for j in range(16):
-        split_cores(
-            place_ref[1], total_ref, j, 64, keep_ref, send_ref, (place_ref[0] ^ (j // 8), j % 8)
-        )
+    for i, to_ref in enumerate((keep_ref, mate_ref)):
+        for z in range(8):
+            j = (place_ref[0] ^ i) * 8 + z
+            split_cores(place_ref[1], total_ref, j, 64, to_ref, send_ref, z, (i, z))
 
 
 def share_parts(yl, c, expanded, grad):
     return pl.pallas_call(
         share_kernel,
         in_specs=[SMEM, VMEM, VMEM],
-        out_specs=[VMEM, VMEM],
+        out_specs=[VMEM] * 3,
         out_shape=split_shapes(64),
         scratch_shapes=[pltpu.VMEM((2048, 384), f32)],
         compiler_params=pltpu.CompilerParams(vmem_limit_bytes=24 * MIB),

time: 203 us -> 201 us (level)
  other arithmetic: 33.7 us -> 31.3 us
    squeeze x2 -> x0, other arithmetic: 5.37 us -> none  [sum_mates(): return (payload(keep[1] + got[1].astype(f32)), (keep[0], got[0]))]
    add x0 -> x2, other arithmetic: none -> 3.21 us  [sum_mates(): return (payload(keep_mate + got[1].astype(f32)), (keep, got[0]))]
    unnamed x91 -> x95, local copies, waits for them, and re-layouts: 11.6 us -> 12.3 us
  transfers between devices with their start and end apart: 31 -> 31, of which waited for: 14 -> 13; matrix products, arithmetic and copies ran while one was open for 18% -> 17% of each run, Pallas kernels for 8% -> 8%
where the time goes in v3:
time: 201 us; the launch traced here: 200 us
  starting transfers between devices  59.5 us (30%)
  waiting for transfers between devices  49.8 us (25%)
  other arithmetic  31.3 us (16%)
  Pallas kernels  21 us (10%)
  local copies, waits for them, and re-layouts  16.6 us (8%)
  between operations  16.5 us (8%)
  matrix products  5.14 us (3%)
    ppermute x13, starting transfers between devices, swap(): return lax.ppermute(a, axis, [(0, 1), (1, 0)])  19.7 us
    ppermute x7, starting transfers between devices, parts_z(): got.append(lax.ppermute(block, 'z', [(i, (i + d) % 8) for i in range(8)]))  13.7 us
    unnamed x95, local copies, waits for them, and re-layouts  12.3 us
    all_gather x2, waiting for transfers between devices, gather_z(): return lax.all_gather(two, 'z').reshape((16,) + two.shape[1:])  12.1 us
    all_to_all x2, starting transfers between devices, swap_col(): return lax.all_to_all(blocks, COL, 0, 0, tiled=True)  11.4 us
    ppermute x13, waiting for transfers between devices, swap(): return lax.ppermute(a, axis, [(0, 1), (1, 0)])  10.7 us
    pallas_call x1, Pallas kernels, weight_parts(): pl.pallas_call(weight_kernel, grid_spec=pltpu.PrefetchScalarGridSpec(num_...  10.5 us
    all_to_all x2, waiting for transfers between devices, swap_col(): return lax.all_to_all(blocks, COL, 0, 0, tiled=True)  9.84 us
  transfers between devices with their start and end apart: 31, of which 13 were waited for; matrix products, arithmetic and copies ran while one was open for 17% of the time, Pallas kernels for 8%

profile of v3, /device:TPU:1, one launch (start us, length us, event | category | flops | bytes accessed | tf_op | source)
XLA Modules:
  0.0 199.8 jit_solution(5239232172279176221)
XLA Ops:
  9.0 2.2 %collective-permute-start.1 = (bf16[320,256]{1,0:T(8,128)(2,1)S(1)}, bf16[320,256]{1,0:T(8,128)(2,1)S(1)}, u32[]{:S(2)}, u32[]{:S(2)}) collective-permute-start(bf16[320,256]{1,0:T(8,128)(2,1)S(1)} %maximum_dynamic-update-slice_fusion), channel_id=1, source_target_pairs={{0,128},{128,0},{1,129},{129,1},{2,130},{130,2},{3,131},{131,3},{4... | collective-permute-start | bytes 491528 | tf_op jit(solution)/shard_map/ppermute | solution.py:19
  11.2 2.7 %collective-permute-done.1 = bf16[320,256]{1,0:T(8,128)(2,1)S(1)} collective-permute-done((bf16[320,256]{1,0:T(8,128)(2,1)S(1)}, bf16[320,256]{1,0:T(8,128)(2,1)S(1)}, u32[]{:S(2)}, u32[]{:S(2)}) %collective-permute-start.1) | collective-permute-done | bytes 163872 | tf_op jit(solution)/shard_map/ppermute | solution.py:19
  15.4 10.5 %shard_map.76 = (f32[8,176,384]{2,1,0:T(8,128)}, f32[8,176,384]{2,1,0:T(8,128)}, bf16[2,8,176,384]{3,2,1,0:T(8,128)(2,1)}) custom-call(s32[2]{0:T(128)} %pad_add_fusion.place_ref, bf16[512,5120]{1,0:T(8,128)(2,1)} %tokens_ref, bf16[512,384]{1,0:T(8,128)(2,1)} %cotangent_ref.1), custom_call_target="tpu_custom_call" | custom-call | flops 2013265920 | bytes 12582912 | tf_op jit(solution)/shard_map/pallas_call | solution.py:194
  25.9 3.7 %collective-permute-start.2 = (bf16[2,8,176,384]{3,2,1,0:T(8,128)(2,1)}, bf16[2,8,176,384]{3,2,1,0:T(8,128)(2,1)S(1)}, u32[]{:S(2)}, u32[]{:S(2)}) collective-permute-start(bf16[2,8,176,384]{3,2,1,0:T(8,128)(2,1)} %get-tuple-element.20), channel_id=1, source_target_pairs={{0,8},{8,0},{1,9},{9,1},{2,10},{10,2},{3,11},{11,3},{4,12},{12,4},... | collective-permute-start | bytes 6488072 | tf_op jit(solution)/shard_map/ppermute | solution.py:19
  31.1 1.9 collective-permute-start
  33.3 5.4 %collective-permute-done = f16[168,512]{1,0:T(8,128)(2,1)S(1)} collective-permute-done((f16[168,512]{1,0:T(8,128)(2,1)S(1)}, f16[168,512]{1,0:T(8,128)(2,1)S(1)}, u32[]{:S(2)}, u32[]{:S(2)}) %collective-permute-start) | collective-permute-done | bytes 172064 | tf_op jit(solution)/shard_map/ppermute | solution.py:19
  38.8 1.9 convert_add_fusion
  42.4 2.7 %collective-permute-start.5 = (f16[2,168,512]{2,1,0:T(8,128)(2,1)S(1)}, f16[2,168,512]{2,1,0:T(8,128)(2,1)S(1)}, u32[]{:S(2)}, u32[]{:S(2)}) collective-permute-start(f16[2,168,512]{2,1,0:T(8,128)(2,1)S(1)} %pad_maximum_fusion), channel_id=1, source_target_pairs={{0,2},{1,3},{2,0},{3,1},{4,6},{5,7},{6,4},{7,5},{8,10},{9,11},{10,... | collective-permute-start | bytes 1032200 | tf_op jit(solution)/shard_map/ppermute | solution.py:125
  47.8 11.4 %all-gather.5.cloned.1.call-done.refs_0_ = bf16[16,320,256]{2,1,0:T(8,128)(2,1)} async-done(((bf16[2,320,256]{2,1,0:T(8,128)(2,1)}), bf16[16,320,256]{2,1,0:T(8,128)(2,1)}) %all-gather.5.cloned.1.call-update) | async-done | bytes 2621456 | tf_op jit(solution)/shard_map/all_gather | solution.py:67
  59.2 3.6 %collective-permute-start.6 = (bf16[16,320,256]{2,1,0:T(8,128)(2,1)}, bf16[16,320,256]{2,1,0:T(8,128)(2,1)S(1)}, u32[]{:S(2)}, u32[]{:S(2)}) collective-permute-start(bf16[16,320,256]{2,1,0:T(8,128)(2,1)} %all-gather.5.cloned.1.call-done.refs_0_), channel_id=1, source_target_pairs={{0,8},{8,0},{1,9},{9,1},{2,10},{10,2},{3,11},{11,3},{4,12},{12,4},... | collective-permute-start | bytes 7864328 | tf_op jit(solution)/shard_map/ppermute | solution.py:19
  67.4 1.7 multiply_exponential_fusion.8
  69.1 1.7 select_add_fusion
  70.9 1.3 select_convert_fusion
  72.2 5.9 %all-to-all-start = ((f16[8,168,384]{2,1,0:T(8,128)(2,1)}), f16[8,168,384]{2,1,0:T(8,128)(2,1)}, u32[]{:S(2)}, u32[]{:S(2)}) async-start(f16[8,168,384]{2,1,0:T(8,128)(2,1)} %select_convert_fusion), calls=%async_computation | async-start | bytes 2064384 | tf_op jit(solution)/shard_map/all_to_all | solution.py:295
  78.1 1.5 copy-done.7
  79.6 1.9 copy-done.6
  81.5 1.7 copy-done.8
  84.2 1.5 abs_reduce_fusion.1
  86.5 2.6 %collective-permute-start.7 = (f16[168,256]{1,0:T(8,128)(2,1)S(1)}, f16[168,256]{1,0:T(8,128)(2,1)S(1)}, u32[]{:S(2)}, u32[]{:S(2)}) collective-permute-start(f16[168,256]{1,0:T(8,128)(2,1)S(1)} %select_convert_fusion.3), channel_id=1, source_target_pairs={{0,4},{4,0},{1,5},{5,1},{2,6},{6,2},{3,7},{7,3},{8,12},{12,8},{9,1... | collective-permute-start | bytes 258056 | tf_op jit(solution)/shard_map/ppermute | solution.py:19
  89.2 2.6 %collective-permute-done.7 = f16[168,256]{1,0:T(8,128)(2,1)S(1)} collective-permute-done((f16[168,256]{1,0:T(8,128)(2,1)S(1)}, f16[168,256]{1,0:T(8,128)(2,1)S(1)}, u32[]{:S(2)}, u32[]{:S(2)}) %collective-permute-start.7) | collective-permute-done | bytes 86048 | tf_op jit(solution)/shard_map/ppermute | solution.py:19
  91.9 2.8 %collective-permute-start.10 = (f16[2,168,256]{2,1,0:T(8,128)(2,1)S(1)}, f16[2,168,256]{2,1,0:T(8,128)(2,1)S(1)}, u32[]{:S(2)}, u32[]{:S(2)}) collective-permute-start(f16[2,168,256]{2,1,0:T(8,128)(2,1)S(1)} %pad_maximum_fusion.3), channel_id=1, source_target_pairs={{0,2},{1,3},{2,0},{3,1},{4,6},{5,7},{6,4},{7,5},{8,10},{9,11},{10,... | collective-permute-start | bytes 516104 | tf_op jit(solution)/shard_map/ppermute | solution.py:125
  94.7 1.6 collective-permute-start.9
  96.4 1.6 collective-permute-done.10
  98.0 4.5 %collective-permute-done.9 = f16[2,168,256]{2,1,0:T(8,128)(2,1)S(1)} collective-permute-done((f16[2,168,256]{2,1,0:T(8,128)(2,1)S(1)}, f16[2,168,256]{2,1,0:T(8,128)(2,1)S(1)}, u32[]{:S(2)}, u32[]{:S(2)}) %collective-permute-start.9) | collective-permute-done | bytes 172064 | tf_op jit(solution)/shard_map/ppermute | solution.py:125
  102.5 1.4 collective-permute-done.8
  104.7 1.5 convolution_convert_fusion
  108.1 1.4 multiply_reduce_fusion.1.a_ref.grad_ref
  110.8 3.6 %shard_map.81 = (f32[8,80,384]{2,1,0:T(8,128)S(1)}, f32[8,80,384]{2,1,0:T(8,128)S(1)}, bf16[2,8,80,384]{3,2,1,0:T(8,128)(2,1)}) custom-call(s32[2]{0:T(128)S(1)} %copy-done.13, f32[160,2048]{1,0:T(8,128)S(1)} %copy-done.5, f32[160,384]{1,0:T(8,128)S(1)} %multiply_reduce_fusion.1.a_ref.grad_ref), custom_call_target="tpu_custom_call" | custom-call | flops 754974720 | bytes 6291456 | tf_op jit(solution)/shard_map/pallas_call | solution.py:237
  116.5 1.6 collective-permute-start.13
  118.4 1.7 shard_map.80
  121.3 5.6 %all-to-all-start.1 = ((f16[8,168,256]{2,1,0:T(8,128)(2,1)}), f16[8,168,256]{2,1,0:T(8,128)(2,1)}, u32[]{:S(2)}, u32[]{:S(2)}) async-start(f16[8,168,256]{2,1,0:T(8,128)(2,1)} %fusion.5), calls=%async_computation.1 | async-start | bytes 1376256 | tf_op jit(solution)/shard_map/all_to_all | solution.py:133
  130.7 9.8 %all-to-all-done.1 = f16[8,168,256]{2,1,0:T(8,128)(2,1)} async-done(((f16[8,168,256]{2,1,0:T(8,128)(2,1)}), f16[8,168,256]{2,1,0:T(8,128)(2,1)}, u32[]{:S(2)}, u32[]{:S(2)}) %all-to-all-start.1) | async-done | bytes 688160 | tf_op jit(solution)/shard_map/all_to_all | solution.py:133
  142.5 1.5 shard_map.82
  145.3 1.7 fusion.1
  147.6 2.6 %collective-permute-start.25 = (f16[72,384]{1,0:T(8,128)(2,1)S(1)}, f16[72,384]{1,0:T(8,128)(2,1)S(1)}, u32[]{:S(2)}, u32[]{:S(2)}) collective-permute-start(f16[72,384]{1,0:T(8,128)(2,1)S(1)} %get-tuple-element.61), channel_id=1, source_target_pairs={{0,112},{16,0},{32,16},{48,32},{64,48},{80,64},{96,80},{112,96},{1... | collective-permute-start | bytes 165896 | tf_op jit(solution)/shard_map/ppermute | solution.py:153
  150.2 5.8 %all-to-all-start.2 = ((f16[8,168,512]{2,1,0:T(8,128)(2,1)}), f16[8,168,512]{2,1,0:T(8,128)(2,1)}, u32[]{:S(2)}, u32[]{:S(2)}) async-start(f16[8,168,512]{2,1,0:T(8,128)(2,1)} %fusion.1), calls=%async_computation.2 | async-start | bytes 2752512 | tf_op jit(solution)/shard_map/all_to_all | solution.py:133
  156.0 2.1 %collective-permute-start.24 = (f16[72,384]{1,0:T(8,128)(2,1)S(1)}, f16[72,384]{1,0:T(8,128)(2,1)S(1)}, u32[]{:S(2)}, u32[]{:S(2)}) collective-permute-start(f16[72,384]{1,0:T(8,128)(2,1)S(1)} %get-tuple-element.62), channel_id=1, source_target_pairs={{0,96},{16,112},{32,0},{48,16},{64,32},{80,48},{96,64},{112,80},{1... | collective-permute-start | bytes 165896 | tf_op jit(solution)/shard_map/ppermute | solution.py:153
  159.3 3.3 %collective-permute-start.22 = (f16[72,384]{1,0:T(8,128)(2,1)S(1)}, f16[72,384]{1,0:T(8,128)(2,1)S(1)}, u32[]{:S(2)}, u32[]{:S(2)}) collective-permute-start(f16[72,384]{1,0:T(8,128)(2,1)S(1)} %get-tuple-element.64), channel_id=1, source_target_pairs={{0,64},{16,80},{32,96},{48,112},{64,0},{80,16},{96,32},{112,48},{1... | collective-permute-start | bytes 165896 | tf_op jit(solution)/shard_map/ppermute | solution.py:153
  162.6 3.3 %collective-permute-start.20 = (f16[72,384]{1,0:T(8,128)(2,1)S(1)}, f16[72,384]{1,0:T(8,128)(2,1)S(1)}, u32[]{:S(2)}, u32[]{:S(2)}) collective-permute-start(f16[72,384]{1,0:T(8,128)(2,1)S(1)} %get-tuple-element.66), channel_id=1, source_target_pairs={{0,32},{16,48},{32,64},{48,80},{64,96},{80,112},{96,0},{112,16},{1... | collective-permute-start | bytes 165896 | tf_op jit(solution)/shard_map/ppermute | solution.py:153
  167.5 5.9 %collective-permute-done.21 = f16[72,384]{1,0:T(8,128)(2,1)S(1)} collective-permute-done((f16[72,384]{1,0:T(8,128)(2,1)S(1)}, f16[72,384]{1,0:T(8,128)(2,1)S(1)}, u32[]{:S(2)}, u32[]{:S(2)}) %collective-permute-start.21) | collective-permute-done | bytes 55328 | tf_op jit(solution)/shard_map/ppermute | solution.py:153
  173.4 1.6 collective-permute-done.20
  175.1 2.0 collective-permute-done.19
  178.4 1.7 fusion.95
  180.1 2.4 %collective-permute-start.14 = (bf16[4,160,384]{2,1,0:T(8,128)(2,1)S(1)}, bf16[4,160,384]{2,1,0:T(8,128)(2,1)S(1)}, u32[]{:S(2)}, u32[]{:S(2)}) collective-permute-start(bf16[4,160,384]{2,1,0:T(8,128)(2,1)S(1)} %get-tuple-element.57.refs_0_), channel_id=1, source_target_pairs={{0,8},{8,0},{1,9},{9,1},{2,10},{10,2},{3,11},{11,3},{4,12},{12,4},... | collective-permute-start | bytes 1474568 | tf_op jit(solution)/shard_map/ppermute | solution.py:19
  183.1 1.5 fusion.17
  185.6 2.5 %multiply_reduce_fusion = f32[160,512]{1,0:T(8,128)} fusion(f16[8,168,512]{2,1,0:T(8,128)(2,1)} %all-to-all-done.2, f32[8,512]{1,0:T(8,128)S(1)} %bitcast.196), kind=kLoop, calls=%fused_computation.3 | loop fusion | flops 1884160 | bytes 1654784 | tf_op jit(solution)/shard_map/reduce_sum | solution.py:306
  188.1 1.5 shard_map.83
  189.6 2.2 %convolution_bitcast_fusion = f32[512,384]{0,1:T(8,128)S(1)} fusion(bf16[5120,384]{1,0:T(8,128)(2,1)S(1)} %bitcast.189, bf16[512,5120]{1,0:T(8,128)(2,1)S(1)} %bitcast.222), kind=kOutput, calls=%fused_computation.15 | convolution fusion | flops 2013265920 | bytes 9961472 | tf_op jit(solution)/shard_map/dot_general | solution.py:312
  (196 shorter events, 36.2 us)
Async XLA Ops:
  7.2 52.0 %all-gather.5.cloned.1.call-start = ((), (), s32[]{:S(2)}) async-start(), calls=%async_computation.3 | async-start | bytes 2949120 | tf_op jit(solution)/shard_map/all_gather | solution.py:67
  9.0 4.9 %collective-permute-start.1 = (bf16[320,256]{1,0:T(8,128)(2,1)S(1)}, bf16[320,256]{1,0:T(8,128)(2,1)S(1)}, u32[]{:S(2)}, u32[]{:S(2)}) collective-permute-start(bf16[320,256]{1,0:T(8,128)(2,1)S(1)} %maximum_dynamic-update-slice_fusion), channel_id=1, source_target_pairs={{0,128},{128,0},{1,129},{129,1},{2,130},{130,2},{3,131},{131,3},{4... | collective-permute-start | bytes 491528 | tf_op jit(solution)/shard_map/ppermute | solution.py:19
  15.4 14.2 %copy-start.15 = (f32[160,512]{1,0:T(8,128)S(1)}, f32[160,512]{1,0:T(8,128)}, u32[]{:S(2)}) copy-start(f32[160,512]{1,0:T(8,128)} %param.8) | copy-start | bytes 983044
  25.9 12.9 %collective-permute-start.2 = (bf16[2,8,176,384]{3,2,1,0:T(8,128)(2,1)}, bf16[2,8,176,384]{3,2,1,0:T(8,128)(2,1)S(1)}, u32[]{:S(2)}, u32[]{:S(2)}) collective-permute-start(bf16[2,8,176,384]{3,2,1,0:T(8,128)(2,1)} %get-tuple-element.20), channel_id=1, source_target_pairs={{0,8},{8,0},{1,9},{9,1},{2,10},{10,2},{3,11},{11,3},{4,12},{12,4},... | collective-permute-start | bytes 6488072 | tf_op jit(solution)/shard_map/ppermute | solution.py:19
  31.1 7.6 %collective-permute-start = (f16[168,512]{1,0:T(8,128)(2,1)S(1)}, f16[168,512]{1,0:T(8,128)(2,1)S(1)}, u32[]{:S(2)}, u32[]{:S(2)}) collective-permute-start(f16[168,512]{1,0:T(8,128)(2,1)S(1)} %select_convert_fusion.2), channel_id=1, source_target_pairs={{0,4},{4,0},{1,5},{5,1},{2,6},{6,2},{3,7},{7,3},{8,12},{12,8},{9,1... | collective-permute-start | bytes 516104 | tf_op jit(solution)/shard_map/ppermute | solution.py:19
  42.1 25.3 %collective-permute-start.12 = (f16[8,168,384]{2,1,0:T(8,128)(2,1)}, f16[8,168,384]{2,1,0:T(8,128)(2,1)}, u32[]{:S(2)}, u32[]{:S(2)}) collective-permute-start(f16[8,168,384]{2,1,0:T(8,128)(2,1)} %fusion.3), channel_id=1, source_target_pairs={{0,128},{128,0},{1,129},{129,1},{2,130},{130,2},{3,131},{131,3},{4... | collective-permute-start | bytes 3096584 | tf_op jit(solution)/shard_map/ppermute | solution.py:19
  42.4 20.5 %collective-permute-start.5 = (f16[2,168,512]{2,1,0:T(8,128)(2,1)S(1)}, f16[2,168,512]{2,1,0:T(8,128)(2,1)S(1)}, u32[]{:S(2)}, u32[]{:S(2)}) collective-permute-start(f16[2,168,512]{2,1,0:T(8,128)(2,1)S(1)} %pad_maximum_fusion), channel_id=1, source_target_pairs={{0,2},{1,3},{2,0},{3,1},{4,6},{5,7},{6,4},{7,5},{8,10},{9,11},{10,... | collective-permute-start | bytes 1032200 | tf_op jit(solution)/shard_map/ppermute | solution.py:125
  45.1 17.8 %collective-permute-start.4 = (f16[2,168,512]{2,1,0:T(8,128)(2,1)S(1)}, f16[2,168,512]{2,1,0:T(8,128)(2,1)}, u32[]{:S(2)}, u32[]{:S(2)}) collective-permute-start(f16[2,168,512]{2,1,0:T(8,128)(2,1)S(1)} %pad_maximum_fusion), channel_id=1, source_target_pairs={{0,3},{1,0},{2,1},{3,2},{4,7},{5,4},{6,5},{7,6},{8,11},{9,8},{10,9... | collective-permute-start | bytes 1032200 | tf_op jit(solution)/shard_map/ppermute | solution.py:125
  46.0 17.7 %collective-permute-start.3 = (f16[2,168,512]{2,1,0:T(8,128)(2,1)S(1)}, f16[2,168,512]{2,1,0:T(8,128)(2,1)}, u32[]{:S(2)}, u32[]{:S(2)}) collective-permute-start(f16[2,168,512]{2,1,0:T(8,128)(2,1)S(1)} %pad_maximum_fusion), channel_id=1, source_target_pairs={{0,1},{1,2},{2,3},{3,0},{4,5},{5,6},{6,7},{7,4},{8,9},{9,10},{10,1... | collective-permute-start | bytes 1032200 | tf_op jit(solution)/shard_map/ppermute | solution.py:125
  59.2 18.9 %collective-permute-start.6 = (bf16[16,320,256]{2,1,0:T(8,128)(2,1)}, bf16[16,320,256]{2,1,0:T(8,128)(2,1)S(1)}, u32[]{:S(2)}, u32[]{:S(2)}) collective-permute-start(bf16[16,320,256]{2,1,0:T(8,128)(2,1)} %all-gather.5.cloned.1.call-done.refs_0_), channel_id=1, source_target_pairs={{0,8},{8,0},{1,9},{9,1},{2,10},{10,2},{3,11},{11,3},{4,12},{12,4},... | collective-permute-start | bytes 7864328 | tf_op jit(solution)/shard_map/ppermute | solution.py:19
  72.2 35.1 %all-to-all-start = ((f16[8,168,384]{2,1,0:T(8,128)(2,1)}), f16[8,168,384]{2,1,0:T(8,128)(2,1)}, u32[]{:S(2)}, u32[]{:S(2)}) async-start(f16[8,168,384]{2,1,0:T(8,128)(2,1)} %select_convert_fusion), calls=%async_computation | async-start | bytes 2064384 | tf_op jit(solution)/shard_map/all_to_all | solution.py:295
  78.0 6.1 %copy-start.1 = (f32[160,4096]{1,0:T(8,128)S(1)}, f32[160,4096]{1,0:T(8,128)}, u32[]{:S(2)}) copy-start(f32[160,4096]{1,0:T(8,128)} %copy-done) | copy-start | bytes 7864324
  86.5 5.3 %collective-permute-start.7 = (f16[168,256]{1,0:T(8,128)(2,1)S(1)}, f16[168,256]{1,0:T(8,128)(2,1)S(1)}, u32[]{:S(2)}, u32[]{:S(2)}) collective-permute-start(f16[168,256]{1,0:T(8,128)(2,1)S(1)} %select_convert_fusion.3), channel_id=1, source_target_pairs={{0,4},{4,0},{1,5},{5,1},{2,6},{6,2},{3,7},{7,3},{8,12},{12,8},{9,1... | collective-permute-start | bytes 258056 | tf_op jit(solution)/shard_map/ppermute | solution.py:19
  91.9 6.1 %collective-permute-start.10 = (f16[2,168,256]{2,1,0:T(8,128)(2,1)S(1)}, f16[2,168,256]{2,1,0:T(8,128)(2,1)S(1)}, u32[]{:S(2)}, u32[]{:S(2)}) collective-permute-start(f16[2,168,256]{2,1,0:T(8,128)(2,1)S(1)} %pad_maximum_fusion.3), channel_id=1, source_target_pairs={{0,2},{1,3},{2,0},{3,1},{4,6},{5,7},{6,4},{7,5},{8,10},{9,11},{10,... | collective-permute-start | bytes 516104 | tf_op jit(solution)/shard_map/ppermute | solution.py:125
  94.7 7.8 %collective-permute-start.9 = (f16[2,168,256]{2,1,0:T(8,128)(2,1)S(1)}, f16[2,168,256]{2,1,0:T(8,128)(2,1)S(1)}, u32[]{:S(2)}, u32[]{:S(2)}) collective-permute-start(f16[2,168,256]{2,1,0:T(8,128)(2,1)S(1)} %pad_maximum_fusion.3), channel_id=1, source_target_pairs={{0,3},{1,0},{2,1},{3,2},{4,7},{5,4},{6,5},{7,6},{8,11},{9,8},{10,9... | collective-permute-start | bytes 516104 | tf_op jit(solution)/shard_map/ppermute | solution.py:125
  96.3 7.6 %collective-permute-start.8 = (f16[2,168,256]{2,1,0:T(8,128)(2,1)S(1)}, f16[2,168,256]{2,1,0:T(8,128)(2,1)S(1)}, u32[]{:S(2)}, u32[]{:S(2)}) collective-permute-start(f16[2,168,256]{2,1,0:T(8,128)(2,1)S(1)} %pad_maximum_fusion.3), channel_id=1, source_target_pairs={{0,1},{1,2},{2,3},{3,0},{4,5},{5,6},{6,7},{7,4},{8,9},{9,10},{10,1... | collective-permute-start | bytes 516104 | tf_op jit(solution)/shard_map/ppermute | solution.py:125
  104.7 4.8 %copy-start.13 = (s32[2]{0:T(128)S(1)}, s32[2]{0:T(128)}, u32[]{:S(2)}) copy-start(s32[2]{0:T(128)} %pad_add_fusion.place_ref) | copy-start | bytes 28
  116.5 12.2 %collective-permute-start.13 = (bf16[2,8,80,384]{3,2,1,0:T(8,128)(2,1)}, bf16[2,8,80,384]{3,2,1,0:T(8,128)(2,1)}, u32[]{:S(2)}, u32[]{:S(2)}) collective-permute-start(bf16[2,8,80,384]{3,2,1,0:T(8,128)(2,1)} %get-tuple-element.28), channel_id=1, source_target_pairs={{0,8},{8,0},{1,9},{9,1},{2,10},{10,2},{3,11},{11,3},{4,12},{12,4},... | collective-permute-start | bytes 2949128 | tf_op jit(solution)/shard_map/ppermute | solution.py:19
  118.1 8.8 %collective-permute-start.11 = (bf16[160,384]{1,0:T(8,128)(2,1)S(1)}, bf16[160,384]{1,0:T(8,128)(2,1)}, u32[]{:S(2)}, u32[]{:S(2)}) collective-permute-start(bf16[160,384]{1,0:T(8,128)(2,1)S(1)} %convolution_convert_fusion), channel_id=1, source_target_pairs={{0,128},{128,0},{1,129},{129,1},{2,130},{130,2},{3,131},{131,3},{4... | collective-permute-start | bytes 368648 | tf_op jit(solution)/shard_map/ppermute | solution.py:19
  120.2 8.4 %copy-start.10 = (f32[8,80,384]{2,1,0:T(8,128)S(1)}, f32[8,80,384]{2,1,0:T(8,128)}, u32[]{:S(2)}) copy-start(f32[8,80,384]{2,1,0:T(8,128)} %copy-done.9) | copy-start | bytes 2949124
  121.3 19.2 %all-to-all-start.1 = ((f16[8,168,256]{2,1,0:T(8,128)(2,1)}), f16[8,168,256]{2,1,0:T(8,128)(2,1)}, u32[]{:S(2)}, u32[]{:S(2)}) async-start(f16[8,168,256]{2,1,0:T(8,128)(2,1)} %fusion.5), calls=%async_computation.1 | async-start | bytes 1376256 | tf_op jit(solution)/shard_map/all_to_all | solution.py:133
  126.9 51.5 %all-gather.7.cloned.1.call-start = ((), (), s32[]{:S(2)}) async-start(), calls=%async_computation.4 | async-start | bytes 2211840 | tf_op jit(solution)/shard_map/all_gather | solution.py:67
  128.6 13.9 %copy-start.3 = (bf16[32,128,256]{2,1,0:T(8,128)(2,1)S(1)}, bf16[32,128,256]{2,1,0:T(8,128)(2,1)}, u32[]{:S(2)}) copy-start(bf16[32,128,256]{2,1,0:T(8,128)(2,1)} %copy-done.2) | copy-start | bytes 6291460
  130.2 16.7 %collective-permute-start.18 = (f16[8,72,384]{2,1,0:T(8,128)(2,1)S(1)}, f16[8,72,384]{2,1,0:T(8,128)(2,1)S(1)}, u32[]{:S(2)}, u32[]{:S(2)}) collective-permute-start(f16[8,72,384]{2,1,0:T(8,128)(2,1)S(1)} %fusion.7), channel_id=1, source_target_pairs={{0,128},{128,0},{1,129},{129,1},{2,130},{130,2},{3,131},{131,3},{4... | collective-permute-start | bytes 1327112 | tf_op jit(solution)/shard_map/ppermute | solution.py:19
  147.5 29.6 %copy-start.17 = (f16[8,72,384]{2,1,0:T(8,128)(2,1)}, f16[8,72,384]{2,1,0:T(8,128)(2,1)S(1)}, u32[]{:S(2)}) copy-start(f16[8,72,384]{2,1,0:T(8,128)(2,1)S(1)} %select_convert_fusion.1) | copy-start | bytes 1327108
  147.6 15.0 %collective-permute-start.25 = (f16[72,384]{1,0:T(8,128)(2,1)S(1)}, f16[72,384]{1,0:T(8,128)(2,1)S(1)}, u32[]{:S(2)}, u32[]{:S(2)}) collective-permute-start(f16[72,384]{1,0:T(8,128)(2,1)S(1)} %get-tuple-element.61), channel_id=1, source_target_pairs={{0,112},{16,0},{32,16},{48,32},{64,48},{80,64},{96,80},{112,96},{1... | collective-permute-start | bytes 165896 | tf_op jit(solution)/shard_map/ppermute | solution.py:153
  150.2 34.5 %all-to-all-start.2 = ((f16[8,168,512]{2,1,0:T(8,128)(2,1)}), f16[8,168,512]{2,1,0:T(8,128)(2,1)}, u32[]{:S(2)}, u32[]{:S(2)}) async-start(f16[8,168,512]{2,1,0:T(8,128)(2,1)} %fusion.1), calls=%async_computation.2 | async-start | bytes 2752512 | tf_op jit(solution)/shard_map/all_to_all | solution.py:133
  156.0 10.0 %collective-permute-start.24 = (f16[72,384]{1,0:T(8,128)(2,1)S(1)}, f16[72,384]{1,0:T(8,128)(2,1)S(1)}, u32[]{:S(2)}, u32[]{:S(2)}) collective-permute-start(f16[72,384]{1,0:T(8,128)(2,1)S(1)} %get-tuple-element.62), channel_id=1, source_target_pairs={{0,96},{16,112},{32,0},{48,16},{64,32},{80,48},{96,64},{112,80},{1... | collective-permute-start | bytes 165896 | tf_op jit(solution)/shard_map/ppermute | solution.py:153
  158.1 9.2 %collective-permute-start.23 = (f16[72,384]{1,0:T(8,128)(2,1)S(1)}, f16[72,384]{1,0:T(8,128)(2,1)S(1)}, u32[]{:S(2)}, u32[]{:S(2)}) collective-permute-start(f16[72,384]{1,0:T(8,128)(2,1)S(1)} %get-tuple-element.63), channel_id=1, source_target_pairs={{0,80},{16,96},{32,112},{48,0},{64,16},{80,32},{96,48},{112,64},{1... | collective-permute-start | bytes 165896 | tf_op jit(solution)/shard_map/ppermute | solution.py:153
  159.3 8.2 %collective-permute-start.22 = (f16[72,384]{1,0:T(8,128)(2,1)S(1)}, f16[72,384]{1,0:T(8,128)(2,1)S(1)}, u32[]{:S(2)}, u32[]{:S(2)}) collective-permute-start(f16[72,384]{1,0:T(8,128)(2,1)S(1)} %get-tuple-element.64), channel_id=1, source_target_pairs={{0,64},{16,80},{32,96},{48,112},{64,0},{80,16},{96,32},{112,48},{1... | collective-permute-start | bytes 165896 | tf_op jit(solution)/shard_map/ppermute | solution.py:153
  162.6 10.8 %collective-permute-start.21 = (f16[72,384]{1,0:T(8,128)(2,1)S(1)}, f16[72,384]{1,0:T(8,128)(2,1)S(1)}, u32[]{:S(2)}, u32[]{:S(2)}) collective-permute-start(f16[72,384]{1,0:T(8,128)(2,1)S(1)} %get-tuple-element.65), channel_id=1, source_target_pairs={{0,48},{16,64},{32,80},{48,96},{64,112},{80,0},{96,16},{112,32},{1... | collective-permute-start | bytes 165896 | tf_op jit(solution)/shard_map/ppermute | solution.py:153
  162.6 12.4 %collective-permute-start.20 = (f16[72,384]{1,0:T(8,128)(2,1)S(1)}, f16[72,384]{1,0:T(8,128)(2,1)S(1)}, u32[]{:S(2)}, u32[]{:S(2)}) collective-permute-start(f16[72,384]{1,0:T(8,128)(2,1)S(1)} %get-tuple-element.66), channel_id=1, source_target_pairs={{0,32},{16,48},{32,64},{48,80},{64,96},{80,112},{96,0},{112,16},{1... | collective-permute-start | bytes 165896 | tf_op jit(solution)/shard_map/ppermute | solution.py:153
  166.0 11.1 %copy-start.18 = (f16[72,384]{1,0:T(8,128)(2,1)}, f16[72,384]{1,0:T(8,128)(2,1)S(1)}, u32[]{:S(2)}) copy-start(f16[72,384]{1,0:T(8,128)(2,1)S(1)} %collective-permute-done.24) | copy-start | bytes 165892
  166.0 11.0 %collective-permute-start.19 = (f16[72,384]{1,0:T(8,128)(2,1)S(1)}, f16[72,384]{1,0:T(8,128)(2,1)S(1)}, u32[]{:S(2)}, u32[]{:S(2)}) collective-permute-start(f16[72,384]{1,0:T(8,128)(2,1)S(1)} %get-tuple-element.60), channel_id=1, source_target_pairs={{0,16},{16,32},{32,48},{48,64},{64,80},{80,96},{96,112},{112,0},{1... | collective-permute-start | bytes 165896 | tf_op jit(solution)/shard_map/ppermute | solution.py:153
  167.3 9.8 %copy-start.20 = (f16[72,384]{1,0:T(8,128)(2,1)}, f16[72,384]{1,0:T(8,128)(2,1)S(1)}, u32[]{:S(2)}) copy-start(f16[72,384]{1,0:T(8,128)(2,1)S(1)} %collective-permute-done.23) | copy-start | bytes 165892
  167.5 9.6 %copy-start.22 = (f16[72,384]{1,0:T(8,128)(2,1)}, f16[72,384]{1,0:T(8,128)(2,1)S(1)}, u32[]{:S(2)}) copy-start(f16[72,384]{1,0:T(8,128)(2,1)S(1)} %collective-permute-done.22) | copy-start | bytes 165892
  173.4 3.7 %copy-start.24 = (f16[72,384]{1,0:T(8,128)(2,1)}, f16[72,384]{1,0:T(8,128)(2,1)S(1)}, u32[]{:S(2)}) copy-start(f16[72,384]{1,0:T(8,128)(2,1)S(1)} %collective-permute-done.21) | copy-start | bytes 165892
  178.3 4.8 %copy-start.19 = (f16[72,384]{1,0:T(8,128)(2,1)S(1)}, f16[72,384]{1,0:T(8,128)(2,1)}, u32[]{:S(2)}) copy-start(f16[72,384]{1,0:T(8,128)(2,1)} %copy-done.18) | copy-start | bytes 165892
  178.3 4.8 %copy-start.21 = (f16[72,384]{1,0:T(8,128)(2,1)S(1)}, f16[72,384]{1,0:T(8,128)(2,1)}, u32[]{:S(2)}) copy-start(f16[72,384]{1,0:T(8,128)(2,1)} %copy-done.20) | copy-start | bytes 165892
  178.3 4.8 %copy-start.23 = (f16[72,384]{1,0:T(8,128)(2,1)S(1)}, f16[72,384]{1,0:T(8,128)(2,1)}, u32[]{:S(2)}) copy-start(f16[72,384]{1,0:T(8,128)(2,1)} %copy-done.22) | copy-start | bytes 165892
  178.4 4.8 %copy-start.25 = (f16[72,384]{1,0:T(8,128)(2,1)S(1)}, f16[72,384]{1,0:T(8,128)(2,1)}, u32[]{:S(2)}) copy-start(f16[72,384]{1,0:T(8,128)(2,1)} %copy-done.24) | copy-start | bytes 165892
  178.4 4.8 %copy-start.27 = (f16[72,384]{1,0:T(8,128)(2,1)S(1)}, f16[72,384]{1,0:T(8,128)(2,1)}, u32[]{:S(2)}) copy-start(f16[72,384]{1,0:T(8,128)(2,1)} %copy-done.26) | copy-start | bytes 165892
  178.4 4.8 %copy-start.29 = (f16[72,384]{1,0:T(8,128)(2,1)S(1)}, f16[72,384]{1,0:T(8,128)(2,1)}, u32[]{:S(2)}) copy-start(f16[72,384]{1,0:T(8,128)(2,1)} %copy-done.28) | copy-start | bytes 165892
  180.1 8.0 %collective-permute-start.14 = (bf16[4,160,384]{2,1,0:T(8,128)(2,1)S(1)}, bf16[4,160,384]{2,1,0:T(8,128)(2,1)S(1)}, u32[]{:S(2)}, u32[]{:S(2)}) collective-permute-start(bf16[4,160,384]{2,1,0:T(8,128)(2,1)S(1)} %get-tuple-element.57.refs_0_), channel_id=1, source_target_pairs={{0,8},{8,0},{1,9},{9,1},{2,10},{10,2},{3,11},{11,3},{4,12},{12,4},... | collective-permute-start | bytes 1474568 | tf_op jit(solution)/shard_map/ppermute | solution.py:19
  182.5 5.6 %collective-permute-start.15 = (bf16[4,160,384]{2,1,0:T(8,128)(2,1)S(1)}, bf16[4,160,384]{2,1,0:T(8,128)(2,1)S(1)}, u32[]{:S(2)}, u32[]{:S(2)}) collective-permute-start(bf16[4,160,384]{2,1,0:T(8,128)(2,1)S(1)} %get-tuple-element.56.refs_1_), channel_id=1, source_target_pairs={{0,8},{8,0},{1,9},{9,1},{2,10},{10,2},{3,11},{11,3},{4,12},{12,4},... | collective-permute-start | bytes 1474568 | tf_op jit(solution)/shard_map/ppermute | solution.py:19
  182.6 5.5 %collective-permute-start.16 = (bf16[4,160,384]{2,1,0:T(8,128)(2,1)S(1)}, bf16[4,160,384]{2,1,0:T(8,128)(2,1)S(1)}, u32[]{:S(2)}, u32[]{:S(2)}) collective-permute-start(bf16[4,160,384]{2,1,0:T(8,128)(2,1)S(1)} %get-tuple-element.55.refs_2_), channel_id=1, source_target_pairs={{0,8},{8,0},{1,9},{9,1},{2,10},{10,2},{3,11},{11,3},{4,12},{12,4},... | collective-permute-start | bytes 1474568 | tf_op jit(solution)/shard_map/ppermute | solution.py:19
  183.0 5.1 %collective-permute-start.17 = (bf16[4,160,384]{2,1,0:T(8,128)(2,1)S(1)}, bf16[4,160,384]{2,1,0:T(8,128)(2,1)}, u32[]{:S(2)}, u32[]{:S(2)}) collective-permute-start(bf16[4,160,384]{2,1,0:T(8,128)(2,1)S(1)} %get-tuple-element.54.refs_3_), channel_id=1, source_target_pairs={{0,8},{8,0},{1,9},{9,1},{2,10},{10,2},{3,11},{11,3},{4,12},{12,4},... | collective-permute-start | bytes 1474568 | tf_op jit(solution)/shard_map/ppermute | solution.py:19
  185.6 4.0 %slice-start = ((s8[5242880]{0:T(1024)(128)(4,1)}), s8[4194304]{0:T(1024)(128)(4,1)S(1)}, s32[]{:S(2)}) async-start(s8[5242880]{0:T(1024)(128)(4,1)} %bitcast.221), calls=%async_computation.5 | async-start | bytes 8388608
  (15 other events, 25.4 us)
Sparse Core Ops, SparseCore 0:
  14.9 44.2 all-gather.4
  130.1 48.2 all-gather.6

commit v4 on v3

--- a/solution.py
+++ b/solution.py
@@ -298,7 +298,7 @@
     student_two = pair_y(student, yl)
     student_own = gather_z(student_two)
 
-    grad = jnp.sum(dec(after(blocks, student)), axis=0)
+    grad = jnp.sum(dec(after(blocks, student_two)), axis=0)
     sent, own = sum_mates(*share_parts(yl, c, expanded, grad))
     side = swap_col(payload(blocks_of(grad, heads)))
     side = jnp.sum(dec(after(side, sent, student_two)), axis=0)

time: 201 us -> 201 us (level)
  waiting for transfers between devices: 49.8 us -> 52.2 us
    ppermute x13, waiting for transfers between devices: 10.7 us -> 14.4 us  [swap(): return lax.ppermute(a, axis, [(0, 1), (1, 0)])]
    ppermute x7, waiting for transfers between devices: 9.61 us -> 6.84 us  [parts_z(): got.append(lax.ppermute(block, 'z', [(i, (i + d) % 8) for i in range(8)]))]
    all_to_all x2, waiting for transfers between devices: 9.84 us -> 12 us  [swap_col(): return lax.all_to_all(blocks, COL, 0, 0, tiled=True)]
  transfers between devices with their start and end apart: 31 -> 31, of which waited for: 13 -> 12; matrix products, arithmetic and copies ran while one was open for 17% -> 17% of each run, Pallas kernels for 8% -> 8%
where the time goes in v4:
time: 201 us; the launch traced here: 199 us
  starting transfers between devices  58.3 us (29%)
  waiting for transfers between devices  52.2 us (26%)
  other arithmetic  30.4 us (15%)
  Pallas kernels  21 us (10%)
  between operations  16.5 us (8%)
  local copies, waits for them, and re-layouts  15.6 us (8%)
  matrix products  5.15 us (3%)
    ppermute x13, starting transfers between devices, swap(): return lax.ppermute(a, axis, [(0, 1), (1, 0)])  19.2 us
    ppermute x13, waiting for transfers between devices, swap(): return lax.ppermute(a, axis, [(0, 1), (1, 0)])  14.4 us
    ppermute x7, starting transfers between devices, parts_z(): got.append(lax.ppermute(block, 'z', [(i, (i + d) % 8) for i in range(8)]))  13.9 us
    all_to_all x2, waiting for transfers between devices, swap_col(): return lax.all_to_all(blocks, COL, 0, 0, tiled=True)  12 us
    all_gather x2, waiting for transfers between devices, gather_z(): return lax.all_gather(two, 'z').reshape((16,) + two.shape[1:])  11.4 us
    unnamed x95, local copies, waits for them, and re-layouts  11.3 us
    all_to_all x2, starting transfers between devices, swap_col(): return lax.all_to_all(blocks, COL, 0, 0, tiled=True)  10.6 us
    pallas_call x1, Pallas kernels, weight_parts(): pl.pallas_call(weight_kernel, grid_spec=pltpu.PrefetchScalarGridSpec(num_...  10.5 us
  transfers between devices with their start and end apart: 31, of which 12 were waited for; matrix products, arithmetic and copies ran while one was open for 17% of the time, Pallas kernels for 8%

profile of v4, /device:TPU:1, one launch (start us, length us, event | category | flops | bytes accessed | tf_op | source)
XLA Modules:
  0.0 199.2 jit_solution(9164746516714421471)
XLA Ops:
  9.0 2.2 %collective-permute-start.1 = (bf16[320,256]{1,0:T(8,128)(2,1)S(1)}, bf16[320,256]{1,0:T(8,128)(2,1)S(1)}, u32[]{:S(2)}, u32[]{:S(2)}) collective-permute-start(bf16[320,256]{1,0:T(8,128)(2,1)S(1)} %maximum_dynamic-update-slice_fusion), channel_id=1, source_target_pairs={{0,128},{128,0},{1,129},{129,1},{2,130},{130,2},{3,131},{131,3},{4... | collective-permute-start | bytes 491528 | tf_op jit(solution)/shard_map/ppermute | solution.py:19
  11.2 2.7 %collective-permute-done.1 = bf16[320,256]{1,0:T(8,128)(2,1)S(1)} collective-permute-done((bf16[320,256]{1,0:T(8,128)(2,1)S(1)}, bf16[320,256]{1,0:T(8,128)(2,1)S(1)}, u32[]{:S(2)}, u32[]{:S(2)}) %collective-permute-start.1) | collective-permute-done | bytes 163872 | tf_op jit(solution)/shard_map/ppermute | solution.py:19
  15.4 10.5 %shard_map.76 = (f32[8,176,384]{2,1,0:T(8,128)}, f32[8,176,384]{2,1,0:T(8,128)}, bf16[2,8,176,384]{3,2,1,0:T(8,128)(2,1)}) custom-call(s32[2]{0:T(128)} %pad_add_fusion.place_ref, bf16[512,5120]{1,0:T(8,128)(2,1)} %tokens_ref, bf16[512,384]{1,0:T(8,128)(2,1)} %cotangent_ref.1), custom_call_target="tpu_custom_call" | custom-call | flops 2013265920 | bytes 12582912 | tf_op jit(solution)/shard_map/pallas_call | solution.py:194
  25.9 3.7 %collective-permute-start.2 = (bf16[2,8,176,384]{3,2,1,0:T(8,128)(2,1)}, bf16[2,8,176,384]{3,2,1,0:T(8,128)(2,1)S(1)}, u32[]{:S(2)}, u32[]{:S(2)}) collective-permute-start(bf16[2,8,176,384]{3,2,1,0:T(8,128)(2,1)} %get-tuple-element.20), channel_id=1, source_target_pairs={{0,8},{8,0},{1,9},{9,1},{2,10},{10,2},{3,11},{11,3},{4,12},{12,4},... | collective-permute-start | bytes 6488072 | tf_op jit(solution)/shard_map/ppermute | solution.py:19
  31.1 1.9 collective-permute-start
  33.3 5.4 %collective-permute-done = f16[168,512]{1,0:T(8,128)(2,1)S(1)} collective-permute-done((f16[168,512]{1,0:T(8,128)(2,1)S(1)}, f16[168,512]{1,0:T(8,128)(2,1)S(1)}, u32[]{:S(2)}, u32[]{:S(2)}) %collective-permute-start) | collective-permute-done | bytes 172064 | tf_op jit(solution)/shard_map/ppermute | solution.py:19
  38.8 1.9 convert_add_fusion
  42.4 2.7 %collective-permute-start.5 = (f16[2,168,512]{2,1,0:T(8,128)(2,1)S(1)}, f16[2,168,512]{2,1,0:T(8,128)(2,1)S(1)}, u32[]{:S(2)}, u32[]{:S(2)}) collective-permute-start(f16[2,168,512]{2,1,0:T(8,128)(2,1)S(1)} %pad_maximum_fusion), channel_id=1, source_target_pairs={{0,2},{1,3},{2,0},{3,1},{4,6},{5,7},{6,4},{7,5},{8,10},{9,11},{10,... | collective-permute-start | bytes 1032200 | tf_op jit(solution)/shard_map/ppermute | solution.py:125
  47.8 11.4 %all-gather.5.cloned.1.call-done.refs_0_ = bf16[16,320,256]{2,1,0:T(8,128)(2,1)} async-done(((bf16[2,320,256]{2,1,0:T(8,128)(2,1)}), bf16[16,320,256]{2,1,0:T(8,128)(2,1)}) %all-gather.5.cloned.1.call-update) | async-done | bytes 2621456 | tf_op jit(solution)/shard_map/all_gather | solution.py:67
  59.2 3.6 %collective-permute-start.6 = (bf16[16,320,256]{2,1,0:T(8,128)(2,1)}, bf16[16,320,256]{2,1,0:T(8,128)(2,1)S(1)}, u32[]{:S(2)}, u32[]{:S(2)}) collective-permute-start(bf16[16,320,256]{2,1,0:T(8,128)(2,1)} %all-gather.5.cloned.1.call-done.refs_0_), channel_id=1, source_target_pairs={{0,8},{8,0},{1,9},{9,1},{2,10},{10,2},{3,11},{11,3},{4,12},{12,4},... | collective-permute-start | bytes 7864328 | tf_op jit(solution)/shard_map/ppermute | solution.py:19
  67.4 1.7 multiply_exponential_fusion.8
  69.1 1.7 select_add_fusion
  70.9 1.3 select_convert_fusion
  72.2 5.9 %all-to-all-start = ((f16[8,168,384]{2,1,0:T(8,128)(2,1)}), f16[8,168,384]{2,1,0:T(8,128)(2,1)}, u32[]{:S(2)}, u32[]{:S(2)}) async-start(f16[8,168,384]{2,1,0:T(8,128)(2,1)} %select_convert_fusion), calls=%async_computation | async-start | bytes 2064384 | tf_op jit(solution)/shard_map/all_to_all | solution.py:295
  78.1 1.5 copy-done.7
  79.6 1.9 copy-done.6
  81.6 1.7 copy-done.8
  84.2 1.5 abs_reduce_fusion.1
  86.5 2.6 %collective-permute-start.7 = (f16[168,256]{1,0:T(8,128)(2,1)S(1)}, f16[168,256]{1,0:T(8,128)(2,1)S(1)}, u32[]{:S(2)}, u32[]{:S(2)}) collective-permute-start(f16[168,256]{1,0:T(8,128)(2,1)S(1)} %select_convert_fusion.3), channel_id=1, source_target_pairs={{0,4},{4,0},{1,5},{5,1},{2,6},{6,2},{3,7},{7,3},{8,12},{12,8},{9,1... | collective-permute-start | bytes 258056 | tf_op jit(solution)/shard_map/ppermute | solution.py:19
  89.2 2.6 %collective-permute-done.7 = f16[168,256]{1,0:T(8,128)(2,1)S(1)} collective-permute-done((f16[168,256]{1,0:T(8,128)(2,1)S(1)}, f16[168,256]{1,0:T(8,128)(2,1)S(1)}, u32[]{:S(2)}, u32[]{:S(2)}) %collective-permute-start.7) | collective-permute-done | bytes 86048 | tf_op jit(solution)/shard_map/ppermute | solution.py:19
  91.9 2.8 %collective-permute-start.10 = (f16[2,168,256]{2,1,0:T(8,128)(2,1)S(1)}, f16[2,168,256]{2,1,0:T(8,128)(2,1)S(1)}, u32[]{:S(2)}, u32[]{:S(2)}) collective-permute-start(f16[2,168,256]{2,1,0:T(8,128)(2,1)S(1)} %pad_maximum_fusion.3), channel_id=1, source_target_pairs={{0,2},{1,3},{2,0},{3,1},{4,6},{5,7},{6,4},{7,5},{8,10},{9,11},{10,... | collective-permute-start | bytes 516104 | tf_op jit(solution)/shard_map/ppermute | solution.py:125
  94.7 1.6 collective-permute-start.9
  96.4 1.6 collective-permute-done.10
  98.0 4.5 %collective-permute-done.9 = f16[2,168,256]{2,1,0:T(8,128)(2,1)S(1)} collective-permute-done((f16[2,168,256]{2,1,0:T(8,128)(2,1)S(1)}, f16[2,168,256]{2,1,0:T(8,128)(2,1)S(1)}, u32[]{:S(2)}, u32[]{:S(2)}) %collective-permute-start.9) | collective-permute-done | bytes 172064 | tf_op jit(solution)/shard_map/ppermute | solution.py:125
  102.5 1.4 collective-permute-done.8
  104.7 1.5 convolution_convert_fusion
  106.3 3.7 %collective-permute-done.11 = bf16[160,384]{1,0:T(8,128)(2,1)S(1)} collective-permute-done((bf16[160,384]{1,0:T(8,128)(2,1)S(1)}, bf16[160,384]{1,0:T(8,128)(2,1)S(1)}, u32[]{:S(2)}, u32[]{:S(2)}) %collective-permute-start.11) | collective-permute-done | bytes 122912 | tf_op jit(solution)/shard_map/ppermute | solution.py:19
  111.7 1.4 multiply_reduce_fusion.1.a_ref.grad_ref
  114.4 3.6 %shard_map.81 = (f32[8,80,384]{2,1,0:T(8,128)S(1)}, f32[8,80,384]{2,1,0:T(8,128)S(1)}, bf16[2,8,80,384]{3,2,1,0:T(8,128)(2,1)}) custom-call(s32[2]{0:T(128)S(1)} %copy-done.13, f32[160,2048]{1,0:T(8,128)S(1)} %copy-done.5, f32[160,384]{1,0:T(8,128)S(1)} %multiply_reduce_fusion.1.a_ref.grad_ref), custom_call_target="tpu_custom_call" | custom-call | flops 754974720 | bytes 6291456 | tf_op jit(solution)/shard_map/pallas_call | solution.py:237
  120.0 2.8 %collective-permute-start.13 = (bf16[2,8,80,384]{3,2,1,0:T(8,128)(2,1)}, bf16[2,8,80,384]{3,2,1,0:T(8,128)(2,1)}, u32[]{:S(2)}, u32[]{:S(2)}) collective-permute-start(bf16[2,8,80,384]{3,2,1,0:T(8,128)(2,1)} %get-tuple-element.28), channel_id=1, source_target_pairs={{0,8},{8,0},{1,9},{9,1},{2,10},{10,2},{3,11},{11,3},{4,12},{12,4},... | collective-permute-start | bytes 2949128 | tf_op jit(solution)/shard_map/ppermute | solution.py:19
  122.9 1.7 shard_map.80
  125.7 5.2 %all-to-all-start.1 = ((f16[8,168,256]{2,1,0:T(8,128)(2,1)}), f16[8,168,256]{2,1,0:T(8,128)(2,1)}, u32[]{:S(2)}, u32[]{:S(2)}) async-start(f16[8,168,256]{2,1,0:T(8,128)(2,1)} %fusion.5), calls=%async_computation.1 | async-start | bytes 1376256 | tf_op jit(solution)/shard_map/all_to_all | solution.py:133
  132.6 12.0 %all-to-all-done.1 = f16[8,168,256]{2,1,0:T(8,128)(2,1)} async-done(((f16[8,168,256]{2,1,0:T(8,128)(2,1)}), f16[8,168,256]{2,1,0:T(8,128)(2,1)}, u32[]{:S(2)}, u32[]{:S(2)}) %all-to-all-start.1) | async-done | bytes 688160 | tf_op jit(solution)/shard_map/all_to_all | solution.py:133
  146.6 1.5 shard_map.82
  149.3 1.6 fusion.1
  151.7 2.7 %collective-permute-start.25 = (f16[72,384]{1,0:T(8,128)(2,1)S(1)}, f16[72,384]{1,0:T(8,128)(2,1)S(1)}, u32[]{:S(2)}, u32[]{:S(2)}) collective-permute-start(f16[72,384]{1,0:T(8,128)(2,1)S(1)} %get-tuple-element.61), channel_id=1, source_target_pairs={{0,112},{16,0},{32,16},{48,32},{64,48},{80,64},{96,80},{112,96},{1... | collective-permute-start | bytes 165896 | tf_op jit(solution)/shard_map/ppermute | solution.py:153
  154.4 5.5 %all-to-all-start.2 = ((f16[8,168,512]{2,1,0:T(8,128)(2,1)}), f16[8,168,512]{2,1,0:T(8,128)(2,1)}, u32[]{:S(2)}, u32[]{:S(2)}) async-start(f16[8,168,512]{2,1,0:T(8,128)(2,1)} %fusion.1), calls=%async_computation.2 | async-start | bytes 2752512 | tf_op jit(solution)/shard_map/all_to_all | solution.py:133
  159.8 2.1 %collective-permute-start.24 = (f16[72,384]{1,0:T(8,128)(2,1)S(1)}, f16[72,384]{1,0:T(8,128)(2,1)S(1)}, u32[]{:S(2)}, u32[]{:S(2)}) collective-permute-start(f16[72,384]{1,0:T(8,128)(2,1)S(1)} %get-tuple-element.62), channel_id=1, source_target_pairs={{0,96},{16,112},{32,0},{48,16},{64,32},{80,48},{96,64},{112,80},{1... | collective-permute-start | bytes 165896 | tf_op jit(solution)/shard_map/ppermute | solution.py:153
  163.1 3.3 %collective-permute-start.22 = (f16[72,384]{1,0:T(8,128)(2,1)S(1)}, f16[72,384]{1,0:T(8,128)(2,1)S(1)}, u32[]{:S(2)}, u32[]{:S(2)}) collective-permute-start(f16[72,384]{1,0:T(8,128)(2,1)S(1)} %get-tuple-element.64), channel_id=1, source_target_pairs={{0,64},{16,80},{32,96},{48,112},{64,0},{80,16},{96,32},{112,48},{1... | collective-permute-start | bytes 165896 | tf_op jit(solution)/shard_map/ppermute | solution.py:153
  166.5 3.3 %collective-permute-start.20 = (f16[72,384]{1,0:T(8,128)(2,1)S(1)}, f16[72,384]{1,0:T(8,128)(2,1)S(1)}, u32[]{:S(2)}, u32[]{:S(2)}) collective-permute-start(f16[72,384]{1,0:T(8,128)(2,1)S(1)} %get-tuple-element.66), channel_id=1, source_target_pairs={{0,32},{16,48},{32,64},{48,80},{64,96},{80,112},{96,0},{112,16},{1... | collective-permute-start | bytes 165896 | tf_op jit(solution)/shard_map/ppermute | solution.py:153
  171.2 3.5 %collective-permute-done.21 = f16[72,384]{1,0:T(8,128)(2,1)S(1)} collective-permute-done((f16[72,384]{1,0:T(8,128)(2,1)S(1)}, f16[72,384]{1,0:T(8,128)(2,1)S(1)}, u32[]{:S(2)}, u32[]{:S(2)}) %collective-permute-start.21) | collective-permute-done | bytes 55328 | tf_op jit(solution)/shard_map/ppermute | solution.py:153
  176.1 2.0 %collective-permute-done.19 = f16[72,384]{1,0:T(8,128)(2,1)S(1)} collective-permute-done((f16[72,384]{1,0:T(8,128)(2,1)S(1)}, f16[72,384]{1,0:T(8,128)(2,1)S(1)}, u32[]{:S(2)}, u32[]{:S(2)}) %collective-permute-start.19) | collective-permute-done | bytes 55328 | tf_op jit(solution)/shard_map/ppermute | solution.py:153
  178.8 1.7 fusion.95
  180.5 1.3 collective-permute-start.14
  182.5 1.5 fusion.17
  184.9 2.5 %multiply_reduce_fusion = f32[160,512]{1,0:T(8,128)} fusion(f16[8,168,512]{2,1,0:T(8,128)(2,1)} %all-to-all-done.2, f32[8,512]{1,0:T(8,128)S(1)} %bitcast.196), kind=kLoop, calls=%fused_computation.3 | loop fusion | flops 1884160 | bytes 1654784 | tf_op jit(solution)/shard_map/reduce_sum | solution.py:306
  187.4 1.5 shard_map.83
  188.9 2.2 %convolution_bitcast_fusion = f32[512,384]{0,1:T(8,128)S(1)} fusion(bf16[5120,384]{1,0:T(8,128)(2,1)S(1)} %bitcast.189, bf16[512,5120]{1,0:T(8,128)(2,1)S(1)} %bitcast.222), kind=kOutput, calls=%fused_computation.15 | convolution fusion | flops 2013265920 | bytes 9961472 | tf_op jit(solution)/shard_map/dot_general | solution.py:312
  (196 shorter events, 34.1 us)
Async XLA Ops:
  7.2 52.0 %all-gather.5.cloned.1.call-start = ((), (), s32[]{:S(2)}) async-start(), calls=%async_computation.3 | async-start | bytes 2949120 | tf_op jit(solution)/shard_map/all_gather | solution.py:67
  9.0 4.9 %collective-permute-start.1 = (bf16[320,256]{1,0:T(8,128)(2,1)S(1)}, bf16[320,256]{1,0:T(8,128)(2,1)S(1)}, u32[]{:S(2)}, u32[]{:S(2)}) collective-permute-start(bf16[320,256]{1,0:T(8,128)(2,1)S(1)} %maximum_dynamic-update-slice_fusion), channel_id=1, source_target_pairs={{0,128},{128,0},{1,129},{129,1},{2,130},{130,2},{3,131},{131,3},{4... | collective-permute-start | bytes 491528 | tf_op jit(solution)/shard_map/ppermute | solution.py:19
  15.4 14.2 %copy-start.15 = (f32[160,512]{1,0:T(8,128)S(1)}, f32[160,512]{1,0:T(8,128)}, u32[]{:S(2)}) copy-start(f32[160,512]{1,0:T(8,128)} %param.8) | copy-start | bytes 983044
  25.9 12.9 %collective-permute-start.2 = (bf16[2,8,176,384]{3,2,1,0:T(8,128)(2,1)}, bf16[2,8,176,384]{3,2,1,0:T(8,128)(2,1)S(1)}, u32[]{:S(2)}, u32[]{:S(2)}) collective-permute-start(bf16[2,8,176,384]{3,2,1,0:T(8,128)(2,1)} %get-tuple-element.20), channel_id=1, source_target_pairs={{0,8},{8,0},{1,9},{9,1},{2,10},{10,2},{3,11},{11,3},{4,12},{12,4},... | collective-permute-start | bytes 6488072 | tf_op jit(solution)/shard_map/ppermute | solution.py:19
  31.1 7.6 %collective-permute-start = (f16[168,512]{1,0:T(8,128)(2,1)S(1)}, f16[168,512]{1,0:T(8,128)(2,1)S(1)}, u32[]{:S(2)}, u32[]{:S(2)}) collective-permute-start(f16[168,512]{1,0:T(8,128)(2,1)S(1)} %select_convert_fusion.2), channel_id=1, source_target_pairs={{0,4},{4,0},{1,5},{5,1},{2,6},{6,2},{3,7},{7,3},{8,12},{12,8},{9,1... | collective-permute-start | bytes 516104 | tf_op jit(solution)/shard_map/ppermute | solution.py:19
  42.1 25.3 %collective-permute-start.12 = (f16[8,168,384]{2,1,0:T(8,128)(2,1)}, f16[8,168,384]{2,1,0:T(8,128)(2,1)}, u32[]{:S(2)}, u32[]{:S(2)}) collective-permute-start(f16[8,168,384]{2,1,0:T(8,128)(2,1)} %fusion.3), channel_id=1, source_target_pairs={{0,128},{128,0},{1,129},{129,1},{2,130},{130,2},{3,131},{131,3},{4... | collective-permute-start | bytes 3096584 | tf_op jit(solution)/shard_map/ppermute | solution.py:19
  42.4 20.5 %collective-permute-start.5 = (f16[2,168,512]{2,1,0:T(8,128)(2,1)S(1)}, f16[2,168,512]{2,1,0:T(8,128)(2,1)S(1)}, u32[]{:S(2)}, u32[]{:S(2)}) collective-permute-start(f16[2,168,512]{2,1,0:T(8,128)(2,1)S(1)} %pad_maximum_fusion), channel_id=1, source_target_pairs={{0,2},{1,3},{2,0},{3,1},{4,6},{5,7},{6,4},{7,5},{8,10},{9,11},{10,... | collective-permute-start | bytes 1032200 | tf_op jit(solution)/shard_map/ppermute | solution.py:125
  45.1 17.8 %collective-permute-start.4 = (f16[2,168,512]{2,1,0:T(8,128)(2,1)S(1)}, f16[2,168,512]{2,1,0:T(8,128)(2,1)}, u32[]{:S(2)}, u32[]{:S(2)}) collective-permute-start(f16[2,168,512]{2,1,0:T(8,128)(2,1)S(1)} %pad_maximum_fusion), channel_id=1, source_target_pairs={{0,3},{1,0},{2,1},{3,2},{4,7},{5,4},{6,5},{7,6},{8,11},{9,8},{10,9... | collective-permute-start | bytes 1032200 | tf_op jit(solution)/shard_map/ppermute | solution.py:125
  46.0 17.7 %collective-permute-start.3 = (f16[2,168,512]{2,1,0:T(8,128)(2,1)S(1)}, f16[2,168,512]{2,1,0:T(8,128)(2,1)}, u32[]{:S(2)}, u32[]{:S(2)}) collective-permute-start(f16[2,168,512]{2,1,0:T(8,128)(2,1)S(1)} %pad_maximum_fusion), channel_id=1, source_target_pairs={{0,1},{1,2},{2,3},{3,0},{4,5},{5,6},{6,7},{7,4},{8,9},{9,10},{10,1... | collective-permute-start | bytes 1032200 | tf_op jit(solution)/shard_map/ppermute | solution.py:125
  59.2 18.9 %collective-permute-start.6 = (bf16[16,320,256]{2,1,0:T(8,128)(2,1)}, bf16[16,320,256]{2,1,0:T(8,128)(2,1)S(1)}, u32[]{:S(2)}, u32[]{:S(2)}) collective-permute-start(bf16[16,320,256]{2,1,0:T(8,128)(2,1)} %all-gather.5.cloned.1.call-done.refs_0_), channel_id=1, source_target_pairs={{0,8},{8,0},{1,9},{9,1},{2,10},{10,2},{3,11},{11,3},{4,12},{12,4},... | collective-permute-start | bytes 7864328 | tf_op jit(solution)/shard_map/ppermute | solution.py:19
  67.4 3.4 %copy-start = (f32[160,4096]{1,0:T(8,128)}, f32[160,4096]{1,0:T(8,128)S(1)}, u32[]{:S(2)}) copy-start(f32[160,4096]{1,0:T(8,128)S(1)} %shard_map.77) | copy-start | bytes 7864324
  72.2 38.6 %all-to-all-start = ((f16[8,168,384]{2,1,0:T(8,128)(2,1)}), f16[8,168,384]{2,1,0:T(8,128)(2,1)}, u32[]{:S(2)}, u32[]{:S(2)}) async-start(f16[8,168,384]{2,1,0:T(8,128)(2,1)} %select_convert_fusion), calls=%async_computation | async-start | bytes 2064384 | tf_op jit(solution)/shard_map/all_to_all | solution.py:295
  78.0 100.7 %all-gather.7.cloned.1.call-start = ((), (), s32[]{:S(2)}) async-start(), calls=%async_computation.4 | async-start | bytes 2211840 | tf_op jit(solution)/shard_map/all_gather | solution.py:67
  78.1 6.1 %copy-start.1 = (f32[160,4096]{1,0:T(8,128)S(1)}, f32[160,4096]{1,0:T(8,128)}, u32[]{:S(2)}) copy-start(f32[160,4096]{1,0:T(8,128)} %copy-done) | copy-start | bytes 7864324
  86.5 5.3 %collective-permute-start.7 = (f16[168,256]{1,0:T(8,128)(2,1)S(1)}, f16[168,256]{1,0:T(8,128)(2,1)S(1)}, u32[]{:S(2)}, u32[]{:S(2)}) collective-permute-start(f16[168,256]{1,0:T(8,128)(2,1)S(1)} %select_convert_fusion.3), channel_id=1, source_target_pairs={{0,4},{4,0},{1,5},{5,1},{2,6},{6,2},{3,7},{7,3},{8,12},{12,8},{9,1... | collective-permute-start | bytes 258056 | tf_op jit(solution)/shard_map/ppermute | solution.py:19
  91.9 6.1 %collective-permute-start.10 = (f16[2,168,256]{2,1,0:T(8,128)(2,1)S(1)}, f16[2,168,256]{2,1,0:T(8,128)(2,1)S(1)}, u32[]{:S(2)}, u32[]{:S(2)}) collective-permute-start(f16[2,168,256]{2,1,0:T(8,128)(2,1)S(1)} %pad_maximum_fusion.3), channel_id=1, source_target_pairs={{0,2},{1,3},{2,0},{3,1},{4,6},{5,7},{6,4},{7,5},{8,10},{9,11},{10,... | collective-permute-start | bytes 516104 | tf_op jit(solution)/shard_map/ppermute | solution.py:125
  94.7 7.8 %collective-permute-start.9 = (f16[2,168,256]{2,1,0:T(8,128)(2,1)S(1)}, f16[2,168,256]{2,1,0:T(8,128)(2,1)S(1)}, u32[]{:S(2)}, u32[]{:S(2)}) collective-permute-start(f16[2,168,256]{2,1,0:T(8,128)(2,1)S(1)} %pad_maximum_fusion.3), channel_id=1, source_target_pairs={{0,3},{1,0},{2,1},{3,2},{4,7},{5,4},{6,5},{7,6},{8,11},{9,8},{10,9... | collective-permute-start | bytes 516104 | tf_op jit(solution)/shard_map/ppermute | solution.py:125
  96.4 7.6 %collective-permute-start.8 = (f16[2,168,256]{2,1,0:T(8,128)(2,1)S(1)}, f16[2,168,256]{2,1,0:T(8,128)(2,1)S(1)}, u32[]{:S(2)}, u32[]{:S(2)}) collective-permute-start(f16[2,168,256]{2,1,0:T(8,128)(2,1)S(1)} %pad_maximum_fusion.3), channel_id=1, source_target_pairs={{0,1},{1,2},{2,3},{3,0},{4,5},{5,6},{6,7},{7,4},{8,9},{9,10},{10,1... | collective-permute-start | bytes 516104 | tf_op jit(solution)/shard_map/ppermute | solution.py:125
  106.2 6.9 %copy-start.13 = (s32[2]{0:T(128)S(1)}, s32[2]{0:T(128)}, u32[]{:S(2)}) copy-start(s32[2]{0:T(128)} %pad_add_fusion.place_ref) | copy-start | bytes 28
  106.2 3.8 %collective-permute-start.11 = (bf16[160,384]{1,0:T(8,128)(2,1)S(1)}, bf16[160,384]{1,0:T(8,128)(2,1)S(1)}, u32[]{:S(2)}, u32[]{:S(2)}) collective-permute-start(bf16[160,384]{1,0:T(8,128)(2,1)S(1)} %convolution_convert_fusion), channel_id=1, source_target_pairs={{0,128},{128,0},{1,129},{129,1},{2,130},{130,2},{3,131},{131,3},{4... | collective-permute-start | bytes 368648 | tf_op jit(solution)/shard_map/ppermute | solution.py:19
  120.0 10.9 %collective-permute-start.13 = (bf16[2,8,80,384]{3,2,1,0:T(8,128)(2,1)}, bf16[2,8,80,384]{3,2,1,0:T(8,128)(2,1)}, u32[]{:S(2)}, u32[]{:S(2)}) collective-permute-start(bf16[2,8,80,384]{3,2,1,0:T(8,128)(2,1)} %get-tuple-element.28), channel_id=1, source_target_pairs={{0,8},{8,0},{1,9},{9,1},{2,10},{10,2},{3,11},{11,3},{4,12},{12,4},... | collective-permute-start | bytes 2949128 | tf_op jit(solution)/shard_map/ppermute | solution.py:19
  124.6 6.3 %copy-start.10 = (f32[8,80,384]{2,1,0:T(8,128)S(1)}, f32[8,80,384]{2,1,0:T(8,128)}, u32[]{:S(2)}) copy-start(f32[8,80,384]{2,1,0:T(8,128)} %copy-done.9) | copy-start | bytes 2949124
  125.7 18.8 %all-to-all-start.1 = ((f16[8,168,256]{2,1,0:T(8,128)(2,1)}), f16[8,168,256]{2,1,0:T(8,128)(2,1)}, u32[]{:S(2)}, u32[]{:S(2)}) async-start(f16[8,168,256]{2,1,0:T(8,128)(2,1)} %fusion.5), calls=%async_computation.1 | async-start | bytes 1376256 | tf_op jit(solution)/shard_map/all_to_all | solution.py:133
  130.9 15.7 %copy-start.3 = (bf16[32,128,256]{2,1,0:T(8,128)(2,1)S(1)}, bf16[32,128,256]{2,1,0:T(8,128)(2,1)}, u32[]{:S(2)}) copy-start(bf16[32,128,256]{2,1,0:T(8,128)(2,1)} %copy-done.2) | copy-start | bytes 6291460
  132.5 18.5 %collective-permute-start.18 = (f16[8,72,384]{2,1,0:T(8,128)(2,1)S(1)}, f16[8,72,384]{2,1,0:T(8,128)(2,1)S(1)}, u32[]{:S(2)}, u32[]{:S(2)}) collective-permute-start(f16[8,72,384]{2,1,0:T(8,128)(2,1)S(1)} %fusion.7), channel_id=1, source_target_pairs={{0,128},{128,0},{1,129},{129,1},{2,130},{130,2},{3,131},{131,3},{4... | collective-permute-start | bytes 1327112 | tf_op jit(solution)/shard_map/ppermute | solution.py:19
  151.6 26.6 %copy-start.17 = (f16[8,72,384]{2,1,0:T(8,128)(2,1)}, f16[8,72,384]{2,1,0:T(8,128)(2,1)S(1)}, u32[]{:S(2)}) copy-start(f16[8,72,384]{2,1,0:T(8,128)(2,1)S(1)} %select_convert_fusion.1) | copy-start | bytes 1327108
  151.7 14.8 %collective-permute-start.25 = (f16[72,384]{1,0:T(8,128)(2,1)S(1)}, f16[72,384]{1,0:T(8,128)(2,1)S(1)}, u32[]{:S(2)}, u32[]{:S(2)}) collective-permute-start(f16[72,384]{1,0:T(8,128)(2,1)S(1)} %get-tuple-element.61), channel_id=1, source_target_pairs={{0,112},{16,0},{32,16},{48,32},{64,48},{80,64},{96,80},{112,96},{1... | collective-permute-start | bytes 165896 | tf_op jit(solution)/shard_map/ppermute | solution.py:153
  154.4 29.6 %all-to-all-start.2 = ((f16[8,168,512]{2,1,0:T(8,128)(2,1)}), f16[8,168,512]{2,1,0:T(8,128)(2,1)}, u32[]{:S(2)}, u32[]{:S(2)}) async-start(f16[8,168,512]{2,1,0:T(8,128)(2,1)} %fusion.1), calls=%async_computation.2 | async-start | bytes 2752512 | tf_op jit(solution)/shard_map/all_to_all | solution.py:133
  159.8 10.0 %collective-permute-start.24 = (f16[72,384]{1,0:T(8,128)(2,1)S(1)}, f16[72,384]{1,0:T(8,128)(2,1)S(1)}, u32[]{:S(2)}, u32[]{:S(2)}) collective-permute-start(f16[72,384]{1,0:T(8,128)(2,1)S(1)} %get-tuple-element.62), channel_id=1, source_target_pairs={{0,96},{16,112},{32,0},{48,16},{64,32},{80,48},{96,64},{112,80},{1... | collective-permute-start | bytes 165896 | tf_op jit(solution)/shard_map/ppermute | solution.py:153
  161.9 9.2 %collective-permute-start.23 = (f16[72,384]{1,0:T(8,128)(2,1)S(1)}, f16[72,384]{1,0:T(8,128)(2,1)S(1)}, u32[]{:S(2)}, u32[]{:S(2)}) collective-permute-start(f16[72,384]{1,0:T(8,128)(2,1)S(1)} %get-tuple-element.63), channel_id=1, source_target_pairs={{0,80},{16,96},{32,112},{48,0},{64,16},{80,32},{96,48},{112,64},{1... | collective-permute-start | bytes 165896 | tf_op jit(solution)/shard_map/ppermute | solution.py:153
  163.1 8.0 %collective-permute-start.22 = (f16[72,384]{1,0:T(8,128)(2,1)S(1)}, f16[72,384]{1,0:T(8,128)(2,1)S(1)}, u32[]{:S(2)}, u32[]{:S(2)}) collective-permute-start(f16[72,384]{1,0:T(8,128)(2,1)S(1)} %get-tuple-element.64), channel_id=1, source_target_pairs={{0,64},{16,80},{32,96},{48,112},{64,0},{80,16},{96,32},{112,48},{1... | collective-permute-start | bytes 165896 | tf_op jit(solution)/shard_map/ppermute | solution.py:153
  166.4 8.4 %collective-permute-start.21 = (f16[72,384]{1,0:T(8,128)(2,1)S(1)}, f16[72,384]{1,0:T(8,128)(2,1)S(1)}, u32[]{:S(2)}, u32[]{:S(2)}) collective-permute-start(f16[72,384]{1,0:T(8,128)(2,1)S(1)} %get-tuple-element.65), channel_id=1, source_target_pairs={{0,48},{16,64},{32,80},{48,96},{64,112},{80,0},{96,16},{112,32},{1... | collective-permute-start | bytes 165896 | tf_op jit(solution)/shard_map/ppermute | solution.py:153
  166.5 9.6 %collective-permute-start.20 = (f16[72,384]{1,0:T(8,128)(2,1)S(1)}, f16[72,384]{1,0:T(8,128)(2,1)S(1)}, u32[]{:S(2)}, u32[]{:S(2)}) collective-permute-start(f16[72,384]{1,0:T(8,128)(2,1)S(1)} %get-tuple-element.66), channel_id=1, source_target_pairs={{0,32},{16,48},{32,64},{48,80},{64,96},{80,112},{96,0},{112,16},{1... | collective-permute-start | bytes 165896 | tf_op jit(solution)/shard_map/ppermute | solution.py:153
  169.8 8.3 %copy-start.18 = (f16[72,384]{1,0:T(8,128)(2,1)}, f16[72,384]{1,0:T(8,128)(2,1)S(1)}, u32[]{:S(2)}) copy-start(f16[72,384]{1,0:T(8,128)(2,1)S(1)} %collective-permute-done.24) | copy-start | bytes 165892
  169.8 8.3 %collective-permute-start.19 = (f16[72,384]{1,0:T(8,128)(2,1)S(1)}, f16[72,384]{1,0:T(8,128)(2,1)S(1)}, u32[]{:S(2)}, u32[]{:S(2)}) collective-permute-start(f16[72,384]{1,0:T(8,128)(2,1)S(1)} %get-tuple-element.60), channel_id=1, source_target_pairs={{0,16},{16,32},{32,48},{48,64},{64,80},{80,96},{96,112},{112,0},{1... | collective-permute-start | bytes 165896 | tf_op jit(solution)/shard_map/ppermute | solution.py:153
  171.1 7.0 %copy-start.20 = (f16[72,384]{1,0:T(8,128)(2,1)}, f16[72,384]{1,0:T(8,128)(2,1)S(1)}, u32[]{:S(2)}) copy-start(f16[72,384]{1,0:T(8,128)(2,1)S(1)} %collective-permute-done.23) | copy-start | bytes 165892
  171.2 7.0 %copy-start.22 = (f16[72,384]{1,0:T(8,128)(2,1)}, f16[72,384]{1,0:T(8,128)(2,1)S(1)}, u32[]{:S(2)}) copy-start(f16[72,384]{1,0:T(8,128)(2,1)S(1)} %collective-permute-done.22) | copy-start | bytes 165892
  178.7 3.7 %copy-start.19 = (f16[72,384]{1,0:T(8,128)(2,1)S(1)}, f16[72,384]{1,0:T(8,128)(2,1)}, u32[]{:S(2)}) copy-start(f16[72,384]{1,0:T(8,128)(2,1)} %copy-done.18) | copy-start | bytes 165892
  178.7 3.7 %copy-start.21 = (f16[72,384]{1,0:T(8,128)(2,1)S(1)}, f16[72,384]{1,0:T(8,128)(2,1)}, u32[]{:S(2)}) copy-start(f16[72,384]{1,0:T(8,128)(2,1)} %copy-done.20) | copy-start | bytes 165892
  178.7 3.7 %copy-start.23 = (f16[72,384]{1,0:T(8,128)(2,1)S(1)}, f16[72,384]{1,0:T(8,128)(2,1)}, u32[]{:S(2)}) copy-start(f16[72,384]{1,0:T(8,128)(2,1)} %copy-done.22) | copy-start | bytes 165892
  178.7 3.7 %copy-start.25 = (f16[72,384]{1,0:T(8,128)(2,1)S(1)}, f16[72,384]{1,0:T(8,128)(2,1)}, u32[]{:S(2)}) copy-start(f16[72,384]{1,0:T(8,128)(2,1)} %copy-done.24) | copy-start | bytes 165892
  178.8 3.7 %copy-start.27 = (f16[72,384]{1,0:T(8,128)(2,1)S(1)}, f16[72,384]{1,0:T(8,128)(2,1)}, u32[]{:S(2)}) copy-start(f16[72,384]{1,0:T(8,128)(2,1)} %copy-done.26) | copy-start | bytes 165892
  178.8 3.7 %copy-start.29 = (f16[72,384]{1,0:T(8,128)(2,1)S(1)}, f16[72,384]{1,0:T(8,128)(2,1)}, u32[]{:S(2)}) copy-start(f16[72,384]{1,0:T(8,128)(2,1)} %copy-done.28) | copy-start | bytes 165892
  180.5 6.9 %collective-permute-start.14 = (bf16[4,160,384]{2,1,0:T(8,128)(2,1)S(1)}, bf16[4,160,384]{2,1,0:T(8,128)(2,1)S(1)}, u32[]{:S(2)}, u32[]{:S(2)}) collective-permute-start(bf16[4,160,384]{2,1,0:T(8,128)(2,1)S(1)} %get-tuple-element.57.refs_0_), channel_id=1, source_target_pairs={{0,8},{8,0},{1,9},{9,1},{2,10},{10,2},{3,11},{11,3},{4,12},{12,4},... | collective-permute-start | bytes 1474568 | tf_op jit(solution)/shard_map/ppermute | solution.py:19
  181.8 5.6 %collective-permute-start.15 = (bf16[4,160,384]{2,1,0:T(8,128)(2,1)S(1)}, bf16[4,160,384]{2,1,0:T(8,128)(2,1)S(1)}, u32[]{:S(2)}, u32[]{:S(2)}) collective-permute-start(bf16[4,160,384]{2,1,0:T(8,128)(2,1)S(1)} %get-tuple-element.56.refs_1_), channel_id=1, source_target_pairs={{0,8},{8,0},{1,9},{9,1},{2,10},{10,2},{3,11},{11,3},{4,12},{12,4},... | collective-permute-start | bytes 1474568 | tf_op jit(solution)/shard_map/ppermute | solution.py:19
  181.9 5.5 %collective-permute-start.16 = (bf16[4,160,384]{2,1,0:T(8,128)(2,1)S(1)}, bf16[4,160,384]{2,1,0:T(8,128)(2,1)S(1)}, u32[]{:S(2)}, u32[]{:S(2)}) collective-permute-start(bf16[4,160,384]{2,1,0:T(8,128)(2,1)S(1)} %get-tuple-element.55.refs_2_), channel_id=1, source_target_pairs={{0,8},{8,0},{1,9},{9,1},{2,10},{10,2},{3,11},{11,3},{4,12},{12,4},... | collective-permute-start | bytes 1474568 | tf_op jit(solution)/shard_map/ppermute | solution.py:19
  182.4 5.1 %collective-permute-start.17 = (bf16[4,160,384]{2,1,0:T(8,128)(2,1)S(1)}, bf16[4,160,384]{2,1,0:T(8,128)(2,1)}, u32[]{:S(2)}, u32[]{:S(2)}) collective-permute-start(bf16[4,160,384]{2,1,0:T(8,128)(2,1)S(1)} %get-tuple-element.54.refs_3_), channel_id=1, source_target_pairs={{0,8},{8,0},{1,9},{9,1},{2,10},{10,2},{3,11},{11,3},{4,12},{12,4},... | collective-permute-start | bytes 1474568 | tf_op jit(solution)/shard_map/ppermute | solution.py:19
  184.9 4.0 %slice-start = ((s8[5242880]{0:T(1024)(128)(4,1)}), s8[4194304]{0:T(1024)(128)(4,1)S(1)}, s32[]{:S(2)}) async-start(s8[5242880]{0:T(1024)(128)(4,1)} %bitcast.221), calls=%async_computation.5 | async-start | bytes 8388608
  (15 other events, 25.8 us)
Sparse Core Ops, SparseCore 0:
  14.9 44.2 all-gather.4
  123.0 36.6 all-gather.6
